TPU v7x, 32 devices: a whole 2x2x4 slice. The times are simulated.
32 devices in a mesh: rows: 4 (over z), seq: 8 (over y, x, core).
Axes of the slice: x: 2, y: 2, z: 4, core: 2. Of those that a mesh axis runs over, the one named last changes fastest.
Arguments:
- tokens: bfloat16 [8, 2048, 1024], P('rows', 'seq'), may hold values from -6 to 6
- cotangent: bfloat16 [8, 2048, 1024], P('rows', 'seq'), may hold values from -6 to 6
- bounds: int32 [8, 2], P('rows'), may hold values from 1 to 2048, as said below
- ln1_gain: bfloat16 [1024], replicated, may hold values from 0.5 to 1.5
- ln1_bias: bfloat16 [1024], replicated, may hold values from -1.25 to 1.25
- in_weight: bfloat16 [1024, 3072], replicated, may hold values from -0.1875 to 0.1875
- in_bias: bfloat16 [3072], replicated, may hold values from -1.75 to 1.75
- short_weight: bfloat16 [3, 3072], replicated, may hold values from -3.5 to 3.5
- short_bias: bfloat16 [3072], replicated, may hold values from -1.75 to 1.75
- f1_weight: bfloat16 [33, 64], replicated, may hold values from -6 to 6
- f1_bias: bfloat16 [64], replicated, may hold values from -6 to 6
- f2_weight: bfloat16 [64, 64], replicated, may hold values from -0.75 to 0.75
- f2_bias: bfloat16 [64], replicated, may hold values from -3 to 3
- f3_weight: bfloat16 [64, 1024], P(None, 'seq'), may hold values from -0.09375 to 0.09375
- filter_skip: bfloat16 [1024], P('seq'), may hold values from -6 to 6
- out_weight: bfloat16 [1024, 1024], replicated, may hold values from -0.1875 to 0.1875
- out_bias: bfloat16 [1024], replicated, may hold values from -1.25 to 1.25
- ln2_gain: bfloat16 [1024], replicated, may hold values from 0.5 to 1.5
- ln2_bias: bfloat16 [1024], replicated, may hold values from -1.25 to 1.25
- up_weight: bfloat16 [1024, 4096], replicated, may hold values from -0.1875 to 0.1875
- up_bias: bfloat16 [4096], replicated, may hold values from -1.75 to 1.75
- down_weight: bfloat16 [4096, 1024], replicated, may hold values from -0.09375 to 0.09375
- down_bias: bfloat16 [1024], replicated, may hold values from -1.25 to 1.25
Outputs:
- output: bfloat16 [8, 2048, 1024], P('rows', 'seq')
- grad_tokens: float32 [8, 2048, 1024], P('rows', 'seq')
- grad_ln1_gain: float32 [1024], P(('rows', 'seq'))
- grad_ln1_bias: float32 [1024], P(('rows', 'seq'))
- grad_in_weight: float32 [1024, 3072], P(('rows', 'seq'))
- grad_in_bias: float32 [3072], P(('rows', 'seq'))
- grad_short_weight: float32 [3, 3072], P(None, ('rows', 'seq'))
- grad_short_bias: float32 [3072], P(('rows', 'seq'))
- grad_f1_weight: float32 [33, 64], replicated
- grad_f1_bias: float32 [64], replicated
- grad_f2_weight: float32 [64, 64], replicated
- grad_f2_bias: float32 [64], replicated
- grad_f3_weight: float32 [64, 1024], P(None, 'seq')
- grad_filter_skip: float32 [1024], P('seq')
- grad_out_weight: float32 [1024, 1024], P(('rows', 'seq'))
- grad_out_bias: float32 [1024], P(('rows', 'seq'))
- grad_ln2_gain: float32 [1024], P(('rows', 'seq'))
- grad_ln2_bias: float32 [1024], P(('rows', 'seq'))
- grad_up_weight: float32 [1024, 4096], P(('rows', 'seq'))
- grad_up_bias: float32 [4096], P(('rows', 'seq'))
- grad_down_weight: float32 [4096, 1024], P(('rows', 'seq'))
- grad_down_bias: float32 [1024], P(('rows', 'seq'))
Inputs may be any that keep to these rules, and one draw needn't show every extreme that they name: `bounds`: in each row the cut points do not fall; a cut at 2048 starts no document; in every group of 2 rows on one index of rows one row is a single document.
All inputs are finite; a program needn't handle non-finite values.
Results may differ from a plain program's by a relative error of at most 0.0097.
Values may be sent and summed in bfloat16 or wider, within the bound.
No kernel may reach another device: no remote copies, remote signals or barrier semaphores. Data moves between devices by JAX's collectives and lax.ppermute only.
A program may use at most 384 MiB of HBM per device.

v0:
```python
import functools
import math

import jax
import jax.numpy as jnp
import ml_dtypes
import numpy as np
from jax import lax
from jax.experimental import pallas as pl
from jax.experimental.pallas import tpu as pltpu
from jax.sharding import PartitionSpec as P

D = 1024
EMB = 33
HIGH = lax.Precision.HIGHEST
eps = 1e-05
slow_rate = math.log(100.0) / 1.5
fast_rate = math.log(100.0) / 0.3
BOTH = ("rows", "seq")
F32 = jnp.float32
BF16 = jnp.bfloat16
VMEM_MIB = 58
LITTLE = pl.CostEstimate(flops=1, bytes_accessed=1, transcendentals=0)
MUCH = pl.CostEstimate(flops=5 * 10**10, bytes_accessed=2 * 10**8, transcendentals=0)


def passed_along(value, axis, steps):
    count = lax.axis_size(axis)
    first, last = (max(0, -steps), min(count, count - steps))
    return lax.ppermute(value, axis, [(source, source + steps) for source in range(first, last)])


def layer_norm(values, gain, shift):
    center = values - jnp.mean(values, axis=-1, keepdims=True)
    spread = jnp.mean(center * center, axis=-1, keepdims=True)
    return center * lax.rsqrt(spread + eps) * gain + shift


def gelu_tanh(values):
    return jax.nn.gelu(values, approximate=True)


def features(length):
    steps = np.arange(length, dtype=np.float64)
    bands = (EMB - 1) // 2
    freqs = 0.0001 + np.arange(bands, dtype=np.float64) * ((bands - 1 - 0.0001) / (bands - 1))
    angles = (steps * (2.0 * math.pi / length))[:, None] * freqs[None, :]
    timeline = steps / (length - 1)
    table = np.concatenate([timeline[:, None], np.cos(angles), -np.sin(angles)], axis=1)
    return jnp.asarray(table.astype(np.float32)), jnp.asarray(timeline.astype(np.float32))


def filter_taps(w_one, b_one, w_two, b_two, w_three, first, length):
    feats, timeline = features(length)
    hidden = jnp.sin(jnp.dot(feats, w_one, precision=HIGH) + b_one)
    hidden = jnp.sin(jnp.dot(hidden, w_two, precision=HIGH) + b_two)
    raw_taps = jnp.dot(hidden, w_three, precision=HIGH)
    channels = (first + jnp.arange(w_three.shape[1], dtype=jnp.int32)).astype(F32)
    rates = slow_rate + channels * ((fast_rate - slow_rate) / (D - 1))
    return raw_taps * jnp.exp(-timeline[:, None] * rates[None, :])


def close_dot(left, right, dims):
    def one(a, b):
        return lax.dot_general(a, b, (dims, ((), ())), preferred_element_type=F32)

    (a, a_rest), (b, b_rest) = split32(left), split32(right)
    return one(a, b) + one(a, b_rest) + one(a_rest, b)


def line_up(out_ref, count, parts):
    line = 0
    for ref, lead, rows in parts:
        width = ref.shape[-1]
        share = rows * width // count // 128
        for z in range(count):
            for k in range(share):
                at = (z * share + k) * 128
                row, lane = at // width, at % width
                index = ((row,) if rows > 1 else ()) + tuple(lead)
                value = ref[index + (slice(lane, lane + 128),)]
                out_ref[z, line + k : line + k + 1] = value.reshape(1, 128)
        line += share


def filter_backward_kernel(
    first_ref,
    row_ref,
    grad_ref,
    feats_ref,
    one_ref,
    two_ref,
    w2_ref,
    w3_ref,
    skip_ref,
    middle_ref,
    up_ref,
    norm_ref,
    short_ref,
    outs,
    lines,
    out_ref,
):
    lines[...] = jnp.zeros_like(lines)
    parts = [(middle_ref, (k,), 1) for k in range(4)] + [(norm_ref, (k,), 1) for k in range(2)]
    parts += [(up_ref, (0,), 1)] + [(short_ref, (k,), 3) for k in range(5)]
    line_up(lines, len(outs), parts)
    length, lanes = grad_ref.shape
    units = one_ref.shape[1] // 2
    bands = feats_ref.shape[1]
    inner = grad_ref[...] * decay(first_ref, 0, length, lanes, length)
    over_time, over_last = ((0,), (0,)), ((1,), (1,))
    out_ref[...] = jnp.zeros_like(out_ref)
    out_ref[:units] = close_dot(two_ref[:, :units], inner, over_time)
    out_ref[units : units + 1] = skip_ref[...]
    two = close_dot(inner, w3_ref[...].astype(F32), over_last) * two_ref[:, units:]
    one = close_dot(two, w2_ref[...].astype(F32), over_last) * one_ref[:, units:]
    below = units + 8
    out_ref[below : below + units, :units] = close_dot(one_ref[:, :units], two, over_time)
    out_ref[below : below + bands, units:] = close_dot(feats_ref[...], one, over_time)
    out_ref[below + bands : below + bands + 1, units:] = jnp.sum(one, axis=0, keepdims=True)
    out_ref[below + bands + 1 : below + bands + 2, units:] = jnp.sum(two, axis=0, keepdims=True)
    for k, payload in enumerate(outs):
        payload[: 2 * units + 8] = out_ref[...]
        payload[2 * units + 8 :] = lines[row_ref[0] ^ k]


LINES = 56


def filter_backward(first, row, count, g_taps, kept, w_two, w_three, g_skip, sums, ready):
    feats, one, two = kept
    units, lanes = w_three.shape
    vmem = pl.BlockSpec(memory_space=pltpu.VMEM)
    height = 2 * units + 8

    def kernel(*refs):
        outs, scratch = refs[13 + len(ready) : -2], refs[-2:]
        filter_backward_kernel(*refs[:13], outs, *scratch)

    return pl.pallas_call(
        kernel,
        in_specs=[smem()] * 2 + [vmem] * 11 + [pl.BlockSpec(memory_space=pl.ANY)] * len(ready),
        out_specs=[vmem] * count,
        out_shape=[jax.ShapeDtypeStruct((height + LINES, lanes), F32)] * count,
        scratch_shapes=[
            pltpu.VMEM((count, LINES, lanes), F32),
            pltpu.VMEM((height, lanes), F32),
        ],
        compiler_params=pltpu.CompilerParams(vmem_limit_bytes=VMEM_MIB * 2**20),
        cost_estimate=MUCH,
        name="filter_backward",
    )(first, row, g_taps, feats, one, two, w_two, w_three, g_skip, *sums, *ready)


def split16(values):
    high = values.astype(ml_dtypes.bfloat16)
    return high, (values - high.astype(np.float64)).astype(ml_dtypes.bfloat16)


def transform_tables(block):
    freq = np.arange(block)[:, None]
    time = np.arange(block)[None, :]
    angles = ((2 * freq + 1) * time % (4 * block)) * (math.pi / (2 * block))
    ahead = np.concatenate([np.cos(angles), -np.sin(angles)], axis=0)
    ahead_high, ahead_low = split16(ahead)
    back_high, back_low = split16(ahead.T / block)
    return tuple(jnp.asarray(t) for t in (ahead_high, ahead_low, back_high, back_low))


def piece_table(bounds, blocks, block):
    length = blocks * block
    edges = jnp.broadcast_to(jnp.arange(blocks, dtype=jnp.int32) * block, (bounds.shape[0], blocks))
    for cut in range(bounds.shape[1]):
        one = bounds[:, cut : cut + 1]
        low = jnp.concatenate([jnp.full_like(one, -1), edges], axis=1)
        high = jnp.concatenate([edges, jnp.full_like(one, length)], axis=1)
        edges = jnp.maximum(low, jnp.minimum(one, high))
    ends = jnp.concatenate([edges[:, 1:], jnp.full_like(edges[:, :1], length)], axis=1)
    index = jnp.minimum(edges // block, blocks - 1)
    start = jnp.max(
        jnp.where(bounds[:, :, None] <= edges[:, None, :], bounds[:, :, None], 0), axis=1
    )
    stop = jnp.min(
        jnp.where(bounds[:, :, None] > edges[:, None, :], bounds[:, :, None], length), axis=1
    )
    empty = ends <= edges
    earlier = jnp.where(empty, 0, index - start // block + 1)
    later = jnp.where(empty, 0, (stop - 1) // block - index + 1)
    return jnp.stack([edges, ends, index, earlier, later]).astype(jnp.int32)


def dot32(left, right):
    return jnp.dot(left, right, preferred_element_type=F32)


def split32(values):
    high = values.astype(BF16)
    return high, (values - high.astype(F32)).astype(BF16)


def wide_dot(high, low, values):
    top, rest = split32(values)
    return dot32(high, top) + dot32(high, rest) + dot32(low, top)


def alternating(rows, lanes):
    odd = lax.broadcasted_iota(jnp.int32, (rows, lanes), 0) % 2
    return 1.0 - 2.0 * odd.astype(F32)


def sine_cosine(angle):
    turns = jnp.floor(angle * (2.0 / math.pi) + 0.5)
    rest = angle - turns * 1.5703125
    rest = rest - turns * 4.837512969970703125e-4
    rest = rest - turns * 7.549789948768648e-8
    square = rest * rest
    sine = ((-1.9515295891e-4 * square + 8.3321608736e-3) * square - 1.6666654611e-1) * square
    sine = sine * rest + rest
    cosine = (2.443315711809948e-5 * square - 1.388731625493765e-3) * square
    cosine = (cosine + 4.166664568298827e-2) * square * square - 0.5 * square + 1.0
    quarter = turns.astype(jnp.int32)
    swap = (quarter & 1) == 1
    sine, cosine = jnp.where(swap, cosine, sine), jnp.where(swap, sine, cosine)
    return (
        jnp.where((quarter & 2) == 2, -sine, sine),
        jnp.where(((quarter + 1) & 2) == 2, -cosine, cosine),
    )


def near_dot(left, right):
    top, rest = split32(left)
    return dot32(top, right) + dot32(rest, right)


def decay(first_ref, begin, count, lanes, length):
    spot = (lax.broadcasted_iota(jnp.int32, (count, lanes), 0) + begin).astype(F32)
    channel = (lax.broadcasted_iota(jnp.int32, (1, lanes), 1) + first_ref[0]).astype(F32)
    rates = slow_rate + channel * ((fast_rate - slow_rate) / (D - 1))
    return jnp.exp(-(spot * (1.0 / (length - 1))) * rates)


def taps_kernel(
    first_ref, feats_ref, w1, b1, w2, b2, w3, high_ref, low_ref, _, out_ref, one_ref, two_ref, own
):
    blocks, double, lanes = out_ref.shape
    block = double // 2
    for k in range(blocks):
        at = slice(k * block, (k + 1) * block)
        sine, cosine = sine_cosine(near_dot(feats_ref[at], w1[...]) + row_of(b1))
        one_ref[at] = jnp.concatenate([sine, cosine], axis=1)
        sine, cosine = sine_cosine(near_dot(sine, w2[...]) + row_of(b2))
        two_ref[at] = jnp.concatenate([sine, cosine], axis=1)
        taps = near_dot(sine, w3[...]) * decay(first_ref, k * block, block, lanes, blocks * block)
        own[k] = wide_dot(high_ref[...], low_ref[...], taps)
    sign = alternating(block, lanes)
    out_ref[0] = own[0]
    for k in range(1, blocks):
        out_ref[k, :block] = own[k, :block] - sign * own[k - 1, block:]
        out_ref[k, block:] = own[k, block:] + sign * own[k - 1, :block]


def taps_and_spectrum(first, blocks, block, w1, b1, w2, b2, w3, tables, ready):
    lanes, units = w3.shape[1], w2.shape[0]
    length = blocks * block
    feats, _ = features(length)
    vmem = pl.BlockSpec(memory_space=pltpu.VMEM)
    spectra, one, two = pl.pallas_call(
        taps_kernel,
        in_specs=[smem()] + [vmem] * 8 + [pl.BlockSpec(memory_space=pl.ANY)],
        out_specs=[vmem] * 3,
        out_shape=[jax.ShapeDtypeStruct((blocks, 2 * block, lanes), F32)]
        + [jax.ShapeDtypeStruct((length, 2 * units), F32)] * 2,
        scratch_shapes=[pltpu.VMEM((blocks, 2 * block, lanes), F32)],
        compiler_params=pltpu.CompilerParams(vmem_limit_bytes=VMEM_MIB * 2**20),
        cost_estimate=LITTLE,
        name="taps_and_spectrum",
    )(first, feats, w1, b1, w2, b2, w3, tables[0], tables[1], ready)
    return spectra, (feats, one, two)


def piece_mask(table_ref, row, piece, block, lanes):
    at = table_ref[2, row, piece]
    spot = lax.broadcasted_iota(jnp.int32, (block, lanes), 0) + at * block
    return at, (spot >= table_ref[0, row, piece]) & (spot < table_ref[1, row, piece])


def piece_spectra(table_ref, series_ref, ahead_ref, out_ref):
    blocks, rows, block, lanes = series_ref.shape
    for piece in range(out_ref.shape[0]):
        parts = []
        for row in range(rows):
            at, inside = piece_mask(table_ref, row, piece, block, lanes)
            values = series_ref[at, row].astype(F32)
            parts.append(jnp.where(inside, values, 0.0).astype(BF16))
        out_ref[piece] = dot32(ahead_ref[...], jnp.concatenate(parts, axis=1))


def each_piece(table_ref, which, pieces, rows, lanes, blocks, visit):
    def body(index, carry):
        piece, row = index // rows, index % rows
        lane = pl.ds(pl.multiple_of(row * lanes, lanes), lanes)
        found = table_ref[which, row, piece]
        for count in range(blocks + 1):

            @pl.when(found == count)
            def _(count=count):
                visit(piece, lane, count)

        return carry

    lax.fori_loop(0, pieces * rows, body, 0)


def halves_of(block, tile):
    for begin in range(0, block, tile):
        yield pl.ds(begin, tile), pl.ds(block + begin, tile)


def couple(table_ref, step, taps_ref, series_ref, into_ref):
    blocks, double, lanes = taps_ref.shape
    block = double // 2
    pieces, _, both = series_ref.shape

    def visit(piece, lane, count):
        for real_rows, imag_rows in halves_of(block, 32):
            real = imag = jnp.zeros((32, lanes), F32)
            for k in range(count):
                tap_r, tap_i = taps_ref[k, real_rows, :], taps_ref[k, imag_rows, :]
                val_r = series_ref[piece + step * k, real_rows, lane]
                val_i = series_ref[piece + step * k, imag_rows, lane]
                if step > 0:
                    real = real + (tap_r * val_r + tap_i * val_i)
                    imag = imag + (tap_r * val_i - tap_i * val_r)
                else:
                    real = real + (tap_r * val_r - tap_i * val_i)
                    imag = imag + (tap_r * val_i + tap_i * val_r)
            into_ref[piece, real_rows, lane] = real
            into_ref[piece, imag_rows, lane] = imag

    each_piece(table_ref, 3 if step < 0 else 4, pieces, both // lanes, lanes, blocks, visit)


def correlate(table_ref, series_ref, grad_ref, into_ref):
    blocks, double, lanes = into_ref.shape
    block = double // 2
    pieces, _, both = series_ref.shape
    into_ref[...] = jnp.zeros_like(into_ref)

    def visit(piece, lane, count):
        for real_rows, imag_rows in halves_of(block, 32):
            if count:
                out_r, out_i = grad_ref[piece, real_rows, lane], grad_ref[piece, imag_rows, lane]
            for k in range(count):
                val_r = series_ref[piece - k, real_rows, lane]
                val_i = series_ref[piece - k, imag_rows, lane]
                into_ref[k, real_rows, :] += val_r * out_r + val_i * out_i
                into_ref[k, imag_rows, :] += val_r * out_i - val_i * out_r

    each_piece(table_ref, 3, pieces, both // lanes, lanes, blocks, visit)


def write_pieces(table_ref, work, back_ref, series_ref, skip_ref, out_ref):
    blocks, rows, block, lanes = series_ref.shape
    for piece in range(work.shape[0]):
        result = dot32(back_ref[...], work[piece].astype(BF16))
        for row in range(rows):
            at, inside = piece_mask(table_ref, row, piece, block, lanes)
            direct = skip_ref[...].astype(F32).reshape(1, -1) * series_ref[at, row].astype(F32)
            value = result[:, row * lanes : (row + 1) * lanes] + direct
            kept = out_ref[at, row, :block].astype(F32)
            out_ref[at, row, :block] = jnp.where(inside, value, kept).astype(BF16)


def long_forward_kernel(
    table_ref, series_ref, taps_ref, skip_ref, ahead_ref, back_ref, out_ref, spec, work
):
    piece_spectra(table_ref, series_ref, ahead_ref, spec)
    couple(table_ref, -1, taps_ref, spec, work)
    write_pieces(table_ref, work, back_ref, series_ref, skip_ref, out_ref)


def long_forward(table, series, taps_spec, skip, tables):
    blocks, rows, block, lanes = series.shape
    pieces = table.shape[2]
    vmem = pl.BlockSpec(memory_space=pltpu.VMEM)
    return pl.pallas_call(
        long_forward_kernel,
        in_specs=[smem()] + [vmem] * 5,
        out_specs=vmem,
        out_shape=jax.ShapeDtypeStruct(series.shape, BF16),
        scratch_shapes=[pltpu.VMEM((pieces, 2 * block, rows * lanes), F32)] * 2,
        compiler_params=pltpu.CompilerParams(vmem_limit_bytes=VMEM_MIB * 2**20),
        cost_estimate=MUCH,
        name="long_forward",
    )(table, series, taps_spec, skip, tables[0], tables[2])


def long_backward_kernel(
    table_ref, grad_ref, series_ref, taps_ref, skip_ref, ahead_ref, back_ref, *others
):
    out_ref, taps_out_ref, skip_out_ref, token_out, spec, grad_spec, work, cross = others[-8:]
    token_out[0] = 0
    blocks, rows, block, lanes = series_ref.shape
    piece_spectra(table_ref, grad_ref, ahead_ref, grad_spec)
    couple(table_ref, 1, taps_ref, grad_spec, work)
    write_pieces(table_ref, work, back_ref, grad_ref, skip_ref, out_ref)
    for at in range(blocks):
        for row in range(rows):
            if at + 1 < blocks:
                out_ref[at, row, block:] = out_ref[at + 1, row, : out_ref.shape[2] - block]
            else:
                out_ref[at, row, block:] = jnp.zeros_like(out_ref[at, row, block:])
    piece_spectra(table_ref, series_ref, ahead_ref, spec)
    correlate(table_ref, spec, grad_spec, cross)
    sign = alternating(block, lanes)
    for k in range(blocks):
        if k + 1 < blocks:
            cross[k, :block] = cross[k, :block] + sign * cross[k + 1, block:]
            cross[k, block:] = cross[k, block:] - sign * cross[k + 1, :block]
        taps_out_ref[k] = dot32(back_ref[...], cross[k].astype(BF16))
    total = jnp.zeros((8, lanes), F32)
    for at in range(blocks):
        for row in range(rows):
            both = grad_ref[at, row].astype(F32) * series_ref[at, row].astype(F32)
            total = total + jnp.sum(both.reshape(block // 8, 8, lanes), axis=0)
    skip_out_ref[...] = jnp.sum(total, axis=0, keepdims=True)


def long_backward(table, grad, series, taps_spec, skip, tables, ready):
    blocks, rows, block, lanes = series.shape
    pieces = table.shape[2]
    vmem = pl.BlockSpec(memory_space=pltpu.VMEM)
    return pl.pallas_call(
        long_backward_kernel,
        in_specs=[smem()] + [vmem] * 6 + [pl.BlockSpec(memory_space=pl.ANY)] * len(ready),
        out_specs=[vmem] * 3 + [smem()],
        out_shape=[
            jax.ShapeDtypeStruct((blocks, rows, block + HALO, lanes), BF16),
            jax.ShapeDtypeStruct((blocks, block, lanes), F32),
            jax.ShapeDtypeStruct((1, lanes), F32),
            jax.ShapeDtypeStruct((1,), jnp.int32),
        ],
        scratch_shapes=[pltpu.VMEM((pieces, 2 * block, rows * lanes), F32)] * 3
        + [pltpu.VMEM((blocks, 2 * block, lanes), F32)],
        compiler_params=pltpu.CompilerParams(vmem_limit_bytes=VMEM_MIB * 2**20),
        cost_estimate=MUCH,
        name="long_backward",
    )(table, grad, series, taps_spec, skip, tables[0], tables[2], *ready)


def document_masks(bounds, positions, length):
    lower = jnp.concatenate([jnp.zeros_like(bounds[:, :1]), bounds], axis=1)
    upper = jnp.concatenate([bounds, jnp.full_like(bounds[:, :1], length)], axis=1)
    inside = (positions[None, None, :] >= lower[:, :, None]) & (
        positions[None, None, :] < upper[:, :, None]
    )
    return inside.astype(F32)


def cos_sin(count_a, count_b, modulus):
    table = (
        jnp.arange(count_a, dtype=jnp.int32)[:, None]
        * jnp.arange(count_b, dtype=jnp.int32)[None, :]
        % modulus
    )
    angles = table.astype(F32) * (2.0 * math.pi / modulus)
    return (jnp.cos(angles), jnp.sin(angles))


def make_plan(blocks, block_len):
    outer = 2 * blocks
    cos_outer, sin_outer = cos_sin(outer, outer, outer)
    cos_twist, sin_twist = cos_sin(outer, block_len, outer * block_len)
    cos_inner, sin_inner = cos_sin(block_len, block_len, block_len)
    return (blocks, block_len, cos_outer, sin_outer, cos_twist, sin_twist, cos_inner, sin_inner)


def right_mul(left, table):
    return jnp.einsum("...km,mj->...kj", left, table, precision=HIGH)


def spectrum(series, plan):
    blocks, block_len, cos_outer, sin_outer, cos_twist, sin_twist, cos_inner, sin_inner = plan
    folded = series.reshape(series.shape[:-1] + (blocks, block_len))
    real_a = jnp.einsum("kn,...nm->...km", cos_outer[:, :blocks], folded, precision=HIGH)
    imag_a = -jnp.einsum("kn,...nm->...km", sin_outer[:, :blocks], folded, precision=HIGH)
    real_t = real_a * cos_twist + imag_a * sin_twist
    imag_t = imag_a * cos_twist - real_a * sin_twist
    real_x = right_mul(real_t, cos_inner) + right_mul(imag_t, sin_inner)
    imag_x = right_mul(imag_t, cos_inner) - right_mul(real_t, sin_inner)
    return (real_x, imag_x)


def inverse(real_x, imag_x, plan):
    blocks, block_len, cos_outer, sin_outer, cos_twist, sin_twist, cos_inner, sin_inner = plan
    real_b = right_mul(real_x, cos_inner) - right_mul(imag_x, sin_inner)
    imag_b = right_mul(imag_x, cos_inner) + right_mul(real_x, sin_inner)
    real_u = real_b * cos_twist - imag_b * sin_twist
    imag_u = imag_b * cos_twist + real_b * sin_twist
    folded = jnp.einsum("nk,...km->...nm", cos_outer[:blocks], real_u, precision=HIGH) - jnp.einsum(
        "nk,...km->...nm", sin_outer[:blocks], imag_u, precision=HIGH
    )
    folded = folded * (1.0 / (2 * blocks * block_len))
    return folded.reshape(folded.shape[:-2] + (blocks * block_len,))


def by_channel(blocked):
    blocks, rows, block, lanes = blocked.shape
    return blocked.astype(F32).transpose(1, 3, 0, 2).reshape(rows, lanes, blocks * block)


def by_block(series, blocks):
    rows, lanes, length = series.shape
    return series.reshape(rows, lanes, blocks, length // blocks).transpose(2, 0, 3, 1).astype(BF16)


class WholeSpectra:
    def __init__(self, bounds, taps, skip):
        blocks, block, lanes = taps.shape
        self.blocks, self.plan = blocks, make_plan(blocks, block)
        length = blocks * block
        everywhere = jnp.arange(length, dtype=jnp.int32)
        self.masks = document_masks(bounds, everywhere, length)[:, :, None, :]
        self.skip = skip[0][None, :, None]
        self.taps_real, self.taps_imag = spectrum(taps.reshape(length, lanes).T, self.plan)

    def forward(self, series):
        carried = by_channel(series)
        self.carried = carried
        real, imag = spectrum(self.masks * carried[:, None], self.plan)
        self.spec = real, imag
        docs = inverse(
            real * self.taps_real - imag * self.taps_imag,
            real * self.taps_imag + imag * self.taps_real,
            self.plan,
        )
        conv = jnp.sum(self.masks * docs, axis=1) + self.skip * carried
        return by_block(conv, self.blocks)

    def backward(self, grad):
        g_long = by_channel(grad)
        spec_real, spec_imag = self.spec
        g_skip = jnp.sum(g_long * self.carried, axis=(0, 2))
        real, imag = spectrum(self.masks * g_long[:, None], self.plan)
        docs = inverse(
            self.taps_real * real + self.taps_imag * imag,
            self.taps_real * imag - self.taps_imag * real,
            self.plan,
        )
        g_carried = jnp.sum(self.masks * docs, axis=1) + self.skip * g_long
        cross_real = jnp.sum(real * spec_real + imag * spec_imag, axis=(0, 1))
        cross_imag = jnp.sum(imag * spec_real - real * spec_imag, axis=(0, 1))
        g_taps = inverse(cross_real, cross_imag, self.plan)
        return by_block(g_carried, self.blocks), g_taps.T, g_skip[None, :]


def device_index():
    return lax.axis_index("rows") * lax.axis_size("seq") + lax.axis_index("seq")


def device_bits():
    return int(math.log2(lax.axis_size("rows") * lax.axis_size("seq")))


def swapped(value, mask_of):
    count = lax.axis_size("rows") * lax.axis_size("seq")
    return lax.ppermute(value, BOTH, [(one, one ^ mask_of(one)) for one in range(count)])


def pick(array, index, axis):
    return lax.dynamic_index_in_dim(array, index, axis=axis, keepdims=False)


def added(kept, arrived, kind):
    return (kept.astype(F32) + arrived.astype(F32)).astype(kind)


def halved(pieces, bit, axis, kind):
    mine = (device_index() >> bit) & 1
    arrived = swapped(pick(pieces, 1 - mine, axis), lambda one: 1 << bit)
    return added(pick(pieces, mine, axis), arrived, kind)


def quartered(pieces, axis, kind):
    index = device_index()
    core, low, high = index & 1, (index >> 1) & 1, (index >> 2) & 1

    def two(low_bit, high_bit):
        return jnp.stack(
            [
                pick(pieces, jnp.where(core == 0, 2 * j + low_bit, 2 * high_bit + j), axis)
                for j in range(2)
            ],
            axis=axis,
        )

    arrived = swapped(two(1 - low, 1 - high), lambda one: 4 if one & 1 else 2)
    pieces = added(two(low, high), arrived, kind)
    mine = jnp.where(core == 0, high, low)
    arrived = swapped(pick(pieces, 1 - mine, axis), lambda one: 2 if one & 1 else 4)
    return added(pick(pieces, mine, axis), arrived, kind)


def scattered(pieces, kind):
    rest = pieces.shape[1:]
    bits = device_bits()
    pieces = quartered(pieces.reshape((-1, 4) + rest), 1, kind)
    for bit in range(3, bits):
        last = bit == bits - 1
        pieces = halved(pieces.reshape((-1, 2) + rest), bit, 1, F32 if last else kind)
    return pieces.reshape(rest)


def weight_gradient(first, second):
    tokens, width = first.shape
    shares = 1 << device_bits()
    share = width // shares
    core = device_index() & 1
    halves = first.reshape(tokens, shares // 2, 2, share).transpose(2, 0, 1, 3)
    halves = halves.reshape(2, tokens, width // 2)

    def product(which):
        return jnp.einsum(
            "ti,tj->ij", pick(halves, which, 0), second, preferred_element_type=F32
        )

    arrived = swapped(product(1 - core).astype(BF16), lambda one: 1)
    kept = added(product(core), arrived, BF16)
    return scattered(kept.reshape(shares // 2, share, second.shape[1]), BF16)


def small_scattered(vectors):
    pieces = halved(vectors.reshape(-1, 2, vectors.shape[1]), 0, 1, F32)
    return scattered(pieces, F32)


def summed(value, bits):
    for bit in bits:
        value = value + swapped(value, lambda one, bit=bit: 1 << bit)
    return value


def back_product(grad_low, weight):
    return jnp.einsum("tj,ij->ti", grad_low, weight, preferred_element_type=F32)


def plain_device(
    tokens,
    cotangent,
    bounds,
    ln1_gain,
    ln1_bias,
    in_weight,
    in_bias,
    short_weight,
    short_bias,
    f1_weight,
    f1_bias,
    f2_weight,
    f2_bias,
    f3_weight,
    filter_skip,
    out_weight,
    out_bias,
    ln2_gain,
    ln2_bias,
    up_weight,
    up_bias,
    down_weight,
    down_bias,
):
    seq_count = lax.axis_size("seq")
    row_count, tok_count, width = tokens.shape
    flat_count = row_count * tok_count
    length = tok_count * seq_count
    lanes = f3_weight.shape[1]
    first_channel = lax.axis_index("seq") * lanes
    x_in = tokens.astype(F32).reshape(flat_count, width)
    n1, ln1_pull = jax.vjp(layer_norm, x_in, ln1_gain.astype(F32), ln1_bias.astype(F32))
    n1_low = n1.astype(BF16)
    proj = jnp.dot(n1_low, in_weight, preferred_element_type=F32) + in_bias.astype(F32)
    proj_low = proj.astype(BF16).reshape(row_count, tok_count, 3 * width)
    here = lax.axis_index("seq") * tok_count + jnp.arange(tok_count, dtype=jnp.int32)
    starts = jnp.max(
        jnp.where(bounds[:, :, None] <= here[None, None, :], bounds[:, :, None], 0), axis=1
    )
    keep_one = (here[None, :] - 1 >= starts).astype(F32)[:, :, None]
    keep_two = (here[None, :] - 2 >= starts).astype(F32)[:, :, None]
    rim = passed_along(proj_low[:, tok_count - 2 :, :], "seq", 1)
    extended = jnp.concatenate([rim, proj_low], axis=1).astype(F32)
    current = extended[:, 2:, :]
    before_one = extended[:, 1:-1, :]
    before_two = extended[:, :-2, :]
    taps_short = short_weight.astype(F32)
    shorted = (
        taps_short[0] * current
        + keep_one * taps_short[1] * before_one
        + keep_two * taps_short[2] * before_two
        + short_bias.astype(F32)
    )
    gate_out = shorted[:, :, :width]
    gate_in = shorted[:, :, width : 2 * width]
    values = shorted[:, :, 2 * width :]
    carried_low = (gate_in * values).astype(BF16)

    def to_channels(array):
        array = array.reshape(row_count, tok_count, seq_count, lanes).transpose(2, 0, 1, 3)
        return lax.all_to_all(array, "seq", split_axis=0, concat_axis=0, tiled=True)

    def to_positions(array):
        array = lax.all_to_all(array, "seq", split_axis=0, concat_axis=0, tiled=True)
        return array.transpose(1, 2, 0, 3).reshape(row_count, tok_count, width)

    carried = to_channels(carried_low)

    def make_taps(w_one, b_one, w_two, b_two, w_three):
        return filter_taps(w_one, b_one, w_two, b_two, w_three, first_channel, length)

    taps, filter_pull = jax.vjp(
        make_taps,
        f1_weight.astype(F32),
        f1_bias.astype(F32),
        f2_weight.astype(F32),
        f2_bias.astype(F32),
        f3_weight.astype(F32),
    )
    long_filter = WholeSpectra(
        bounds, taps.reshape(seq_count, tok_count, lanes), filter_skip.astype(F32)[None, :]
    )
    long_low = long_filter.forward(carried)
    long_seq = to_positions(long_low).astype(F32)
    mixed_low = (gate_out * long_seq).astype(BF16).reshape(flat_count, width)
    branch = jnp.dot(mixed_low, out_weight, preferred_element_type=F32) + out_bias.astype(F32)
    resid = x_in + branch
    n2, ln2_pull = jax.vjp(layer_norm, resid, ln2_gain.astype(F32), ln2_bias.astype(F32))
    n2_low = n2.astype(BF16)
    pre = jnp.dot(n2_low, up_weight, preferred_element_type=F32) + up_bias.astype(F32)
    act, gelu_pull = jax.vjp(gelu_tanh, pre)
    act_low = act.astype(BF16)
    result = (
        resid
        + jnp.dot(act_low, down_weight, preferred_element_type=F32)
        + down_bias.astype(F32)
    )
    output = result.astype(BF16).reshape(row_count, tok_count, width)
    grad_low = cotangent.reshape(flat_count, width)
    grad_float = grad_low.astype(F32)
    g_down_w = weight_gradient(act_low, grad_low)
    g_down_b = jnp.sum(grad_float, axis=0)
    g_act = back_product(grad_low, down_weight)
    (g_pre,) = gelu_pull(g_act)
    g_pre_low = g_pre.astype(BF16)
    g_up_w = weight_gradient(n2_low, g_pre_low)
    g_up_b = jnp.sum(g_pre_low.astype(F32), axis=0)
    g_n2 = back_product(g_pre_low, up_weight)
    g_resid_part, g_ln2_gain, g_ln2_bias = ln2_pull(g_n2)
    g_resid = grad_float + g_resid_part
    g_branch_low = g_resid.astype(BF16)
    g_out_w = weight_gradient(mixed_low, g_branch_low)
    g_out_b = jnp.sum(g_branch_low.astype(F32), axis=0)
    g_mixed = back_product(g_branch_low, out_weight).reshape(row_count, tok_count, width)
    g_gate_out = g_mixed * long_seq
    g_long_low = (g_mixed * gate_out).astype(BF16)
    g_carried_low, g_taps, g_skip = long_filter.backward(to_channels(g_long_low))
    g_f1_w, g_f1_b, g_f2_w, g_f2_b, g_f3_w = filter_pull(g_taps)
    g_carried_seq = to_positions(g_carried_low).astype(F32)
    g_shorted = jnp.concatenate(
        [g_gate_out, g_carried_seq * values, g_carried_seq * gate_in], axis=-1
    )
    lead_one = keep_one * g_shorted
    lead_two = keep_two * g_shorted
    ahead = passed_along(
        jnp.concatenate([lead_one[:, :2], lead_two[:, :2]], axis=1).astype(BF16), "seq", -1
    ).astype(F32)
    after_one = jnp.concatenate([lead_one[:, 1:], ahead[:, :1]], axis=1)
    after_two = jnp.concatenate([lead_two[:, 2:], ahead[:, 2:4]], axis=1)
    g_proj = taps_short[0] * g_shorted + taps_short[1] * after_one + taps_short[2] * after_two
    g_short_w = jnp.stack(
        [
            jnp.sum(g_shorted * current, axis=(0, 1)),
            jnp.sum(lead_one * before_one, axis=(0, 1)),
            jnp.sum(lead_two * before_two, axis=(0, 1)),
        ],
        axis=0,
    )
    g_short_b = jnp.sum(g_shorted, axis=(0, 1))
    g_proj_low = g_proj.astype(BF16).reshape(flat_count, 3 * width)
    g_in_w = weight_gradient(n1_low, g_proj_low)
    g_in_b = jnp.sum(g_proj_low.astype(F32), axis=0)
    g_n1 = back_product(g_proj_low, in_weight)
    g_x_part, g_ln1_gain, g_ln1_bias = ln1_pull(g_n1)
    grad_tokens = (g_resid + g_x_part).reshape(row_count, tok_count, width)

    def lined(parts):
        flat = jnp.concatenate([part.reshape(-1) for part in parts])
        return jnp.pad(flat, (0, -flat.shape[0] % 128)).reshape(-1, 128)

    net = lined((g_f1_w, g_f1_b, g_f2_w, g_f2_b))
    net_rows = net.shape[0]
    own = lined((g_f3_w, g_skip))
    bits = device_bits()
    seq_bits = int(math.log2(seq_count))
    joint = summed(jnp.concatenate([net, own]), range(seq_bits, bits))
    net = summed(joint[:net_rows], range(seq_bits)).reshape(-1)
    own = joint[net_rows:].reshape(-1)
    g_f1_w, g_f1_b, g_f2_w, g_f2_b = (
        part.reshape(like.shape)
        for part, like in zip(
            jnp.split(net, np.cumsum([f1_weight.size, f1_bias.size, f2_weight.size, f2_bias.size])),
            (f1_weight, f1_bias, f2_weight, f2_bias),
        )
    )
    g_f3_w = own[: f3_weight.size].reshape(f3_weight.shape)
    g_skip = own[f3_weight.size : f3_weight.size + lanes]

    shares = 1 << bits
    vectors = (g_ln2_gain, g_ln2_bias, g_up_b, g_down_b, g_out_b)
    vectors += (g_ln1_gain, g_ln1_bias, g_in_b, g_short_b) + tuple(g_short_w)
    rows = jnp.concatenate([v.reshape(shares, -1) for v in vectors], axis=1)
    sums = small_scattered(rows)
    cuts = np.cumsum([v.shape[0] // shares for v in vectors])[:-1]
    (
        g_ln2_gain,
        g_ln2_bias,
        g_up_b,
        g_down_b,
        g_out_b,
        g_ln1_gain,
        g_ln1_bias,
        g_in_b,
        g_short_b,
        *g_short_w,
    ) = jnp.split(sums, cuts)
    return (
        output,
        grad_tokens,
        g_ln1_gain,
        g_ln1_bias,
        g_in_w,
        g_in_b,
        jnp.stack(g_short_w),
        g_short_b,
        g_f1_w,
        g_f1_b,
        g_f2_w,
        g_f2_b,
        g_f3_w,
        g_skip,
        g_out_w,
        g_out_b,
        g_ln2_gain,
        g_ln2_bias,
        g_up_w,
        g_up_b,
        g_down_w,
        g_down_b,
    )


HALO = 16


def turned_halves(values, share, out_ref, at):
    turned = values.T.astype(BF16)
    for run in range(turned.shape[0] // share):
        into = pl.ds(run // 2 * share, share)
        out_ref[run % 2, into, at] = turned[run * share : (run + 1) * share]


def row_of(ref):
    return ref[...].astype(F32).reshape(1, -1)


def keeps(cuts_ref, first_ref, row, count, lanes):
    spot = lax.broadcasted_iota(jnp.int32, (count, lanes), 0) + first_ref[0]

    def begins(at):
        found = at == 0
        for cut in range(cuts_ref.shape[1]):
            found = found | (at == cuts_ref[row, cut])
        return found

    here, before = begins(spot), begins(spot - 1)
    return jnp.where(here, 0.0, 1.0), jnp.where(here | before, 0.0, 1.0)


def short_filter(values, weight, shift, keep_one, keep_two, begin, count):
    one = pltpu.roll(values, 1, 0)[begin : begin + count]
    two = pltpu.roll(values, 2, 0)[begin : begin + count]
    here = values[begin : begin + count]
    return weight[0:1] * here + keep_one * (weight[1:2] * one) + keep_two * (weight[2:3] * two) + shift


def normed(values):
    center = values - jnp.mean(values, axis=-1, keepdims=True)
    spread = jnp.mean(center * center, axis=-1, keepdims=True)
    scale = lax.rsqrt(spread + eps)
    return center * scale, scale


def in_forward_kernel(
    cuts_ref,
    first_ref,
    before_ref,
    x_ref,
    beyond_ref,
    gain_ref,
    bias_ref,
    w0,
    w1,
    w2,
    b0,
    b1,
    b2,
    s1,
    s2,
    c1,
    c2,
    norm_out,
    proj_out,
    carried_out,
    norm,
):
    rows, count, width = x_ref.shape
    extent = count + 2 * HALO
    group = carried_out.shape[3]

    @pl.when(pl.program_id(0) == 0)
    def _():
        for row in range(rows):
            around = [ref[row].astype(F32) for ref in (before_ref, x_ref, beyond_ref)]
            hat, _ = normed(jnp.concatenate(around, axis=0))
            value = hat * row_of(gain_ref) + row_of(bias_ref)
            norm[row * extent : (row + 1) * extent] = value.astype(BF16)
            turned_halves(
                value[HALO : HALO + count], 32, norm_out, pl.ds(row * count, count)
            )

    parts = []
    for third, (w, b) in enumerate(((w0, b0), (w1, b1), (w2, b2))):
        part = dot32(norm[...], w[...]) + row_of(b)
        low = part.astype(BF16)
        for row in range(rows):
            proj_out[third, row] = low[row * extent : (row + 1) * extent]
        parts.append(low.astype(F32))
    lanes = parts[0].shape[1]
    for row in range(rows):
        keep_one, keep_two = keeps(cuts_ref, first_ref, row, count, lanes)
        sides = [
            short_filter(
                parts[third][row * extent : (row + 1) * extent],
                s[...].astype(F32),
                row_of(c),
                keep_one,
                keep_two,
                HALO,
                count,
            )
            for third, s, c in ((1, s1, c1), (2, s2, c2))
        ]
        carried = (sides[0] * sides[1]).astype(BF16)
        for index in range(lanes // group):
            carried_out[index, row] = carried[:, index * group : (index + 1) * group]


def smem():
    return pl.BlockSpec(memory_space=pltpu.SMEM)


def whole(shape):
    return pl.BlockSpec(shape, lambda i: (0,) * len(shape), pipeline_mode=pl.Buffered(1))


def params():
    return pltpu.CompilerParams(
        vmem_limit_bytes=VMEM_MIB * 2**20, dimension_semantics=("arbitrary",)
    )


def third_block(shape, which, steps):
    lead = (0,) * (len(shape) - 1)
    return pl.BlockSpec(shape, lambda i: lead + (which * steps + i,))


def in_forward(
    cuts, first, before, x, beyond, gain, bias, in_weight, in_bias, short_weight, short_bias, group
):
    rows, count, width = x.shape
    extent = count + 2 * HALO
    lanes = 256
    steps = width // lanes
    return pl.pallas_call(
        in_forward_kernel,
        grid=(steps,),
        in_specs=[smem(), smem(), whole(before.shape), whole(x.shape), whole(beyond.shape)]
        + [whole(gain.shape), whole(bias.shape)]
        + [third_block((width, lanes), t, steps) for t in range(3)]
        + [third_block((lanes,), t, steps) for t in range(3)]
        + [third_block((3, lanes), t, steps) for t in (1, 2)]
        + [third_block((lanes,), t, steps) for t in (1, 2)],
        out_specs=[
            whole((2, width // 2, rows * count)),
            pl.BlockSpec((3, rows, extent, lanes), lambda i: (0, 0, 0, i)),
            pl.BlockSpec((lanes // group, rows, count, group), lambda i: (i, 0, 0, 0)),
        ],
        out_shape=[
            jax.ShapeDtypeStruct((2, width // 2, rows * count), BF16),
            jax.ShapeDtypeStruct((3, rows, extent, width), BF16),
            jax.ShapeDtypeStruct((width // group, rows, count, group), BF16),
        ],
        scratch_shapes=[pltpu.VMEM((rows * extent, width), BF16)],
        compiler_params=params(),
        cost_estimate=MUCH,
        name="in_forward",
    )(
        cuts,
        first,
        before,
        x,
        beyond,
        gain,
        bias,
        *[in_weight] * 3,
        *[in_bias] * 3,
        *[short_weight] * 2,
        *[short_bias] * 2,
    )


def gates(cuts_ref, first_ref, proj_ref, weight_ref, shift_ref, row, index, group):
    at = pl.ds(index * group, group)
    extent = proj_ref.shape[2]
    count = extent - 2 * HALO
    keep_one, keep_two = keeps(cuts_ref, first_ref, row, count, group)
    return short_filter(
        proj_ref[0, row, :, at].astype(F32),
        weight_ref[:, at].astype(F32),
        shift_ref[at].astype(F32).reshape(1, -1),
        keep_one,
        keep_two,
        HALO,
        count,
    )


def middle_forward_kernel(
    cuts_ref,
    first_ref,
    long_ref,
    proj_ref,
    weight_ref,
    shift_ref,
    x_ref,
    out_w_ref,
    out_b_ref,
    gain_ref,
    bias_ref,
    up_ref,
    up_b_ref,
    g_act_ref,
    mixed_out,
    resid_out,
    norm_out,
    act_out,
    split_out,
    g_pre_out,
    g_up_b_out,
    mixed,
    norm,
):
    groups, rows, count, group = long_ref.shape

    @pl.when(pl.program_id(0) == 0)
    def _():
        for row in range(rows):
            own = pl.ds(row * count, count)
            for index in range(groups):
                gate = gates(cuts_ref, first_ref, proj_ref, weight_ref, shift_ref, row, index, group)
                value = gate * long_ref[index, row].astype(F32)
                mixed[own, pl.ds(index * group, group)] = value.astype(BF16)
        for row in range(rows):
            own = pl.ds(row * count, count)
            turned_halves(mixed[own, :].astype(F32), 32, mixed_out, own)
            branch = dot32(mixed[own, :], out_w_ref[...]) + row_of(out_b_ref)
            resid = x_ref[own, :].astype(F32) + branch
            resid_out[own, :] = resid
            hat, _ = normed(resid)
            value = hat * row_of(gain_ref) + row_of(bias_ref)
            norm[own, :] = value.astype(BF16)
            turned_halves(value, 32, norm_out, own)

    pre = dot32(norm[...], up_ref[...]) + row_of(up_b_ref)
    scale = math.sqrt(2.0 / math.pi)
    square = pre * pre
    inner = pre * (scale + (scale * 0.044715) * square)
    half = 0.5 + 0.5 * jnp.tanh(inner)
    act = pre * half
    act_out[...] = act.astype(BF16)
    turned_halves(act, 128, split_out, pl.ds(0, act.shape[0]))
    slope = pre * (2.0 * scale + (6.0 * scale * 0.044715) * square)
    slope = half + slope * (half * (1.0 - half))
    g_pre = (g_act_ref[...].astype(F32) * slope).astype(BF16)
    g_pre_out[...] = g_pre
    g_up_b_out[...] = jnp.sum(g_pre.astype(F32), axis=0, keepdims=True)


def middle_forward(
    cuts, first, long, proj, short_weight, short_bias, x, out_w, out_b, gain, bias, up, up_b, g_act
):
    groups, rows, count, group = long.shape
    extent = proj.shape[2]
    tokens, width = x.shape
    hidden = up.shape[1]
    lanes = width
    steps = hidden // lanes

    def part(height):
        return pl.BlockSpec((height, lanes), lambda i: (0, i))

    return pl.pallas_call(
        middle_forward_kernel,
        grid=(steps,),
        in_specs=[
            smem(),
            smem(),
            whole(long.shape),
            whole((1, rows, extent, width)),
            whole((3, width)),
            whole((width,)),
            whole((tokens, width)),
            whole((width, width)),
            whole((width,)),
            whole((width,)),
            whole((width,)),
            part(width),
            pl.BlockSpec((lanes,), lambda i: (i,)),
            part(tokens),
        ],
        out_specs=[
            whole((2, width // 2, tokens)),
            whole((tokens, width)),
            whole((2, width // 2, tokens)),
            part(tokens),
            pl.BlockSpec((2, lanes // 2, tokens), lambda i: (0, i, 0)),
            part(tokens),
            part(1),
        ],
        out_shape=[
            jax.ShapeDtypeStruct((2, width // 2, tokens), BF16),
            jax.ShapeDtypeStruct((tokens, width), F32),
            jax.ShapeDtypeStruct((2, width // 2, tokens), BF16),
            jax.ShapeDtypeStruct((tokens, hidden), BF16),
            jax.ShapeDtypeStruct((2, hidden // 2, tokens), BF16),
            jax.ShapeDtypeStruct((tokens, hidden), BF16),
            jax.ShapeDtypeStruct((1, hidden), F32),
        ],
        scratch_shapes=[pltpu.VMEM((tokens, width), BF16), pltpu.VMEM((tokens, width), BF16)],
        compiler_params=params(),
        cost_estimate=MUCH,
        name="middle_forward",
    )(
        cuts,
        first,
        long,
        proj,
        short_weight,
        short_bias,
        x,
        out_w,
        out_b,
        gain,
        bias,
        up,
        up_b,
        g_act,
    )


def turned_dot(left, right):
    return lax.dot_general(left, right, (((1,), (1,)), ((), ())), preferred_element_type=F32)


def normed_back(values, grad, gain):
    hat, scale = normed(values)
    inward = grad * gain
    mean = jnp.mean(inward, axis=-1, keepdims=True)
    along = jnp.mean(inward * hat, axis=-1, keepdims=True)
    g_gain = jnp.sum(grad * hat, axis=0, keepdims=True)
    return scale * (inward - mean - hat * along), g_gain, jnp.sum(grad, axis=0, keepdims=True)


def fetched(step, last, sources, targets, sems):
    @pl.when(step == 0)
    def _():
        for k, (source, target) in enumerate(zip(sources, targets)):
            pltpu.make_async_copy(source, target, sems.at[k]).start()

    @pl.when(step == last)
    def _():
        for k, (source, target) in enumerate(zip(sources, targets)):
            pltpu.make_async_copy(source, target, sems.at[k]).wait()


def middle_backward_kernel(
    cuts_ref,
    first_ref,
    long_at,
    proj_at,
    weight_ref,
    shift_ref,
    resid_at,
    grad_at,
    gain_ref,
    out_w_at,
    g_pre_ref,
    up_ref,
    _,
    g_long_out,
    g_gate_out,
    g_resid_out,
    g_branch_out,
    sums_out,
    token_out,
    total,
    long_ref,
    proj_ref,
    resid_ref,
    grad_ref,
    out_w_ref,
    sems,
):
    groups, rows, count, group = long_ref.shape
    step = pl.program_id(0)
    token_out[0] = 0
    fetched(
        step,
        pl.num_programs(0) - 1,
        (long_at, proj_at.at[pl.ds(0, 1)], resid_at, grad_at, out_w_at),
        (long_ref, proj_ref, resid_ref, grad_ref, out_w_ref),
        sems,
    )

    @pl.when(step == 0)
    def _():
        total[...] = turned_dot(g_pre_ref[...], up_ref[...])

    @pl.when(step > 0)
    def _():
        total[...] += turned_dot(g_pre_ref[...], up_ref[...])

    @pl.when(step == pl.num_programs(0) - 1)
    def _():
        sums = [0.0] * 4
        for row in range(rows):
            own = pl.ds(row * count, count)
            grad = grad_ref[own, :].astype(F32)
            back, g_gain, g_bias = normed_back(
                resid_ref[own, :], total[own, :], row_of(gain_ref)
            )
            g_resid = grad + back
            g_resid_out[own, :] = g_resid
            low = g_resid.astype(BF16)
            g_branch_out[own, :] = low
            g_out_b = jnp.sum(low.astype(F32), axis=0, keepdims=True)
            g_down_b = jnp.sum(grad, axis=0, keepdims=True)
            sums = [a + b for a, b in zip(sums, (g_gain, g_bias, g_out_b, g_down_b))]
            total[own, :] = turned_dot(low, out_w_ref[...])
        sums_out[...] = jnp.concatenate(sums + [jnp.zeros_like(sums[0])] * 4, axis=0)
        for row in range(rows):
            own = pl.ds(row * count, count)
            for index in range(groups):
                at = pl.ds(index * group, group)
                g_mixed = total[own, at]
                gate = gates(cuts_ref, first_ref, proj_ref, weight_ref, shift_ref, row, index, group)
                g_gate_out[row, :, at] = g_mixed * long_ref[index, row].astype(F32)
                g_long_out[index, row] = (g_mixed * gate).astype(BF16)


def middle_backward(
    cuts, first, long, proj, short_weight, short_bias, resid, grad, gain, out_w, g_pre, up, ready
):
    groups, rows, count, group = long.shape
    extent = proj.shape[2]
    tokens, width = resid.shape
    hidden = up.shape[1]
    lanes = 1024
    steps = hidden // lanes

    def part(height):
        return pl.BlockSpec((height, lanes), lambda i: (0, i))

    anywhere = pl.BlockSpec(memory_space=pl.ANY)
    return pl.pallas_call(
        middle_backward_kernel,
        grid=(steps,),
        in_specs=[
            smem(),
            smem(),
            anywhere,
            anywhere,
            whole((3, width)),
            whole((width,)),
            anywhere,
            anywhere,
            whole((width,)),
            anywhere,
            part(tokens),
            part(width),
            pl.BlockSpec(memory_space=pl.ANY),
        ],
        out_specs=[
            whole(long.shape),
            whole((rows, count, width)),
            whole((tokens, width)),
            whole((tokens, width)),
            whole((8, width)),
            smem(),
        ],
        out_shape=[
            jax.ShapeDtypeStruct(long.shape, BF16),
            jax.ShapeDtypeStruct((rows, count, width), F32),
            jax.ShapeDtypeStruct((tokens, width), F32),
            jax.ShapeDtypeStruct((tokens, width), BF16),
            jax.ShapeDtypeStruct((8, width), F32),
            jax.ShapeDtypeStruct((1,), jnp.int32),
        ],
        scratch_shapes=[
            pltpu.VMEM((tokens, width), F32),
            pltpu.VMEM(long.shape, BF16),
            pltpu.VMEM((1, rows, extent, width), BF16),
            pltpu.VMEM((tokens, width), F32),
            pltpu.VMEM((tokens, width), BF16),
            pltpu.VMEM((width, width), BF16),
            pltpu.SemaphoreType.DMA((5,)),
        ],
        compiler_params=params(),
        cost_estimate=MUCH,
        name="middle_backward",
    )(
        cuts,
        first,
        long,
        proj,
        short_weight,
        short_bias,
        resid,
        grad,
        gain,
        out_w,
        g_pre,
        up,
        ready,
    )


def in_backward_kernel(
    cuts_ref,
    first_ref,
    g_carried_ref,
    g_gate_ref,
    g_next_ref,
    proj_ref,
    s0,
    s1,
    s2,
    c1,
    c2,
    w0,
    w1,
    w2,
    x_at,
    gain_ref,
    g_resid_at,
    *others,
):
    g_proj_out, sums_out, g_tokens_out, norm_sums_out, token_out = others[-9:-4]
    total, x_ref, g_resid_ref, sems = others[-4:]
    token_out[0] = 0
    fetched(
        pl.program_id(0),
        pl.num_programs(0) - 1,
        (x_at, g_resid_at),
        (x_ref, g_resid_ref),
        sems,
    )
    weights = [s[...].astype(F32) for s in (s0, s1, s2)]
    shifts = [None, row_of(c1), row_of(c2)]
    _, rows, extent, lanes = proj_ref.shape
    count = extent - 2 * HALO
    reach = count + HALO
    group = g_carried_ref.shape[3]
    step = pl.program_id(0)
    sums = [[0.0] * 5 for _ in range(3)]
    for row in range(rows):
        keep_one, keep_two = keeps(cuts_ref, first_ref, row, reach, lanes)
        values = [proj_ref[third, row].astype(F32) for third in range(3)]
        sides = [
            short_filter(
                values[t], weights[t], shifts[t], keep_one, keep_two, HALO, reach
            )
            for t in (1, 2)
        ]
        g_carried = jnp.concatenate(
            [g_carried_ref[index, row] for index in range(lanes // group)], axis=1
        ).astype(F32)
        g_gate = jnp.concatenate([g_gate_ref[row], g_next_ref[row].astype(F32)], axis=0)
        grads = (g_gate, g_carried * sides[1], g_carried * sides[0])
        for third, grad in enumerate(grads):
            weight = weights[third]
            lead_one, lead_two = keep_one * grad, keep_two * grad
            g_proj = (
                weight[0:1] * grad
                + weight[1:2] * pltpu.roll(lead_one, reach - 1, 0)
                + weight[2:3] * pltpu.roll(lead_two, reach - 2, 0)
            )[:count]
            low = g_proj.astype(BF16)
            g_proj_out[third, row * count : (row + 1) * count] = low
            before_one = pltpu.roll(values[third], 1, 0)[HALO : HALO + count]
            before_two = pltpu.roll(values[third], 2, 0)[HALO : HALO + count]
            here = values[third][HALO : HALO + count]
            parts = (
                grad[:count] * here,
                lead_one[:count] * before_one,
                lead_two[:count] * before_two,
                grad[:count],
                low.astype(F32),
            )
            sums[third] = [
                a + jnp.sum(b, axis=0, keepdims=True) for a, b in zip(sums[third], parts)
            ]
    for third in range(3):
        sums_out[third] = jnp.concatenate(
            sums[third] + [jnp.zeros((3, lanes), F32)], axis=0
        )
    product = sum(
        turned_dot(g_proj_out[third], w[...]) for third, w in enumerate((w0, w1, w2))
    )

    @pl.when(step == 0)
    def _():
        total[...] = product

    @pl.when(step > 0)
    def _():
        total[...] += product

    @pl.when(step == pl.num_programs(0) - 1)
    def _():
        norm_sums = [0.0, 0.0]
        for row in range(rows):
            own = pl.ds(row * count, count)
            back, g_gain, g_shift = normed_back(
                x_ref[own, :].astype(F32), total[own, :], row_of(gain_ref)
            )
            g_tokens_out[own, :] = g_resid_ref[own, :] + back
            norm_sums = [norm_sums[0] + g_gain, norm_sums[1] + g_shift]
        norm_sums_out[...] = jnp.concatenate(
            norm_sums + [jnp.zeros((6, x_ref.shape[1]), F32)], axis=0
        )


def in_backward(
    cuts,
    first,
    g_carried,
    g_gate,
    g_next,
    proj,
    short_weight,
    short_bias,
    in_w,
    x,
    gain,
    g_resid,
    ready,
):
    _, rows, extent, width = proj.shape
    count = extent - 2 * HALO
    tokens = rows * count
    group = g_carried.shape[3]
    lanes = 256
    steps = width // lanes

    anywhere = pl.BlockSpec(memory_space=pl.ANY)
    return pl.pallas_call(
        in_backward_kernel,
        grid=(steps,),
        in_specs=[
            smem(),
            smem(),
            pl.BlockSpec((lanes // group, rows, count + HALO, group), lambda i: (i, 0, 0, 0)),
            pl.BlockSpec((rows, count, lanes), lambda i: (0, 0, i)),
            pl.BlockSpec((rows, HALO, lanes), lambda i: (0, 0, i)),
            pl.BlockSpec((3, rows, extent, lanes), lambda i: (0, 0, 0, i)),
        ]
        + [third_block((3, lanes), t, steps) for t in range(3)]
        + [third_block((lanes,), t, steps) for t in (1, 2)]
        + [third_block((width, lanes), t, steps) for t in range(3)]
        + [anywhere, whole((width,)), anywhere]
        + [pl.BlockSpec(memory_space=pl.ANY)] * len(ready),
        out_specs=[
            pl.BlockSpec((3, tokens, lanes), lambda i: (0, 0, i)),
            pl.BlockSpec((3, 8, lanes), lambda i: (0, 0, i)),
            whole((tokens, width)),
            whole((8, width)),
            smem(),
        ],
        out_shape=[
            jax.ShapeDtypeStruct((3, tokens, width), BF16),
            jax.ShapeDtypeStruct((3, 8, width), F32),
            jax.ShapeDtypeStruct((tokens, width), F32),
            jax.ShapeDtypeStruct((8, width), F32),
            jax.ShapeDtypeStruct((1,), jnp.int32),
        ],
        scratch_shapes=[
            pltpu.VMEM((tokens, width), F32),
            pltpu.VMEM((tokens, width), BF16),
            pltpu.VMEM((tokens, width), F32),
            pltpu.SemaphoreType.DMA((2,)),
        ],
        compiler_params=params(),
        cost_estimate=MUCH,
        name="in_backward",
    )(
        cuts,
        first,
        g_carried,
        g_gate,
        g_next,
        proj,
        *[short_weight] * 3,
        *[short_bias] * 2,
        *[in_w] * 3,
        x,
        gain,
        g_resid,
        *ready,
    )


def mark(*others):
    def kernel(*refs):
        refs[-1][0] = 0

    return pl.pallas_call(
        kernel,
        in_specs=[pl.BlockSpec(memory_space=pl.ANY)] * len(others),
        out_specs=smem(),
        out_shape=jax.ShapeDtypeStruct((1,), jnp.int32),
        cost_estimate=LITTLE,
        name="mark",
    )(*others)


def matmul_turned(left, right, columns, ready):
    def kernel(left_ref, right_ref, _, out_ref):
        out_ref[...] = turned_dot(left_ref[...], right_ref[...]).astype(BF16)

    height, depth = left.shape
    width = right.shape[0]
    return pl.pallas_call(
        kernel,
        grid=(width // columns,),
        in_specs=[
            whole((height, depth)),
            pl.BlockSpec((columns, depth), lambda i: (i, 0)),
            pl.BlockSpec(memory_space=pl.ANY),
        ],
        out_specs=pl.BlockSpec((height, columns), lambda i: (0, i)),
        out_shape=jax.ShapeDtypeStruct((height, width), BF16),
        compiler_params=params(),
        cost_estimate=LITTLE,
        name="matmul_turned",
    )(left, right, ready)


def down_forward(resid, act, down, bias, ready):
    tokens, width = resid.shape
    depth = 1024
    steps = act.shape[1] // depth

    def kernel(resid_ref, act_ref, down_ref, bias_ref, *refs):
        out_ref, token_out, total = refs[-3:]
        step = pl.program_id(0)
        token_out[0] = 0
        product = dot32(act_ref[...], down_ref[...])

        @pl.when(step == 0)
        def _():
            total[...] = resid_ref[...] + row_of(bias_ref) + product

        @pl.when(step > 0)
        def _():
            total[...] += product

        @pl.when(step == steps - 1)
        def _():
            out_ref[...] = total[...].astype(BF16)

    return pl.pallas_call(
        kernel,
        grid=(steps,),
        in_specs=[
            whole((tokens, width)),
            pl.BlockSpec((tokens, depth), lambda i: (0, i)),
            pl.BlockSpec((depth, width), lambda i: (i, 0)),
            whole((width,)),
        ]
        + [pl.BlockSpec(memory_space=pl.ANY)] * len(ready),
        out_specs=[whole((tokens, width)), smem()],
        out_shape=[
            jax.ShapeDtypeStruct((tokens, width), BF16),
            jax.ShapeDtypeStruct((1,), jnp.int32),
        ],
        scratch_shapes=[pltpu.VMEM((tokens, width), F32)],
        compiler_params=params(),
        cost_estimate=LITTLE,
        name="down_forward",
    )(resid, act, down, bias, *ready)


def after(value, *others):
    return lax.optimization_barrier((value, others))[0]


def gradient_kernel(counts, order_ref, firsts, seconds, arrived, sent, kept, token, total):
    step = pl.program_id(0)
    token[0] = 0

    def write(values, place):
        if not kept:
            sent[place][...] = values.astype(BF16)
            return
        (send,), (keep,), (total_ref,) = sent, kept, total
        total_ref[...] = values
        share = total_ref.shape[0] // 16
        for spot in range(16):
            piece = pl.ds(pl.multiple_of(order_ref[1 + spot] * share, share), share)
            into = (send, keep)[spot // 8]
            into[pl.ds(spot % 8 * share, share)] = (
                total_ref[piece] + arrived[place][piece].astype(F32)
            ).astype(BF16)

    place = 0
    for steps, first, second in zip(counts, firsts, seconds):
        for _ in range(steps):

            @pl.when(step == place)
            def _(first=first, second=second, place=place):
                write(dot32(first[0], second[...]), place)

            place += 1


def gradient(order, pairs, arrived, ready, columns, cost=LITTLE):
    height, tokens = pairs[0][0].shape[1:]
    counts, first_specs, second_specs, begin = [], [], [], 0
    for first, second in pairs:
        parts = second.shape[-1] // columns
        steps = parts * (second.shape[0] if second.ndim == 3 else 1)
        first_specs.append(pl.BlockSpec((1, height, tokens), lambda i, o: (o[0], 0, 0)))

        def place(i, o, begin=begin, steps=steps, parts=parts, deep=second.ndim == 3):
            at = jnp.clip(i - begin, 0, steps - 1)
            return (at // parts, 0, at % parts) if deep else (0, at)

        shape = (None, tokens, columns) if second.ndim == 3 else (tokens, columns)
        second_specs.append(pl.BlockSpec(shape, place))
        counts.append(steps)
        begin += steps
    single = pl.BlockSpec((height, columns), lambda i, o: (0, 0), pipeline_mode=pl.Buffered(1))
    anywhere = pl.BlockSpec(memory_space=pl.ANY)
    if arrived is None:
        arrived = ()
        sent = [jax.ShapeDtypeStruct((height, columns), BF16)] * begin
        kept, scratch = [], []
        out_specs = [single] * begin
    else:
        sent = [jax.ShapeDtypeStruct((height // 2, begin * columns), BF16)]
        kept, scratch = sent, [pltpu.VMEM((height, columns), F32)]
        out_specs = [pl.BlockSpec((height // 2, columns), lambda i, o: (0, i))] * 2

    def kernel(order_ref, *refs):
        refs = list(refs)

        def take(count):
            taken, refs[:] = refs[:count], refs[count:]
            return taken

        firsts, seconds, arrived_refs = take(len(pairs)), take(len(pairs)), take(len(arrived))
        take(len(ready))
        sent_refs, kept_refs, (token,) = take(len(sent)), take(len(kept)), take(1)
        gradient_kernel(
            counts, order_ref, firsts, seconds, arrived_refs, sent_refs, kept_refs, token, refs
        )

    inputs = [p[0] for p in pairs] + [p[1] for p in pairs] + list(arrived) + list(ready)
    outputs = sent + kept + [jax.ShapeDtypeStruct((1,), jnp.int32)]
    return pl.pallas_call(
        kernel,
        grid_spec=pltpu.PrefetchScalarGridSpec(
            num_scalar_prefetch=1,
            grid=(begin,),
            in_specs=first_specs
            + second_specs
            + [single] * len(arrived)
            + [anywhere] * len(ready),
            out_specs=out_specs + [smem()],
            scratch_shapes=scratch,
        ),
        out_shape=outputs,
        compiler_params=params(),
        cost_estimate=cost,
        name="gradient",
    )(order, *inputs)


def to_sibling(blocks):
    return [swapped(block, lambda one: 1) for block in blocks]


def bit_of(index, bit):
    return (index >> bit) & 1


def choose_bit(index, bit, axis):
    def choose(array, mine):
        own = bit_of(index, bit)
        return pick(array, own if mine else 1 - own, axis)

    return choose


def choose_second(index, axis):
    def choose(array, mine):
        own = jnp.where(bit_of(index, 0) == 0, bit_of(index, 2), bit_of(index, 1))
        return pick(array, own if mine else 1 - own, axis)

    return choose


def choose_first(index, axis):
    def choose(array, mine):
        low, high = bit_of(index, 1), bit_of(index, 2)
        if not mine:
            low, high = 1 - low, 1 - high
        core = bit_of(index, 0)
        return jnp.stack(
            [
                pick(array, jnp.where(core == 0, 2 * j + low, 2 * high + j), axis)
                for j in range(2)
            ],
            axis=axis,
        )

    return choose


def swap_bit(bit):
    return lambda value: swapped(value, lambda one: 1 << bit)


def swap_first(value):
    return swapped(value, lambda one: 4 if one & 1 else 2)


def swap_second(value):
    return swapped(value, lambda one: 2 if one & 1 else 4)


def order_first(index):
    core, low, high = bit_of(index, 0), bit_of(index, 1), bit_of(index, 2)

    def some(low, high):
        return [
            4 * z + jnp.where(core == 0, 2 * j + low, 2 * high + j) for z in range(4) for j in range(2)
        ]

    return jnp.stack([core] + some(1 - low, 1 - high) + some(low, high)).astype(jnp.int32)


def stage_sent(kept, arrived, choose):
    return added(choose(kept, False), choose(arrived, False), BF16)


def stage(kept, arrived, choose):
    sent = stage_sent(kept, arrived, choose)
    return sent, added(choose(kept, True), choose(arrived, True), BF16)


def finished(kept, arrived, own, last, cuts, ready):
    rows, width = last.shape[-2:]
    last = last.reshape(rows, width)

    def kernel(own_ref, kept_ref, arrived_ref, last_ref, *refs):
        outs = refs[len(ready) : len(ready) + len(cuts)]
        refs[-1][0] = 0
        begin = 0
        for out, size in zip(outs, cuts):
            at = slice(begin, begin + size)
            first = kept_ref[:, at].astype(F32) + arrived_ref[:, at].astype(F32)
            out[...] = first + last_ref[:, at].astype(F32)
            begin += size

    half = pl.BlockSpec((None, rows, width), lambda i, o: (o[0], 0, 0))

    def flat(columns):
        return pl.BlockSpec((rows, columns), lambda i, o: (0, 0))

    *outs, token = pl.pallas_call(
        kernel,
        grid_spec=pltpu.PrefetchScalarGridSpec(
            num_scalar_prefetch=1,
            grid=(1,),
            in_specs=[half, half, flat(width)]
            + [pl.BlockSpec(memory_space=pl.ANY)] * len(ready),
            out_specs=[flat(size) for size in cuts] + [smem()],
        ),
        out_shape=[jax.ShapeDtypeStruct((rows, size), F32) for size in cuts]
        + [jax.ShapeDtypeStruct((1,), jnp.int32)],
        compiler_params=params(),
        cost_estimate=LITTLE,
        name="finished",
    )(
        own.astype(jnp.int32).reshape(1),
        kept.reshape(2, rows, width),
        arrived.reshape(2, rows, width),
        last,
        *ready,
    )
    return outs, token


def paired(values):
    while len(values) > 1:
        values = [values[k] + values[k + 1] for k in range(0, len(values), 2)]
    return values[0]


def summed_lines(values, top, ready, cut=True):
    rows, lanes = values[0].shape
    rest = top if cut else 0
    count = len(values)

    def kernel(*refs):
        total = paired([ref[...] for ref in refs[:count]])
        refs[-3][...] = total[:top]
        refs[-2][...] = total[rest:]
        refs[-1][0] = 0

    return pl.pallas_call(
        kernel,
        grid=(1,),
        in_specs=[whole((rows, lanes))] * count + [pl.BlockSpec(memory_space=pl.ANY)] * len(ready),
        out_specs=[whole((top, lanes)), whole((rows - rest, lanes)), smem()],
        out_shape=[
            jax.ShapeDtypeStruct((top, lanes), F32),
            jax.ShapeDtypeStruct((rows - rest, lanes), F32),
            jax.ShapeDtypeStruct((1,), jnp.int32),
        ],
        compiler_params=params(),
        cost_estimate=LITTLE,
        name="summed_lines",
    )(*values, *ready)


def unpacked(seq, seq_count, top, values, units, bands, sizes, ready):
    lanes = top.shape[1]
    count = len(values)

    def kernel(seq_ref, top_ref, *refs):
        outs, below, token = refs[count + len(ready) : -2], refs[-1], refs[-2]
        token[0] = 0
        below[...] = paired([ref[...] for ref in refs[:count]])
        f1_w, f1_b, f2_w, f2_b, f3_w, skip = outs[:6]
        f3_w[...] = top_ref[:units]
        skip[...] = top_ref[units]
        f2_w[...] = below[:units, :units]
        f1_w[...] = below[:bands, units:]
        f1_b[...] = below[bands, units:]
        f2_b[...] = below[bands + 1, units:]
        line, seq = units, seq_ref[0]
        outs = list(outs[6:])
        for kinds, size in sizes:
            begin = seq * size
            for kind in range(kinds):
                at = line + begin // lanes
                two = jnp.concatenate([below[pl.ds(at, 1)], below[pl.ds(at + 1, 1)]], axis=1)
                shift = lax.rem(2 * lanes - begin % lanes, 2 * lanes)
                outs.pop(0)[...] = pltpu.roll(two, shift, 1)[0, :size]
                line += size * seq_count // lanes

    shapes = [(bands, units), (units,), (units, units), (units,), (units, lanes), (lanes,)]
    shapes += [(size,) for kinds, size in sizes for _ in range(kinds)]
    return pl.pallas_call(
        kernel,
        grid=(1,),
        in_specs=[smem(), whole(top.shape)]
        + [whole(values[0].shape)] * count
        + [pl.BlockSpec(memory_space=pl.ANY)] * len(ready),
        out_specs=[whole(shape) for shape in shapes] + [smem()],
        out_shape=[jax.ShapeDtypeStruct(shape, F32) for shape in shapes]
        + [jax.ShapeDtypeStruct((1,), jnp.int32)],
        scratch_shapes=[pltpu.VMEM(values[0].shape, F32)],
        compiler_params=params(),
        cost_estimate=LITTLE,
        name="unpacked",
    )(seq, top, *values, *ready)


def block_device(
    tokens,
    cotangent,
    bounds,
    ln1_gain,
    ln1_bias,
    in_weight,
    in_bias,
    short_weight,
    short_bias,
    f1_weight,
    f1_bias,
    f2_weight,
    f2_bias,
    f3_weight,
    filter_skip,
    out_weight,
    out_bias,
    ln2_gain,
    ln2_bias,
    up_weight,
    up_bias,
    down_weight,
    down_bias,
):
    seq_count = lax.axis_size("seq")
    rows, count, width = tokens.shape
    flat = rows * count
    length = count * seq_count
    lanes = f3_weight.shape[1]
    first_channel = (lax.axis_index("seq") * lanes).astype(jnp.int32)
    first = (lax.axis_index("seq") * count).astype(jnp.int32).reshape(1)

    def exchanged(array):
        return lax.all_to_all(array, "seq", split_axis=0, concat_axis=0, tiled=True)

    index = device_index()
    before = passed_along(tokens[:, count - HALO :], "seq", 1)
    beyond = passed_along(tokens[:, :HALO], "seq", -1)
    norm_halves, proj, carried_own = in_forward(
        bounds,
        first,
        before,
        tokens,
        beyond,
        ln1_gain,
        ln1_bias,
        in_weight,
        in_bias,
        short_weight,
        short_bias,
        lanes,
    )
    carried = exchanged(carried_own)

    tables = transform_tables(count)
    table = piece_table(bounds, seq_count, count)
    skip = filter_skip
    taps_spec, kept = taps_and_spectrum(
        first_channel.reshape(1),
        seq_count,
        count,
        f1_weight,
        f1_bias,
        f2_weight,
        f2_bias,
        f3_weight,
        tables,
        carried_own,
    )
    long_own = long_forward(table, carried, taps_spec, skip, tables)
    long = exchanged(long_own)
    x = tokens.reshape(flat, width)
    grad = cotangent.reshape(flat, width)
    g_act = matmul_turned(grad, down_weight, 1024, long_own)
    mixed_halves, resid, norm2_halves, act, act_halves, g_pre, g_up_b = middle_forward(
        bounds,
        first,
        long,
        proj,
        short_weight,
        short_bias,
        x,
        out_weight,
        out_bias,
        ln2_gain,
        ln2_bias,
        up_weight,
        up_bias,
        g_act,
    )
    first_order = order_first(index)
    send_order = (1 - bit_of(index, 0)).astype(jnp.int32).reshape(1)
    down_pairs = [(act_halves, grad)]
    *down_sent, _ = gradient(send_order, down_pairs, None, (), 512)
    down_arrived = to_sibling(down_sent)
    *up_sent, _ = gradient(send_order, [(norm2_halves, g_pre)], None, down_sent, 1024)
    up_arrived = to_sibling(up_sent)
    down_send, down_keep, _ = gradient(first_order, down_pairs, down_arrived, up_sent, 512)
    down_arrived = swap_first(down_send)
    g_long, g_gate, g_resid, g_branch, middle_sums, token = middle_backward(
        bounds,
        first,
        long,
        proj,
        short_weight,
        short_bias,
        resid,
        grad,
        ln2_gain,
        out_weight,
        g_pre,
        up_weight,
        down_send,
    )
    g_long_all = exchanged(g_long)
    g_next = passed_along(g_gate[:, :HALO].astype(BF16), "seq", -1)

    def shaped(array, lead):
        return array.reshape(lead + (-1, array.shape[-1]))

    *out_sent, _ = gradient(send_order, [(mixed_halves, g_branch)], None, (), 1024)
    up_send, up_keep, token = gradient(
        first_order,
        [(norm2_halves, g_pre), (mixed_halves, g_branch)],
        up_arrived + to_sibling(out_sent),
        (),
        1024,
    )
    up_arrived = swap_first(up_send)
    down_send, down_keep = stage(
        shaped(down_keep, (2, 2, 2)),
        shaped(down_arrived, (2, 2, 2)),
        choose_bit(index + token[0], 3, 1),
    )
    down_arrived = swap_bit(3)(down_send)
    g_series, g_taps, g_skip, token = long_backward(
        table, g_long_all, carried, taps_spec, skip, tables, (up_send, down_send)
    )
    g_carried = exchanged(g_series)
    output, token = down_forward(resid, act, down_weight, down_bias, (g_series,))
    output = output.reshape(rows, count, width)
    later = index + token[0]
    down_send, down_keep = stage(down_keep, down_arrived, choose_bit(later, 4, 0))
    down_arrived = swap_bit(4)(down_send)
    up_send, up_keep = stage(
        shaped(up_keep, (4, 2)), shaped(up_arrived, (4, 2)), choose_second(later, 1)
    )
    up_arrived = swap_second(up_send)
    g_proj, short_sums, g_tokens, norm_sums, token = in_backward(
        bounds,
        first,
        g_carried,
        g_gate,
        g_next,
        proj,
        short_weight,
        short_bias,
        in_weight,
        x,
        ln1_gain,
        g_resid,
        (down_send, up_send),
    )
    later = index + token[0]
    down_send = stage_sent(down_keep, down_arrived, choose_second(later, 0))
    down_last = swap_second(down_send)
    up_send, up_keep = stage(
        shaped(up_keep, (2, 2)), shaped(up_arrived, (2, 2)), choose_bit(later, 3, 1)
    )
    up_arrived = swap_bit(3)(up_send)
    in_pairs = [(norm_halves, g_proj)]
    *in_sent, _ = gradient(send_order, in_pairs, None, (down_send, up_send), 1024, MUCH)
    in_send, in_keep, token = gradient(first_order, in_pairs, to_sibling(in_sent), (), 1024)
    in_arrived = swap_first(in_send)
    row_count = lax.axis_size("rows")
    seq_bits = seq_count.bit_length() - 1
    payloads = filter_backward(
        first_channel.reshape(1),
        lax.axis_index("rows").astype(jnp.int32).reshape(1),
        row_count,
        g_taps.reshape(length, lanes),
        kept,
        f2_weight,
        f3_weight,
        g_skip,
        (middle_sums, g_up_b, norm_sums, short_sums),
        (in_send,),
    )
    arrived = [payloads[0]] + [
        swapped(payloads[k], lambda one, k=k: k << seq_bits) for k in range(1, row_count)
    ]
    later = index + mark(*payloads)[0]
    up_send = stage_sent(up_keep, up_arrived, choose_bit(later, 4, 0))
    up_last = swap_bit(4)(up_send)
    left = jnp.where(bit_of(index, 0) == 0, bit_of(index, 2), bit_of(index, 1))
    (g_down_w,), token = finished(
        down_keep, down_arrived, left, down_last, (width,), (up_send,)
    )
    units, bands = f3_weight.shape[0], f1_weight.shape[0]
    top, mine, token = summed_lines(arrived, units + 8, (token,))
    in_send, in_keep = stage(
        shaped(in_keep, (4, 2)),
        shaped(in_arrived, (4, 2)),
        choose_second(index + token[0], 1),
    )
    in_arrived = swap_second(in_send)
    arrived = swapped(mine, lambda one: 1)
    _, mine, token = summed_lines([mine, arrived], 8, (in_send,), False)
    in_send, in_keep = stage(
        shaped(in_keep, (2, 2)), shaped(in_arrived, (2, 2)), choose_bit(index + token[0], 3, 1)
    )
    in_arrived = swap_bit(3)(in_send)
    arrived = swapped(mine, lambda one: 2)
    _, mine, token = summed_lines([mine, arrived], 8, (in_send,), False)
    (g_up_w, g_out_w), token = finished(
        up_keep, up_arrived, bit_of(index, 4), up_last, (up_weight.shape[1], width), (token,)
    )
    in_send = stage_sent(in_keep, in_arrived, choose_bit(index + token[0], 4, 0))
    in_last = swap_bit(4)(in_send)
    arrived = swapped(mine, lambda one: 4)
    shares = 1 << device_bits()
    sizes = ((6, width // shares), (1, up_weight.shape[1] // shares), (5, 3 * width // shares))
    seq = lax.axis_index("seq").astype(jnp.int32).reshape(1)
    *small, token = unpacked(
        seq, seq_count, top, [mine, arrived], units, bands, sizes, (in_send,)
    )
    (g_in_w,), _ = finished(
        in_keep, in_arrived, bit_of(index, 4), in_last, (3 * width,), (token,)
    )
    (g_f1_w, g_f1_b, g_f2_w, g_f2_b, g_f3_w, g_skip, *small) = small
    (g_ln2_gain, g_ln2_bias, g_out_b, g_down_b, g_ln1_gain, g_ln1_bias, g_up_b, *small) = small
    *g_short_w, g_short_b, g_in_b = small
    g_short_w = jnp.stack(g_short_w)
    grad_tokens = g_tokens.reshape(rows, count, width)
    return (
        output,
        grad_tokens,
        g_ln1_gain,
        g_ln1_bias,
        g_in_w,
        g_in_b,
        g_short_w,
        g_short_b,
        g_f1_w,
        g_f1_b,
        g_f2_w,
        g_f2_b,
        g_f3_w,
        g_skip,
        g_out_w,
        g_out_b,
        g_ln2_gain,
        g_ln2_bias,
        g_up_w,
        g_up_b,
        g_down_w,
        g_down_b,
    )


def per_device(tokens, *others):
    shares = lax.axis_size("rows") * lax.axis_size("seq")
    count, width = tokens.shape[1:]
    hidden = others[20].shape[0]
    lanes = width // lax.axis_size("seq")
    fits = shares == 32 and width == 1024 and hidden == 4096 and lanes == 128 and count % 128 == 0
    return (block_device if fits else plain_device)(tokens, *others)


def solution(mesh):
    return jax.shard_map(
        per_device,
        mesh=mesh,
        in_specs=(
            P("rows", "seq", None),
            P("rows", "seq", None),
            P("rows", None),
            P(),
            P(),
            P(),
            P(),
            P(),
            P(),
            P(),
            P(),
            P(),
            P(),
            P(None, "seq"),
            P("seq"),
            P(),
            P(),
            P(),
            P(),
            P(),
            P(),
            P(),
            P(),
        ),
        out_specs=(
            P("rows", "seq", None),
            P("rows", "seq", None),
            P(("rows", "seq")),
            P(("rows", "seq")),
            P(("rows", "seq"), None),
            P(("rows", "seq")),
            P(None, ("rows", "seq")),
            P(("rows", "seq")),
            P(),
            P(),
            P(),
            P(),
            P(None, "seq"),
            P("seq"),
            P(("rows", "seq"), None),
            P(("rows", "seq")),
            P(("rows", "seq")),
            P(("rows", "seq")),
            P(("rows", "seq"), None),
            P(("rows", "seq")),
            P(("rows", "seq"), None),
            P(("rows", "seq")),
        ),
        check_vma=False,
    )
```

profile of v0, /device:TPU:0, one launch (start us, length us, event | category | flops | bytes accessed | tf_op | source)
XLA Modules:
  0.0 314.4 jit_solution(8153169774493969343)
XLA Ops:
  6.3 2.9 collective-permute-done.1.beyond_ref
  9.8 10.9 %in_forward.1 = (bf16[2,512,512]{2,1,0:T(8,128)(2,1)}, bf16[3,2,288,1024]{3,2,1,0:T(8,128)(2,1)}, bf16[8,2,256,128]{3,2,1,0:T(8,128)(2,1)}) custom-call(s32[2,2]{1,0:T(2,128)} %cuts_ref.7, s32[1]{0:T(128)} %bitcast.first_ref, bf16[2,16,1024]{2,1,0:T(8,128)(2,1)} %copy-done.29, bf16[2,256,1024]{2,1,0:T(8,128)(2,1)} %x_ref.1, bf16[2,16,1024]{2,1,0:T(8,128)(2,1)} %copy-done.30, ...), custom_call_target="tpu_custom_call" | custom-call | flops 49999998976 | bytes 200000000 | tf_op jit(solution)/shard_map/in_forward/pallas_call | solution.py:993
  20.7 6.4 %all-to-all-start = ((bf16[8,2,256,128]{3,2,1,0:T(8,128)(2,1)}), bf16[8,2,256,128]{3,2,1,0:T(8,128)(2,1)S(1)}, u32[]{:S(2)}, u32[]{:S(2)}) async-start(bf16[8,2,256,128]{3,2,1,0:T(8,128)(2,1)} %get-tuple-element.103._), calls=%async_computation | async-start | bytes 2097152 | tf_op jit(solution)/shard_map/all_to_all | solution.py:1946
  27.4 9.1 %taps_and_spectrum.1 = (f32[8,512,128]{2,1,0:T(8,128)}, f32[2048,128]{1,0:T(8,128)}, f32[2048,128]{1,0:T(8,128)}) custom-call(s32[1]{0:T(128)} %bitcast.6.first_ref.refs_0_, f32[2048,33]{1,0:T(8,128)} %constant.169.clone.feats_ref.refs_3_, bf16[33,64]{1,0:T(8,128)(2,1)} %w1.4, bf16[64]{0:T(256)(128)(2,1)} %b1.3, bf16[64,64]{1,0:T(8,128)(2,1)} %refs_6_.1, ...), custom_call_target="tpu_custom_call" | custom-call | flops 1 | bytes 1 | tf_op jit(solution)/shard_map/taps_and_spectrum/pallas_call | solution.py:268
  36.5 6.0 %all-to-all-done.series_ref = bf16[8,2,256,128]{3,2,1,0:T(8,128)(2,1)S(1)} async-done(((bf16[8,2,256,128]{3,2,1,0:T(8,128)(2,1)}), bf16[8,2,256,128]{3,2,1,0:T(8,128)(2,1)S(1)}, u32[]{:S(2)}, u32[]{:S(2)}) %all-to-all-start) | async-done | bytes 1048608 | tf_op jit(solution)/shard_map/all_to_all | solution.py:1946
  43.4 9.3 %long_forward.1._ = bf16[8,2,256,128]{3,2,1,0:T(8,128)(2,1)} custom-call(s32[5,2,10]{2,1,0:T(2,128)} %copy-done.27, bf16[8,2,256,128]{3,2,1,0:T(8,128)(2,1)} %copy-done.12, f32[8,512,128]{2,1,0:T(8,128)} %get-tuple-element.104.taps_ref, bf16[128]{0:T(256)(128)(2,1)} %skip_ref.3, bf16[512,256]{1,0:T(8,128)(2,1)} %constant.166.clone.high_ref.ahead_ref, ...), custom_call_target="tpu_custom_call" | custom-call | flops 49999998976 | bytes 200000000 | tf_op jit(solution)/shard_map/long_forward/pallas_call | solution.py:387
  52.8 3.8 %all-to-all-start.1 = ((bf16[8,2,256,128]{3,2,1,0:T(8,128)(2,1)}), bf16[8,2,256,128]{3,2,1,0:T(8,128)(2,1)S(1)}, u32[]{:S(2)}, u32[]{:S(2)}) async-start(bf16[8,2,256,128]{3,2,1,0:T(8,128)(2,1)} %long_forward.1._), calls=%async_computation.1 | async-start | bytes 2097152 | tf_op jit(solution)/shard_map/all_to_all | solution.py:1946
  56.6 8.9 %matmul_turned.1.g_act_ref = bf16[512,4096]{1,0:T(8,128)(2,1)} custom-call(bf16[512,1024]{1,0:T(8,128)(2,1)} %bitcast.111, bf16[4096,1024]{1,0:T(8,128)(2,1)} %down_ref.1, bf16[8,2,256,128]{3,2,1,0:T(8,128)(2,1)} %long_forward.1._), custom_call_target="tpu_custom_call" | custom-call | flops 1 | bytes 1 | tf_op jit(solution)/shard_map/matmul_turned/pallas_call | solution.py:1562
  65.5 6.4 %all-to-all-done.1.long_ref.long_at = bf16[8,2,256,128]{3,2,1,0:T(8,128)(2,1)S(1)} async-done(((bf16[8,2,256,128]{3,2,1,0:T(8,128)(2,1)}), bf16[8,2,256,128]{3,2,1,0:T(8,128)(2,1)S(1)}, u32[]{:S(2)}, u32[]{:S(2)}) %all-to-all-start.1) | async-done | bytes 1048608 | tf_op jit(solution)/shard_map/all_to_all | solution.py:1946
  72.9 20.7 %middle_forward.1 = (bf16[2,512,512]{2,1,0:T(8,128)(2,1)}, f32[512,1024]{1,0:T(8,128)}, bf16[2,512,512]{2,1,0:T(8,128)(2,1)}, bf16[512,4096]{1,0:T(8,128)(2,1)},...) custom-call(s32[2,2]{1,0:T(2,128)} %cuts_ref.7, s32[1]{0:T(128)} %bitcast.first_ref, ...), custom_call_target="tpu_custom_call" | custom-call | flops 49999998976 | bytes 200000000 | tf_op jit(solution)/shard_map/middle_forward/pallas_call | solution.py:1121
  93.6 6.3 %gradient.7 = (bf16[2048,512]{1,0:T(8,128)(2,1)}, bf16[2048,512]{1,0:T(8,128)(2,1)}, s32[1]{0:T(128)}) custom-call(s32[1]{0:T(128)} %bitcast.26.order_ref, bf16[2,2048,512]{2,1,0:T(8,128)(2,1)} %get-tuple-element.109.refs_0_, bf16[512,1024]{1,0:T(8,128)(2,1)} %bitcast.112), custom_call_target="tpu_custom_call" | custom-call | flops 1 | bytes 1 | tf_op jit(solution)/shard_map/gradient/pallas_call | solution.py:1700
  101.2 6.9 %gradient.8 = (bf16[512,1024]{1,0:T(8,128)(2,1)}, bf16[512,1024]{1,0:T(8,128)(2,1)}, bf16[512,1024]{1,0:T(8,128)(2,1)}, bf16[512,1024]{1,0:T(8,128)(2,1)}, s32[1]{0:T(128)}) custom-call(s32[1]{0:T(128)} %bitcast.26.order_ref, bf16[2,512,512]{2,1,0:T(8,128)(2,1)} %get-tuple-element.112.refs_0_, ...), custom_call_target="tpu_custom_call" | custom-call | flops 1 | bytes 1 | tf_op jit(solution)/shard_map/gradient/pallas_call | solution.py:1700
  110.2 9.0 %gradient.9 = (bf16[1024,1024]{1,0:T(8,128)(2,1)}, bf16[1024,1024]{1,0:T(8,128)(2,1)}, s32[1]{0:T(128)}) custom-call(s32[17]{0:T(128)} %stack.107.order_ref, bf16[2,2048,512]{2,1,0:T(8,128)(2,1)} %get-tuple-element.109.refs_0_, bf16[512,1024]{1,0:T(8,128)(2,1)} %bitcast.113, bf16[2048,512]{1,0:T(8,128)(2,1)} %copy-done.6, ...), custom_call_target="tpu_custom_call" | custom-call | flops 1 | bytes 1 | tf_op jit(solution)/shard_map/gradient/pallas_call | solution.py:1700
  119.7 15.4 %middle_backward.1 = (bf16[8,2,256,128]{3,2,1,0:T(8,128)(2,1)}, f32[2,256,1024]{2,1,0:T(8,128)}, f32[512,1024]{1,0:T(8,128)}, bf16[512,1024]{1,0:T(8,128)(2,1)}, f32[8,1024]{1,0:T(8,128)}, /*index=5*/s32[1]{0:T(128)}) custom-call(s32[2,2]{1,0:T(2,128)} %cuts_ref.7, s32[1]{0:T(128)} %bitcast.first_ref, bf16[8,2,256,128]{3,2,1,0:T(8,128)(2,1)} %copy-done.13, ...), custom_call_target="tpu_custom_call" | custom-call | flops 49999998976 | bytes 200000000 | tf_op jit(solution)/shard_map/middle_backward/pallas_call | solution.py:1294
  135.1 3.1 %gradient.10 = (bf16[512,1024]{1,0:T(8,128)(2,1)}, s32[1]{0:T(128)}) custom-call(s32[1]{0:T(128)} %bitcast.26.order_ref, bf16[2,512,512]{2,1,0:T(8,128)(2,1)} %get-tuple-element.119.refs_0_.refs_1_, bf16[512,1024]{1,0:T(8,128)(2,1)} %get-tuple-element.120.refs_1_.refs_3_), custom_call_target="tpu_custom_call" | custom-call | flops 1 | bytes 1 | tf_op jit(solution)/shard_map/gradient/pallas_call | solution.py:1700
  138.5 4.4 %all-to-all-start.2 = ((bf16[8,2,256,128]{3,2,1,0:T(8,128)(2,1)}), bf16[8,2,256,128]{3,2,1,0:T(8,128)(2,1)}, u32[]{:S(2)}, u32[]{:S(2)}) async-start(bf16[8,2,256,128]{3,2,1,0:T(8,128)(2,1)} %get-tuple-element.118), calls=%async_computation.2 | async-start | bytes 2097152 | tf_op jit(solution)/shard_map/all_to_all | solution.py:1946
  144.0 10.6 %gradient.11 = (bf16[256,5120]{1,0:T(8,128)(2,1)}, bf16[256,5120]{1,0:T(8,128)(2,1)}, s32[1]{0:T(128)}) custom-call(s32[17]{0:T(128)} %stack.107.order_ref, bf16[2,512,512]{2,1,0:T(8,128)(2,1)} %get-tuple-element.112.refs_0_, bf16[2,512,512]{2,1,0:T(8,128)(2,1)} %get-tuple-element.119.refs_0_.refs_1_, ...), custom_call_target="tpu_custom_call" | custom-call | flops 1 | bytes 1 | tf_op jit(solution)/shard_map/gradient/pallas_call | solution.py:1700
  157.3 3.5 %add_convert_fusion.2 = (bf16[2,1,2,128,1024]{4,3,2,1,0:T(8,128)(2,1)S(1)}, bf16[2,2,128,1024]{3,2,1,0:T(8,128)(2,1)}) fusion(bf16[2,2,2,128,1024]{4,3,2,1,0:T(8,128)(2,1)} %bitcast.29, s32[]{:T(128)S(6)} %select_n.150, bf16[2,2,2,128,1024]{4,3,2,1,0:T(8,128)(2,1)S(1)} %bitcast.124, s32[]{:T(128)S(6)} %select_n.149), kind=kLoop, calls=%fused_computation.2 | loop fusion | flops 4194304 | bytes 6291464 | tf_op jit(solution)/shard_map/convert_element_type | solution.py:576
  162.5 15.0 %long_backward.1 = (bf16[8,2,272,128]{3,2,1,0:T(8,128)(2,1)}, f32[8,256,128]{2,1,0:T(8,128)}, f32[1,128]{1,0:T(1,128)}, s32[1]{0:T(128)}) custom-call(s32[5,2,10]{2,1,0:T(2,128)} %copy-done.27, bf16[8,2,256,128]{3,2,1,0:T(8,128)(2,1)} %all-to-all-done.2.grad_ref, bf16[8,2,256,128]{3,2,1,0:T(8,128)(2,1)} %copy-done.12, ...), custom_call_target="tpu_custom_call" | custom-call | flops 49999998976 | bytes 200000000 | tf_op jit(solution)/shard_map/long_backward/pallas_call | solution.py:434
  177.4 4.5 %all-to-all-start.3 = ((bf16[8,2,272,128]{3,2,1,0:T(8,128)(2,1)}), bf16[8,2,272,128]{3,2,1,0:T(8,128)(2,1)}, u32[]{:S(2)}, u32[]{:S(2)}) async-start(bf16[8,2,272,128]{3,2,1,0:T(8,128)(2,1)} %get-tuple-element.125.refs_0_), calls=%async_computation.3 | async-start | bytes 2228224 | tf_op jit(solution)/shard_map/all_to_all | solution.py:1946
  184.1 10.1 %down_forward.1 = (bf16[512,1024]{1,0:T(8,128)(2,1)}, s32[1]{0:T(128)}) custom-call(f32[512,1024]{1,0:T(8,128)} %get-tuple-element.106.resid_at.resid_ref, bf16[512,4096]{1,0:T(8,128)(2,1)} %get-tuple-element.107.act_ref, bf16[4096,1024]{1,0:T(8,128)(2,1)} %down_ref.1, bf16[1024]{0:T(1024)(128)(2,1)} %bias_ref.5, ...), custom_call_target="tpu_custom_call" | custom-call | flops 1 | bytes 1 | tf_op jit(solution)/shard_map/down_forward/pallas_call | solution.py:1601
  201.4 3.8 %collective-permute-start.14 = (bf16[4,32,5120]{2,1,0:T(8,128)(2,1)}, bf16[4,32,5120]{2,1,0:T(8,128)(2,1)S(1)}, u32[]{:S(2)}, u32[]{:S(2)}) collective-permute-start(bf16[4,32,5120]{2,1,0:T(8,128)(2,1)} %fusion.others_1_), channel_id=1, source_target_pairs={{0,4},{1,3},{2,6},{3,1},{4,0},{5,7},{6,2},{7,5},{8,12},{9,11},{10,... | collective-permute-start | bytes 3932168 | tf_op jit(solution)/shard_map/ppermute | solution.py:568
  205.8 16.7 %in_backward.1 = (bf16[3,512,1024]{2,1,0:T(8,128)(2,1)}, f32[3,8,1024]{2,1,0:T(8,128)}, f32[512,1024]{1,0:T(8,128)}, f32[8,1024]{1,0:T(8,128)}, s32[1]{0:T(128)}) custom-call(s32[2,2]{1,0:T(2,128)} %cuts_ref.7, s32[1]{0:T(128)} %bitcast.first_ref, bf16[8,2,272,128]{3,2,1,0:T(8,128)(2,1)} %all-to-all-done.3.g_carried_ref, ...), custom_call_target="tpu_custom_call" | custom-call | flops 49999998976 | bytes 200000000 | tf_op jit(solution)/shard_map/in_backward/pallas_call | solution.py:1486
  227.2 5.8 %gradient.12 = (bf16[512,1024]{1,0:T(8,128)(2,1)}, bf16[512,1024]{1,0:T(8,128)(2,1)}, bf16[512,1024]{1,0:T(8,128)(2,1)}, s32[1]{0:T(128)}) custom-call(s32[1]{0:T(128)} %bitcast.26.order_ref, bf16[2,512,512]{2,1,0:T(8,128)(2,1)} %get-tuple-element.140.refs_0_, bf16[3,512,1024]{2,1,0:T(8,128)(2,1)} %get-tuple-element.141.refs_1_, ...), custom_call_target="tpu_custom_call" | custom-call | flops 49999998976 | bytes 200000000 | tf_op jit(solution)/shard_map/gradient/pallas_call | solution.py:1700
  239.0 7.7 %gradient.13 = (bf16[256,3072]{1,0:T(8,128)(2,1)}, bf16[256,3072]{1,0:T(8,128)(2,1)}, s32[1]{0:T(128)}) custom-call(s32[17]{0:T(128)} %stack.107.order_ref, bf16[2,512,512]{2,1,0:T(8,128)(2,1)} %get-tuple-element.140.refs_0_, bf16[3,512,1024]{2,1,0:T(8,128)(2,1)} %get-tuple-element.141.refs_1_, bf16[512,1024]{1,0:T(8,128)(2,1)} %collective-permute-done.15.refs_2_, ...), custom_call_target="tpu_custom_call" | custom-call | flops 1 | bytes 1 | tf_op jit(solution)/shard_map/gradient/pallas_call | solution.py:1700
  249.0 5.6 %filter_backward.1 = (f32[192,128]{1,0:T(8,128)}, f32[192,128]{1,0:T(8,128)}, f32[192,128]{1,0:T(8,128)}, f32[192,128]{1,0:T(8,128)}) custom-call(s32[1]{0:T(128)} %bitcast.6.first_ref.refs_0_, s32[1]{0:T(128)} %bitcast.40.refs_1_, f32[2048,128]{1,0:T(8,128)} %bitcast.136, f32[2048,33]{1,0:T(8,128)} %constant.169.clone.feats_ref.refs_3_, ...), custom_call_target="tpu_custom_call" | custom-call | flops 49999998976 | bytes 200000000 | tf_op jit(solution)/shard_map/filter_backward/pallas_call | solution.py:141
  255.9 3.2 %collective-permute-start.19 = (f32[192,128]{1,0:T(8,128)}, f32[192,128]{1,0:T(8,128)S(1)}, u32[]{:S(2)}, u32[]{:S(2)}) collective-permute-start(f32[192,128]{1,0:T(8,128)} %get-tuple-element.149.refs_2_), channel_id=1, source_target_pairs={{0,16},{1,17},{2,18},{3,19},{4,20},{5,21},{6,22},{7,23},{8,24},{9,... | collective-permute-start | bytes 294920 | tf_op jit(solution)/shard_map/ppermute | solution.py:568
  264.1 2.9 collective-permute-done.19.refs_2_
  272.5 3.0 collective-permute-start.28
  281.1 3.2 %collective-permute-done.26 = bf16[4,32,3072]{2,1,0:T(8,128)(2,1)} collective-permute-done((bf16[4,32,3072]{2,1,0:T(8,128)(2,1)S(1)}, bf16[4,32,3072]{2,1,0:T(8,128)(2,1)}, u32[]{:S(2)}, u32[]{:S(2)}) %collective-permute-start.26) | collective-permute-done | bytes 786464 | tf_op jit(solution)/shard_map/ppermute | solution.py:568
  295.3 3.7 %collective-permute-done.29.arrived_ref = bf16[2,32,3072]{2,1,0:T(8,128)(2,1)S(1)} collective-permute-done((bf16[2,32,3072]{2,1,0:T(8,128)(2,1)S(1)}, bf16[2,32,3072]{2,1,0:T(8,128)(2,1)S(1)}, u32[]{:S(2)}, u32[]{:S(2)}) %collective-permute-start.29) | collective-permute-done | bytes 393248 | tf_op jit(solution)/shard_map/ppermute | solution.py:568
  307.4 3.4 %collective-permute-done.30.last_ref = bf16[32,3072]{1,0:T(8,128)(2,1)S(1)} collective-permute-done((bf16[32,3072]{1,0:T(8,128)(2,1)S(1)}, bf16[32,3072]{1,0:T(8,128)(2,1)S(1)}, u32[]{:S(2)}, u32[]{:S(2)}) %collective-permute-start.30) | collective-permute-done | bytes 196640 | tf_op jit(solution)/shard_map/ppermute | solution.py:568
  (153 shorter events, 76.0 us)
Async XLA Ops:
  1.5 4.7 %collective-permute-start = (bf16[2,16,1024]{2,1,0:T(8,128)(2,1)S(1)}, bf16[2,16,1024]{2,1,0:T(8,128)(2,1)S(1)}, u32[]{:S(2)}, u32[]{:S(2)}) collective-permute-start(bf16[2,16,1024]{2,1,0:T(8,128)(2,1)S(1)} %get-tuple-element.197), channel_id=1, source_target_pairs={{0,1},{1,2},{2,3},{3,4},{4,5},{5,6},{6,7},{8,9},{9,10},{10,11},{11... | collective-permute-start | bytes 196616 | tf_op jit(solution)/shard_map/ppermute | solution.py:30
  3.9 5.3 %collective-permute-start.1 = (bf16[2,16,1024]{2,1,0:T(8,128)(2,1)S(1)}, bf16[2,16,1024]{2,1,0:T(8,128)(2,1)S(1)}, u32[]{:S(2)}, u32[]{:S(2)}) collective-permute-start(bf16[2,16,1024]{2,1,0:T(8,128)(2,1)S(1)} %get-tuple-element.196), channel_id=1, source_target_pairs={{1,0},{2,1},{3,2},{4,3},{5,4},{6,5},{7,6},{9,8},{10,9},{11,10},{12... | collective-permute-start | bytes 196616 | tf_op jit(solution)/shard_map/ppermute | solution.py:30
  20.7 21.8 %all-to-all-start = ((bf16[8,2,256,128]{3,2,1,0:T(8,128)(2,1)}), bf16[8,2,256,128]{3,2,1,0:T(8,128)(2,1)S(1)}, u32[]{:S(2)}, u32[]{:S(2)}) async-start(bf16[8,2,256,128]{3,2,1,0:T(8,128)(2,1)} %get-tuple-element.103._), calls=%async_computation | async-start | bytes 2097152 | tf_op jit(solution)/shard_map/all_to_all | solution.py:1946
  52.8 19.1 %all-to-all-start.1 = ((bf16[8,2,256,128]{3,2,1,0:T(8,128)(2,1)}), bf16[8,2,256,128]{3,2,1,0:T(8,128)(2,1)S(1)}, u32[]{:S(2)}, u32[]{:S(2)}) async-start(bf16[8,2,256,128]{3,2,1,0:T(8,128)(2,1)} %long_forward.1._), calls=%async_computation.1 | async-start | bytes 2097152 | tf_op jit(solution)/shard_map/all_to_all | solution.py:1946
  100.0 8.8 %collective-permute-start.2 = (bf16[2048,512]{1,0:T(8,128)(2,1)}, bf16[2048,512]{1,0:T(8,128)(2,1)S(1)}, u32[]{:S(2)}, u32[]{:S(2)}) collective-permute-start(bf16[2048,512]{1,0:T(8,128)(2,1)} %get-tuple-element.110.refs_2_), channel_id=1, source_target_pairs={{0,1},{1,0},{2,3},{3,2},{4,5},{5,4},{6,7},{7,6},{8,9},{9,8},{10,11... | collective-permute-start | bytes 6291464 | tf_op jit(solution)/shard_map/ppermute | solution.py:568
  100.0 9.2 %collective-permute-start.3 = (bf16[2048,512]{1,0:T(8,128)(2,1)}, bf16[2048,512]{1,0:T(8,128)(2,1)}, u32[]{:S(2)}, u32[]{:S(2)}) collective-permute-start(bf16[2048,512]{1,0:T(8,128)(2,1)} %get-tuple-element.111.refs_3_), channel_id=1, source_target_pairs={{0,1},{1,0},{2,3},{3,2},{4,5},{5,4},{6,7},{7,6},{8,9},{9,8},{10,11... | collective-permute-start | bytes 6291464 | tf_op jit(solution)/shard_map/ppermute | solution.py:568
  108.1 30.1 %collective-permute-start.4 = (bf16[512,1024]{1,0:T(8,128)(2,1)}, bf16[512,1024]{1,0:T(8,128)(2,1)}, u32[]{:S(2)}, u32[]{:S(2)}) collective-permute-start(bf16[512,1024]{1,0:T(8,128)(2,1)} %get-tuple-element.113.refs_4_), channel_id=1, source_target_pairs={{0,1},{1,0},{2,3},{3,2},{4,5},{5,4},{6,7},{7,6},{8,9},{9,8},{10,11... | collective-permute-start | bytes 3145736 | tf_op jit(solution)/shard_map/ppermute | solution.py:568
  108.3 34.7 %collective-permute-start.5 = (bf16[512,1024]{1,0:T(8,128)(2,1)}, bf16[512,1024]{1,0:T(8,128)(2,1)}, u32[]{:S(2)}, u32[]{:S(2)}) collective-permute-start(bf16[512,1024]{1,0:T(8,128)(2,1)} %get-tuple-element.114.refs_5_), channel_id=1, source_target_pairs={{0,1},{1,0},{2,3},{3,2},{4,5},{5,4},{6,7},{7,6},{8,9},{9,8},{10,11... | collective-permute-start | bytes 3145736 | tf_op jit(solution)/shard_map/ppermute | solution.py:568
  108.7 34.2 %collective-permute-start.6 = (bf16[512,1024]{1,0:T(8,128)(2,1)}, bf16[512,1024]{1,0:T(8,128)(2,1)}, u32[]{:S(2)}, u32[]{:S(2)}) collective-permute-start(bf16[512,1024]{1,0:T(8,128)(2,1)} %get-tuple-element.115.refs_6_), channel_id=1, source_target_pairs={{0,1},{1,0},{2,3},{3,2},{4,5},{5,4},{6,7},{7,6},{8,9},{9,8},{10,11... | collective-permute-start | bytes 3145736 | tf_op jit(solution)/shard_map/ppermute | solution.py:568
  108.8 34.2 %collective-permute-start.7 = (bf16[512,1024]{1,0:T(8,128)(2,1)}, bf16[512,1024]{1,0:T(8,128)(2,1)}, u32[]{:S(2)}, u32[]{:S(2)}) collective-permute-start(bf16[512,1024]{1,0:T(8,128)(2,1)} %get-tuple-element.116.refs_7_), channel_id=1, source_target_pairs={{0,1},{1,0},{2,3},{3,2},{4,5},{5,4},{6,7},{7,6},{8,9},{9,8},{10,11... | collective-permute-start | bytes 3145736 | tf_op jit(solution)/shard_map/ppermute | solution.py:568
  119.2 38.1 %collective-permute-start.9 = (bf16[1024,1024]{1,0:T(8,128)(2,1)}, bf16[1024,1024]{1,0:T(8,128)(2,1)}, u32[]{:S(2)}, u32[]{:S(2)}) collective-permute-start(bf16[1024,1024]{1,0:T(8,128)(2,1)} %get-tuple-element.117._), channel_id=1, source_target_pairs={{0,2},{1,5},{2,0},{3,7},{4,6},{5,1},{6,4},{7,3},{8,10},{9,13},{10,... | collective-permute-start | bytes 6291464 | tf_op jit(solution)/shard_map/ppermute | solution.py:568
  138.3 4.7 %collective-permute-start.8 = (bf16[512,1024]{1,0:T(8,128)(2,1)}, bf16[512,1024]{1,0:T(8,128)(2,1)S(1)}, u32[]{:S(2)}, u32[]{:S(2)}) collective-permute-start(bf16[512,1024]{1,0:T(8,128)(2,1)} %get-tuple-element.121), channel_id=1, source_target_pairs={{0,1},{1,0},{2,3},{3,2},{4,5},{5,4},{6,7},{7,6},{8,9},{9,8},{10,11... | collective-permute-start | bytes 3145736 | tf_op jit(solution)/shard_map/ppermute | solution.py:568
  138.5 23.9 %all-to-all-start.2 = ((bf16[8,2,256,128]{3,2,1,0:T(8,128)(2,1)}), bf16[8,2,256,128]{3,2,1,0:T(8,128)(2,1)}, u32[]{:S(2)}, u32[]{:S(2)}) async-start(bf16[8,2,256,128]{3,2,1,0:T(8,128)(2,1)} %get-tuple-element.118), calls=%async_computation.2 | async-start | bytes 2097152 | tf_op jit(solution)/shard_map/all_to_all | solution.py:1946
  155.2 43.3 %collective-permute-start.12 = (bf16[256,5120]{1,0:T(8,128)(2,1)}, bf16[256,5120]{1,0:T(8,128)(2,1)}, u32[]{:S(2)}, u32[]{:S(2)}) collective-permute-start(bf16[256,5120]{1,0:T(8,128)(2,1)} %get-tuple-element.122.others_0_), channel_id=1, source_target_pairs={{0,2},{1,5},{2,0},{3,7},{4,6},{5,1},{6,4},{7,3},{8,10},{9,13},{10,... | collective-permute-start | bytes 7864328 | tf_op jit(solution)/shard_map/ppermute | solution.py:568
  160.8 34.1 %collective-permute-start.11 = (bf16[2,2,128,1024]{3,2,1,0:T(8,128)(2,1)}, bf16[2,2,128,1024]{3,2,1,0:T(8,128)(2,1)S(1)}, u32[]{:S(2)}, u32[]{:S(2)}) collective-permute-start(bf16[2,2,128,1024]{3,2,1,0:T(8,128)(2,1)} %get-tuple-element.193.others_1_), channel_id=1, source_target_pairs={{0,8},{1,9},{2,10},{3,11},{4,12},{5,13},{6,14},{7,15},{8,0},{9,1},... | collective-permute-start | bytes 3145736 | tf_op jit(solution)/shard_map/ppermute | solution.py:568
  177.4 27.7 %all-to-all-start.3 = ((bf16[8,2,272,128]{3,2,1,0:T(8,128)(2,1)}), bf16[8,2,272,128]{3,2,1,0:T(8,128)(2,1)}, u32[]{:S(2)}, u32[]{:S(2)}) async-start(bf16[8,2,272,128]{3,2,1,0:T(8,128)(2,1)} %get-tuple-element.125.refs_0_), calls=%async_computation.3 | async-start | bytes 2228224 | tf_op jit(solution)/shard_map/all_to_all | solution.py:1946
  182.8 22.3 %collective-permute-start.10 = (bf16[2,16,1024]{2,1,0:T(8,128)(2,1)S(1)}, bf16[2,16,1024]{2,1,0:T(8,128)(2,1)S(1)}, u32[]{:S(2)}, u32[]{:S(2)}) collective-permute-start(bf16[2,16,1024]{2,1,0:T(8,128)(2,1)S(1)} %slice.29), channel_id=1, source_target_pairs={{1,0},{2,1},{3,2},{4,3},{5,4},{6,5},{7,6},{9,8},{10,9},{11,10},{12... | collective-permute-start | bytes 196616 | tf_op jit(solution)/shard_map/ppermute | solution.py:30
  196.2 27.0 %collective-permute-start.13 = (bf16[2,128,1024]{2,1,0:T(8,128)(2,1)}, bf16[2,128,1024]{2,1,0:T(8,128)(2,1)S(1)}, u32[]{:S(2)}, u32[]{:S(2)}) collective-permute-start(bf16[2,128,1024]{2,1,0:T(8,128)(2,1)} %get-tuple-element.195.others_0_), channel_id=1, source_target_pairs={{0,16},{1,17},{2,18},{3,19},{4,20},{5,21},{6,22},{7,23},{8,24},{9,... | collective-permute-start | bytes 1572872 | tf_op jit(solution)/shard_map/ppermute | solution.py:568
  201.4 24.8 %collective-permute-start.14 = (bf16[4,32,5120]{2,1,0:T(8,128)(2,1)}, bf16[4,32,5120]{2,1,0:T(8,128)(2,1)S(1)}, u32[]{:S(2)}, u32[]{:S(2)}) collective-permute-start(bf16[4,32,5120]{2,1,0:T(8,128)(2,1)} %fusion.others_1_), channel_id=1, source_target_pairs={{0,4},{1,3},{2,6},{3,1},{4,0},{5,7},{6,2},{7,5},{8,12},{9,11},{10,... | collective-permute-start | bytes 3932168 | tf_op jit(solution)/shard_map/ppermute | solution.py:568
  233.1 4.4 %collective-permute-start.16 = (bf16[512,1024]{1,0:T(8,128)(2,1)}, bf16[512,1024]{1,0:T(8,128)(2,1)}, u32[]{:S(2)}, u32[]{:S(2)}) collective-permute-start(bf16[512,1024]{1,0:T(8,128)(2,1)} %get-tuple-element.144), channel_id=1, source_target_pairs={{0,1},{1,0},{2,3},{3,2},{4,5},{5,4},{6,7},{7,6},{8,9},{9,8},{10,11... | collective-permute-start | bytes 3145736 | tf_op jit(solution)/shard_map/ppermute | solution.py:568
  233.5 5.5 %collective-permute-start.17 = (bf16[512,1024]{1,0:T(8,128)(2,1)}, bf16[512,1024]{1,0:T(8,128)(2,1)}, u32[]{:S(2)}, u32[]{:S(2)}) collective-permute-start(bf16[512,1024]{1,0:T(8,128)(2,1)} %get-tuple-element.145), channel_id=1, source_target_pairs={{0,1},{1,0},{2,3},{3,2},{4,5},{5,4},{6,7},{7,6},{8,9},{9,8},{10,11... | collective-permute-start | bytes 3145736 | tf_op jit(solution)/shard_map/ppermute | solution.py:568
  233.7 28.4 %collective-permute-start.21 = (bf16[128,1024]{1,0:T(8,128)(2,1)S(1)}, bf16[128,1024]{1,0:T(8,128)(2,1)}, u32[]{:S(2)}, u32[]{:S(2)}) collective-permute-start(bf16[128,1024]{1,0:T(8,128)(2,1)S(1)} %copy-done.16), channel_id=1, source_target_pairs={{0,4},{1,3},{2,6},{3,1},{4,0},{5,7},{6,2},{7,5},{8,12},{9,11},{10,... | collective-permute-start | bytes 786440 | tf_op jit(solution)/shard_map/ppermute | solution.py:568
  235.8 23.3 %collective-permute-start.22 = (bf16[2,32,5120]{2,1,0:T(8,128)(2,1)}, bf16[2,32,5120]{2,1,0:T(8,128)(2,1)}, u32[]{:S(2)}, u32[]{:S(2)}) collective-permute-start(bf16[2,32,5120]{2,1,0:T(8,128)(2,1)} %fusion.5.refs_3_), channel_id=1, source_target_pairs={{0,8},{1,9},{2,10},{3,11},{4,12},{5,13},{6,14},{7,15},{8,0},{9,1},... | collective-permute-start | bytes 1966088 | tf_op jit(solution)/shard_map/ppermute | solution.py:568
  246.8 24.0 %collective-permute-start.24 = (bf16[256,3072]{1,0:T(8,128)(2,1)}, bf16[256,3072]{1,0:T(8,128)(2,1)}, u32[]{:S(2)}, u32[]{:S(2)}) collective-permute-start(bf16[256,3072]{1,0:T(8,128)(2,1)} %get-tuple-element.146.refs_13_), channel_id=1, source_target_pairs={{0,2},{1,5},{2,0},{3,7},{4,6},{5,1},{6,4},{7,3},{8,10},{9,13},{10,... | collective-permute-start | bytes 4718600 | tf_op jit(solution)/shard_map/ppermute | solution.py:568
  255.8 8.3 %collective-permute-start.18 = (f32[192,128]{1,0:T(8,128)}, f32[192,128]{1,0:T(8,128)S(1)}, u32[]{:S(2)}, u32[]{:S(2)}) collective-permute-start(f32[192,128]{1,0:T(8,128)} %get-tuple-element.148.refs_1_), channel_id=1, source_target_pairs={{0,8},{1,9},{2,10},{3,11},{4,12},{5,13},{6,14},{7,15},{8,0},{9,1},... | collective-permute-start | bytes 294920 | tf_op jit(solution)/shard_map/ppermute | solution.py:568
  255.9 11.2 %collective-permute-start.19 = (f32[192,128]{1,0:T(8,128)}, f32[192,128]{1,0:T(8,128)S(1)}, u32[]{:S(2)}, u32[]{:S(2)}) collective-permute-start(f32[192,128]{1,0:T(8,128)} %get-tuple-element.149.refs_2_), channel_id=1, source_target_pairs={{0,16},{1,17},{2,18},{3,19},{4,20},{5,21},{6,22},{7,23},{8,24},{9,... | collective-permute-start | bytes 294920 | tf_op jit(solution)/shard_map/ppermute | solution.py:568
  259.1 8.0 %collective-permute-start.20 = (f32[192,128]{1,0:T(8,128)}, f32[192,128]{1,0:T(8,128)S(1)}, u32[]{:S(2)}, u32[]{:S(2)}) collective-permute-start(f32[192,128]{1,0:T(8,128)} %get-tuple-element.150.refs_3_), channel_id=1, source_target_pairs={{0,24},{1,25},{2,26},{3,27},{4,28},{5,29},{6,30},{7,31},{8,16},{9,... | collective-permute-start | bytes 294920 | tf_op jit(solution)/shard_map/ppermute | solution.py:568
  272.1 12.2 %collective-permute-start.26 = (bf16[4,32,3072]{2,1,0:T(8,128)(2,1)S(1)}, bf16[4,32,3072]{2,1,0:T(8,128)(2,1)}, u32[]{:S(2)}, u32[]{:S(2)}) collective-permute-start(bf16[4,32,3072]{2,1,0:T(8,128)(2,1)S(1)} %fusion.4.refs_2_), channel_id=1, source_target_pairs={{0,4},{1,3},{2,6},{3,1},{4,0},{5,7},{6,2},{7,5},{8,12},{9,11},{10,... | collective-permute-start | bytes 2359304 | tf_op jit(solution)/shard_map/ppermute | solution.py:568
  272.5 18.3 %collective-permute-start.28 = (bf16[32,5120]{1,0:T(8,128)(2,1)S(1)}, bf16[32,5120]{1,0:T(8,128)(2,1)}, u32[]{:S(2)}, u32[]{:S(2)}) collective-permute-start(bf16[32,5120]{1,0:T(8,128)(2,1)S(1)} %copy-done.9), channel_id=1, source_target_pairs={{0,16},{1,17},{2,18},{3,19},{4,20},{5,21},{6,22},{7,23},{8,24},{9,... | collective-permute-start | bytes 983048 | tf_op jit(solution)/shard_map/ppermute | solution.py:568
  278.3 8.8 %collective-permute-start.25 = (f32[120,128]{1,0:T(8,128)}, f32[120,128]{1,0:T(8,128)S(1)}, u32[]{:S(2)}, u32[]{:S(2)}) collective-permute-start(f32[120,128]{1,0:T(8,128)} %get-tuple-element.156.refs_0_), channel_id=1, source_target_pairs={{0,2},{1,3},{2,0},{3,1},{4,6},{5,7},{6,4},{7,5},{8,10},{9,11},{10,... | collective-permute-start | bytes 184328 | tf_op jit(solution)/shard_map/ppermute | solution.py:568
  285.4 13.6 %collective-permute-start.29 = (bf16[2,32,3072]{2,1,0:T(8,128)(2,1)S(1)}, bf16[2,32,3072]{2,1,0:T(8,128)(2,1)S(1)}, u32[]{:S(2)}, u32[]{:S(2)}) collective-permute-start(bf16[2,32,3072]{2,1,0:T(8,128)(2,1)S(1)} %fusion.9.refs_2_), channel_id=1, source_target_pairs={{0,8},{1,9},{2,10},{3,11},{4,12},{5,13},{6,14},{7,15},{8,0},{9,1},... | collective-permute-start | bytes 1179656 | tf_op jit(solution)/shard_map/ppermute | solution.py:568
  299.0 11.8 %collective-permute-start.30 = (bf16[32,3072]{1,0:T(8,128)(2,1)S(1)}, bf16[32,3072]{1,0:T(8,128)(2,1)S(1)}, u32[]{:S(2)}, u32[]{:S(2)}) collective-permute-start(bf16[32,3072]{1,0:T(8,128)(2,1)S(1)} %fusion.13.refs_2_), channel_id=1, source_target_pairs={{0,16},{1,17},{2,18},{3,19},{4,20},{5,21},{6,22},{7,23},{8,24},{9,... | collective-permute-start | bytes 589832 | tf_op jit(solution)/shard_map/ppermute | solution.py:568
  (34 other events, 203.0 us)
where the time goes:
time: 319 us; the launch traced here: 314 us
  Pallas kernels  186 us (58%)
  starting transfers between devices  54.6 us (17%)
  waiting for transfers between devices  35.9 us (11%)
  other arithmetic  19.8 us (6%)
  local copies, waits for them, and re-layouts  12 us (4%)
  between operations  6.07 us (2%)
    pallas_call x7, Pallas kernels, gradient(): pl.pallas_call(kernel, grid_spec=pltpu.PrefetchScalarGridSpec(num_scalar_...  49.5 us
    ppermute x28, starting transfers between devices, swapped(): lax.ppermute(value, BOTH, [(one, one ^ mask_of(one)) for one in range(cou...  30.6 us
    pallas_call x1, Pallas kernels, middle_forward(): pl.pallas_call(middle_forward_kernel, grid=(steps,), in_specs=[smem(), sm...  20.7 us
    ppermute x28, waiting for transfers between devices, swapped(): lax.ppermute(value, BOTH, [(one, one ^ mask_of(one)) for one in range(cou...  20.6 us
    all_to_all x4, starting transfers between devices, exchanged(): return lax.all_to_all(array, 'seq', split_axis=0, concat_axis=0, tiled=True)  19.1 us
    convert_element_type x13, other arithmetic, added(): return (kept.astype(F32) + arrived.astype(F32)).astype(kind)  18.2 us
    pallas_call x1, Pallas kernels, in_backward(): pl.pallas_call(in_backward_kernel, grid=(steps,), in_specs=[smem(), smem(...  16.7 us
    pallas_call x1, Pallas kernels, middle_backward(): pl.pallas_call(middle_backward_kernel, grid=(steps,), in_specs=[smem(), s...  15.4 us
  transfers between devices with their start and end apart: 35, of which 13 were waited for; matrix products, arithmetic and copies ran while one was open for 6% of the time, Pallas kernels for 42%

commit v1 on v0

--- a/solution.py
+++ b/solution.py
@@ -1628,9 +1628,9 @@
     step = pl.program_id(0)
     token[0] = 0
 
-    def write(values, place):
+    def write(values, which):
         if not kept:
-            sent[place][...] = values.astype(BF16)
+            sent[0][...] = values.astype(BF16)
             return
         (send,), (keep,), (total_ref,) = sent, kept, total
         total_ref[...] = values
@@ -1639,23 +1639,22 @@
             piece = pl.ds(pl.multiple_of(order_ref[1 + spot] * share, share), share)
             into = (send, keep)[spot // 8]
             into[pl.ds(spot % 8 * share, share)] = (
-                total_ref[piece] + arrived[place][piece].astype(F32)
+                total_ref[piece] + arrived[which][piece].astype(F32)
             ).astype(BF16)
 
-    place = 0
-    for steps, first, second in zip(counts, firsts, seconds):
-        for _ in range(steps):
-
-            @pl.when(step == place)
-            def _(first=first, second=second, place=place):
-                write(dot32(first[0], second[...]), place)
-
-            place += 1
+    begin = 0
+    for which, (steps, first, second) in enumerate(zip(counts, firsts, seconds)):
+
+        @pl.when((step >= begin) & (step < begin + steps))
+        def _(first=first, second=second, which=which):
+            write(dot32(first[0], second[...]), which)
+
+        begin += steps
 
 
 def gradient(order, pairs, arrived, ready, columns, cost=LITTLE):
     height, tokens = pairs[0][0].shape[1:]
-    counts, first_specs, second_specs, begin = [], [], [], 0
+    counts, first_specs, second_specs, arrived_specs, begin = [], [], [], [], 0
     for first, second in pairs:
         parts = second.shape[-1] // columns
         steps = parts * (second.shape[0] if second.ndim == 3 else 1)
@@ -1665,21 +1664,22 @@
             at = jnp.clip(i - begin, 0, steps - 1)
             return (at // parts, 0, at % parts) if deep else (0, at)
 
+        def flat(i, o, begin=begin, steps=steps):
+            return 0, jnp.clip(i - begin, 0, steps - 1)
+
         shape = (None, tokens, columns) if second.ndim == 3 else (tokens, columns)
         second_specs.append(pl.BlockSpec(shape, place))
+        arrived_specs.append(pl.BlockSpec((height, columns), flat))
         counts.append(steps)
         begin += steps
-    single = pl.BlockSpec((height, columns), lambda i, o: (0, 0), pipeline_mode=pl.Buffered(1))
     anywhere = pl.BlockSpec(memory_space=pl.ANY)
     if arrived is None:
-        arrived = ()
-        sent = [jax.ShapeDtypeStruct((height, columns), BF16)] * begin
-        kept, scratch = [], []
-        out_specs = [single] * begin
+        arrived, arrived_specs = (), []
+        heights, scratch = [height], []
     else:
-        sent = [jax.ShapeDtypeStruct((height // 2, begin * columns), BF16)]
-        kept, scratch = sent, [pltpu.VMEM((height, columns), F32)]
-        out_specs = [pl.BlockSpec((height // 2, columns), lambda i, o: (0, i))] * 2
+        heights, scratch = [height // 2] * 2, [pltpu.VMEM((height, columns), F32)]
+    outputs = [jax.ShapeDtypeStruct((rows, begin * columns), BF16) for rows in heights]
+    out_specs = [pl.BlockSpec((rows, columns), lambda i, o: (0, i)) for rows in heights]
 
     def kernel(order_ref, *refs):
         refs = list(refs)
@@ -1690,26 +1690,22 @@
 
         firsts, seconds, arrived_refs = take(len(pairs)), take(len(pairs)), take(len(arrived))
         take(len(ready))
-        sent_refs, kept_refs, (token,) = take(len(sent)), take(len(kept)), take(1)
+        sent_refs, kept_refs, (token,) = take(1), take(len(heights) - 1), take(1)
         gradient_kernel(
             counts, order_ref, firsts, seconds, arrived_refs, sent_refs, kept_refs, token, refs
         )
 
     inputs = [p[0] for p in pairs] + [p[1] for p in pairs] + list(arrived) + list(ready)
-    outputs = sent + kept + [jax.ShapeDtypeStruct((1,), jnp.int32)]
     return pl.pallas_call(
         kernel,
         grid_spec=pltpu.PrefetchScalarGridSpec(
             num_scalar_prefetch=1,
             grid=(begin,),
-            in_specs=first_specs
-            + second_specs
-            + [single] * len(arrived)
-            + [anywhere] * len(ready),
+            in_specs=first_specs + second_specs + arrived_specs + [anywhere] * len(ready),
             out_specs=out_specs + [smem()],
             scratch_shapes=scratch,
         ),
-        out_shape=outputs,
+        out_shape=outputs + [jax.ShapeDtypeStruct((1,), jnp.int32)],
         compiler_params=params(),
         cost_estimate=cost,
         name="gradient",

time: 319 us -> 315 us (0.987)
    pallas_call x7, Pallas kernels: 49.5 us -> 46.3 us  [gradient(): pl.pallas_call(kernel, grid_spec=pltpu.PrefetchScalarGridSpec(num_scalar_...]
    ppermute x28 -> x22, starting transfers between devices: 30.6 us -> 28.7 us  [swapped(): lax.ppermute(value, BOTH, [(one, one ^ mask_of(one)) for one in range(cou...]
    unnamed x63 -> x61, local copies, waits for them, and re-layouts: 8.47 us -> 7.5 us
    ppermute x28 -> x22, waiting for transfers between devices: 20.6 us -> 21.1 us  [swapped(): lax.ppermute(value, BOTH, [(one, one ^ mask_of(one)) for one in range(cou...]
  transfers between devices with their start and end apart: 35 -> 29, of which waited for: 13 -> 11; matrix products, arithmetic and copies ran while one was open for 6% -> 6% of each run, Pallas kernels for 42% -> 42%
where the time goes in v1:
time: 315 us; the launch traced here: 309 us
  Pallas kernels  184 us (58%)
  starting transfers between devices  52.5 us (17%)
  waiting for transfers between devices  36.3 us (12%)
  other arithmetic  19.7 us (6%)
  local copies, waits for them, and re-layouts  11 us (3%)
  between operations  6.01 us (2%)
    pallas_call x7, Pallas kernels, gradient(): pl.pallas_call(kernel, grid_spec=pltpu.PrefetchScalarGridSpec(num_scalar_...  46.3 us
    ppermute x22, starting transfers between devices, swapped(): lax.ppermute(value, BOTH, [(one, one ^ mask_of(one)) for one in range(cou...  28.7 us
    ppermute x22, waiting for transfers between devices, swapped(): lax.ppermute(value, BOTH, [(one, one ^ mask_of(one)) for one in range(cou...  21.1 us
    pallas_call x1, Pallas kernels, middle_forward(): pl.pallas_call(middle_forward_kernel, grid=(steps,), in_specs=[smem(), sm...  20.7 us
    all_to_all x4, starting transfers between devices, exchanged(): return lax.all_to_all(array, 'seq', split_axis=0, concat_axis=0, tiled=True)  18.9 us
    convert_element_type x13, other arithmetic, added(): return (kept.astype(F32) + arrived.astype(F32)).astype(kind)  18.1 us
    pallas_call x1, Pallas kernels, in_backward(): pl.pallas_call(in_backward_kernel, grid=(steps,), in_specs=[smem(), smem(...  16.7 us
    pallas_call x1, Pallas kernels, middle_backward(): pl.pallas_call(middle_backward_kernel, grid=(steps,), in_specs=[smem(), s...  15.8 us
  transfers between devices with their start and end apart: 29, of which 11 were waited for; matrix products, arithmetic and copies ran while one was open for 6% of the time, Pallas kernels for 42%

profile of v1, /device:TPU:0, one launch (start us, length us, event | category | flops | bytes accessed | tf_op | source)
XLA Modules:
  0.0 309.3 jit_solution(10560160403058351142)
XLA Ops:
  6.3 2.9 collective-permute-done.1.beyond_ref
  9.8 10.9 %in_forward.1 = (bf16[2,512,512]{2,1,0:T(8,128)(2,1)}, bf16[3,2,288,1024]{3,2,1,0:T(8,128)(2,1)}, bf16[8,2,256,128]{3,2,1,0:T(8,128)(2,1)}) custom-call(s32[2,2]{1,0:T(2,128)} %cuts_ref.7, s32[1]{0:T(128)} %bitcast.first_ref, bf16[2,16,1024]{2,1,0:T(8,128)(2,1)} %copy-done.28, bf16[2,256,1024]{2,1,0:T(8,128)(2,1)} %x_ref.1, bf16[2,16,1024]{2,1,0:T(8,128)(2,1)} %copy-done.29, ...), custom_call_target="tpu_custom_call" | custom-call | flops 49999998976 | bytes 200000000 | tf_op jit(solution)/shard_map/in_forward/pallas_call | solution.py:993
  20.7 6.4 %all-to-all-start = ((bf16[8,2,256,128]{3,2,1,0:T(8,128)(2,1)}), bf16[8,2,256,128]{3,2,1,0:T(8,128)(2,1)S(1)}, u32[]{:S(2)}, u32[]{:S(2)}) async-start(bf16[8,2,256,128]{3,2,1,0:T(8,128)(2,1)} %get-tuple-element.97._), calls=%async_computation | async-start | bytes 2097152 | tf_op jit(solution)/shard_map/all_to_all | solution.py:1942
  27.5 9.1 %taps_and_spectrum.1 = (f32[8,512,128]{2,1,0:T(8,128)}, f32[2048,128]{1,0:T(8,128)}, f32[2048,128]{1,0:T(8,128)}) custom-call(s32[1]{0:T(128)} %bitcast.6.first_ref.refs_0_, f32[2048,33]{1,0:T(8,128)} %constant.169.clone.feats_ref.refs_3_, bf16[33,64]{1,0:T(8,128)(2,1)} %w1.4, bf16[64]{0:T(256)(128)(2,1)} %b1.3, bf16[64,64]{1,0:T(8,128)(2,1)} %refs_6_.1, ...), custom_call_target="tpu_custom_call" | custom-call | flops 1 | bytes 1 | tf_op jit(solution)/shard_map/taps_and_spectrum/pallas_call | solution.py:268
  36.5 6.0 %all-to-all-done.series_ref = bf16[8,2,256,128]{3,2,1,0:T(8,128)(2,1)S(1)} async-done(((bf16[8,2,256,128]{3,2,1,0:T(8,128)(2,1)}), bf16[8,2,256,128]{3,2,1,0:T(8,128)(2,1)S(1)}, u32[]{:S(2)}, u32[]{:S(2)}) %all-to-all-start) | async-done | bytes 1048608 | tf_op jit(solution)/shard_map/all_to_all | solution.py:1942
  43.5 9.4 %long_forward.1._ = bf16[8,2,256,128]{3,2,1,0:T(8,128)(2,1)} custom-call(s32[5,2,10]{2,1,0:T(2,128)} %copy-done.26, bf16[8,2,256,128]{3,2,1,0:T(8,128)(2,1)} %copy-done.11, f32[8,512,128]{2,1,0:T(8,128)} %get-tuple-element.98.taps_ref, bf16[128]{0:T(256)(128)(2,1)} %skip_ref.3, bf16[512,256]{1,0:T(8,128)(2,1)} %constant.166.clone.high_ref.ahead_ref, ...), custom_call_target="tpu_custom_call" | custom-call | flops 49999998976 | bytes 200000000 | tf_op jit(solution)/shard_map/long_forward/pallas_call | solution.py:387
  52.9 3.8 %all-to-all-start.1 = ((bf16[8,2,256,128]{3,2,1,0:T(8,128)(2,1)}), bf16[8,2,256,128]{3,2,1,0:T(8,128)(2,1)S(1)}, u32[]{:S(2)}, u32[]{:S(2)}) async-start(bf16[8,2,256,128]{3,2,1,0:T(8,128)(2,1)} %long_forward.1._), calls=%async_computation.1 | async-start | bytes 2097152 | tf_op jit(solution)/shard_map/all_to_all | solution.py:1942
  56.7 9.0 %matmul_turned.1.g_act_ref = bf16[512,4096]{1,0:T(8,128)(2,1)} custom-call(bf16[512,1024]{1,0:T(8,128)(2,1)} %bitcast.111, bf16[4096,1024]{1,0:T(8,128)(2,1)} %down_ref.1, bf16[8,2,256,128]{3,2,1,0:T(8,128)(2,1)} %long_forward.1._), custom_call_target="tpu_custom_call" | custom-call | flops 1 | bytes 1 | tf_op jit(solution)/shard_map/matmul_turned/pallas_call | solution.py:1562
  65.6 6.4 %all-to-all-done.1.long_ref.long_at = bf16[8,2,256,128]{3,2,1,0:T(8,128)(2,1)S(1)} async-done(((bf16[8,2,256,128]{3,2,1,0:T(8,128)(2,1)}), bf16[8,2,256,128]{3,2,1,0:T(8,128)(2,1)S(1)}, u32[]{:S(2)}, u32[]{:S(2)}) %all-to-all-start.1) | async-done | bytes 1048608 | tf_op jit(solution)/shard_map/all_to_all | solution.py:1942
  73.0 20.7 %middle_forward.1 = (bf16[2,512,512]{2,1,0:T(8,128)(2,1)}, f32[512,1024]{1,0:T(8,128)}, bf16[2,512,512]{2,1,0:T(8,128)(2,1)}, bf16[512,4096]{1,0:T(8,128)(2,1)},...) custom-call(s32[2,2]{1,0:T(2,128)} %cuts_ref.7, s32[1]{0:T(128)} %bitcast.first_ref, ...), custom_call_target="tpu_custom_call" | custom-call | flops 49999998976 | bytes 200000000 | tf_op jit(solution)/shard_map/middle_forward/pallas_call | solution.py:1121
  93.7 5.8 %gradient.7 = (bf16[2048,1024]{1,0:T(8,128)(2,1)}, s32[1]{0:T(128)}) custom-call(s32[1]{0:T(128)} %bitcast.26.order_ref, bf16[2,2048,512]{2,1,0:T(8,128)(2,1)} %get-tuple-element.103.refs_0_, bf16[512,1024]{1,0:T(8,128)(2,1)} %bitcast.112), custom_call_target="tpu_custom_call" | custom-call | flops 1 | bytes 1 | tf_op jit(solution)/shard_map/gradient/pallas_call | solution.py:1699
  100.2 6.3 %gradient.8 = (bf16[512,4096]{1,0:T(8,128)(2,1)}, s32[1]{0:T(128)}) custom-call(s32[1]{0:T(128)} %bitcast.26.order_ref, bf16[2,512,512]{2,1,0:T(8,128)(2,1)} %get-tuple-element.105.refs_0_, bf16[512,4096]{1,0:T(8,128)(2,1)} %get-tuple-element.102.refs_1_.g_pre_ref.refs_2_, bf16[2048,1024]{1,0:T(8,128)(2,1)} %get-tuple-element.104.refs_2_), custom_call_target="tpu_custom_call" | custom-call | flops 1 | bytes 1 | tf_op jit(solution)/shard_map/gradient/pallas_call | solution.py:1699
  107.0 7.9 %gradient.9 = (bf16[1024,1024]{1,0:T(8,128)(2,1)}, bf16[1024,1024]{1,0:T(8,128)(2,1)}, s32[1]{0:T(128)}) custom-call(s32[17]{0:T(128)} %stack.107.order_ref, bf16[2,2048,512]{2,1,0:T(8,128)(2,1)} %get-tuple-element.103.refs_0_, bf16[512,1024]{1,0:T(8,128)(2,1)} %bitcast.113, bf16[2048,1024]{1,0:T(8,128)(2,1)} %collective-permute-done.2.refs_2_, ...), custom_call_target="tpu_custom_call" | custom-call | flops 1 | bytes 1 | tf_op jit(solution)/shard_map/gradient/pallas_call | solution.py:1699
  115.4 15.8 %middle_backward.1 = (bf16[8,2,256,128]{3,2,1,0:T(8,128)(2,1)}, f32[2,256,1024]{2,1,0:T(8,128)}, f32[512,1024]{1,0:T(8,128)}, bf16[512,1024]{1,0:T(8,128)(2,1)}, f32[8,1024]{1,0:T(8,128)}, /*index=5*/s32[1]{0:T(128)}) custom-call(s32[2,2]{1,0:T(2,128)} %cuts_ref.7, s32[1]{0:T(128)} %bitcast.first_ref, bf16[8,2,256,128]{3,2,1,0:T(8,128)(2,1)} %copy-done.12, ...), custom_call_target="tpu_custom_call" | custom-call | flops 49999998976 | bytes 200000000 | tf_op jit(solution)/shard_map/middle_backward/pallas_call | solution.py:1294
  131.3 3.1 gradient.10
  134.4 4.4 %all-to-all-start.2 = ((bf16[8,2,256,128]{3,2,1,0:T(8,128)(2,1)}), bf16[8,2,256,128]{3,2,1,0:T(8,128)(2,1)}, u32[]{:S(2)}, u32[]{:S(2)}) async-start(bf16[8,2,256,128]{3,2,1,0:T(8,128)(2,1)} %get-tuple-element.108), calls=%async_computation.2 | async-start | bytes 2097152 | tf_op jit(solution)/shard_map/all_to_all | solution.py:1942
  139.9 10.2 %gradient.11 = (bf16[256,5120]{1,0:T(8,128)(2,1)}, bf16[256,5120]{1,0:T(8,128)(2,1)}, s32[1]{0:T(128)}) custom-call(s32[17]{0:T(128)} %stack.107.order_ref, bf16[2,512,512]{2,1,0:T(8,128)(2,1)} %get-tuple-element.105.refs_0_, bf16[2,512,512]{2,1,0:T(8,128)(2,1)} %get-tuple-element.109.refs_0_.refs_1_, ...), custom_call_target="tpu_custom_call" | custom-call | flops 1 | bytes 1 | tf_op jit(solution)/shard_map/gradient/pallas_call | solution.py:1699
  152.7 3.5 %add_convert_fusion.2 = (bf16[2,1,2,128,1024]{4,3,2,1,0:T(8,128)(2,1)S(1)}, bf16[2,2,128,1024]{3,2,1,0:T(8,128)(2,1)}) fusion(bf16[2,2,2,128,1024]{4,3,2,1,0:T(8,128)(2,1)} %bitcast.29, s32[]{:T(128)S(6)} %select_n.150, bf16[2,2,2,128,1024]{4,3,2,1,0:T(8,128)(2,1)S(1)} %bitcast.124, s32[]{:T(128)S(6)} %select_n.149), kind=kLoop, calls=%fused_computation.2 | loop fusion | flops 4194304 | bytes 6291464 | tf_op jit(solution)/shard_map/convert_element_type | solution.py:576
  158.0 15.1 %long_backward.1 = (bf16[8,2,272,128]{3,2,1,0:T(8,128)(2,1)}, f32[8,256,128]{2,1,0:T(8,128)}, f32[1,128]{1,0:T(1,128)}, s32[1]{0:T(128)}) custom-call(s32[5,2,10]{2,1,0:T(2,128)} %copy-done.26, bf16[8,2,256,128]{3,2,1,0:T(8,128)(2,1)} %all-to-all-done.2.grad_ref, bf16[8,2,256,128]{3,2,1,0:T(8,128)(2,1)} %copy-done.11, ...), custom_call_target="tpu_custom_call" | custom-call | flops 49999998976 | bytes 200000000 | tf_op jit(solution)/shard_map/long_backward/pallas_call | solution.py:434
  173.1 4.3 %all-to-all-start.3 = ((bf16[8,2,272,128]{3,2,1,0:T(8,128)(2,1)}), bf16[8,2,272,128]{3,2,1,0:T(8,128)(2,1)}, u32[]{:S(2)}, u32[]{:S(2)}) async-start(bf16[8,2,272,128]{3,2,1,0:T(8,128)(2,1)} %get-tuple-element.115.refs_0_), calls=%async_computation.3 | async-start | bytes 2228224 | tf_op jit(solution)/shard_map/all_to_all | solution.py:1942
  179.6 10.4 %down_forward.1 = (bf16[512,1024]{1,0:T(8,128)(2,1)}, s32[1]{0:T(128)}) custom-call(f32[512,1024]{1,0:T(8,128)} %get-tuple-element.100.resid_at.resid_ref, bf16[512,4096]{1,0:T(8,128)(2,1)} %get-tuple-element.101.act_ref, bf16[4096,1024]{1,0:T(8,128)(2,1)} %down_ref.1, bf16[1024]{0:T(1024)(128)(2,1)} %bias_ref.5, ...), custom_call_target="tpu_custom_call" | custom-call | flops 1 | bytes 1 | tf_op jit(solution)/shard_map/down_forward/pallas_call | solution.py:1601
  197.1 3.7 %collective-permute-start.10 = (bf16[4,32,5120]{2,1,0:T(8,128)(2,1)}, bf16[4,32,5120]{2,1,0:T(8,128)(2,1)S(1)}, u32[]{:S(2)}, u32[]{:S(2)}) collective-permute-start(bf16[4,32,5120]{2,1,0:T(8,128)(2,1)} %fusion.others_1_), channel_id=1, source_target_pairs={{0,4},{1,3},{2,6},{3,1},{4,0},{5,7},{6,2},{7,5},{8,12},{9,11},{10,... | collective-permute-start | bytes 3932168 | tf_op jit(solution)/shard_map/ppermute | solution.py:568
  201.5 16.7 %in_backward.1 = (bf16[3,512,1024]{2,1,0:T(8,128)(2,1)}, f32[3,8,1024]{2,1,0:T(8,128)}, f32[512,1024]{1,0:T(8,128)}, f32[8,1024]{1,0:T(8,128)}, s32[1]{0:T(128)}) custom-call(s32[2,2]{1,0:T(2,128)} %cuts_ref.7, s32[1]{0:T(128)} %bitcast.first_ref, bf16[8,2,272,128]{3,2,1,0:T(8,128)(2,1)} %all-to-all-done.3.g_carried_ref, ...), custom_call_target="tpu_custom_call" | custom-call | flops 49999998976 | bytes 200000000 | tf_op jit(solution)/shard_map/in_backward/pallas_call | solution.py:1486
  222.9 5.5 %gradient.12 = (bf16[512,3072]{1,0:T(8,128)(2,1)}, s32[1]{0:T(128)}) custom-call(s32[1]{0:T(128)} %bitcast.26.order_ref, bf16[2,512,512]{2,1,0:T(8,128)(2,1)} %get-tuple-element.130.refs_0_, bf16[3,512,1024]{2,1,0:T(8,128)(2,1)} %get-tuple-element.131.refs_1_, bf16[128,1024]{1,0:T(8,128)(2,1)} %fusion.12.refs_2_, bf16[2,32,5120]{2,1,0:T(8,128)(2,1)} %fusion.5.refs_3_), custom_call_target="tpu_custom_call" | custom-call | flops 49999998976 | bytes 200000000 | tf_op jit(solution)/shard_map/gradient/pallas_call | solution.py:1699
  230.8 3.7 %collective-permute-done.11.refs_2_ = bf16[512,3072]{1,0:T(8,128)(2,1)} collective-permute-done((bf16[512,3072]{1,0:T(8,128)(2,1)}, bf16[512,3072]{1,0:T(8,128)(2,1)}, u32[]{:S(2)}, u32[]{:S(2)}) %collective-permute-start.11) | collective-permute-done | bytes 3145760 | tf_op jit(solution)/shard_map/ppermute | solution.py:568
  234.4 7.6 %gradient.13 = (bf16[256,3072]{1,0:T(8,128)(2,1)}, bf16[256,3072]{1,0:T(8,128)(2,1)}, s32[1]{0:T(128)}) custom-call(s32[17]{0:T(128)} %stack.107.order_ref, bf16[2,512,512]{2,1,0:T(8,128)(2,1)} %get-tuple-element.130.refs_0_, bf16[3,512,1024]{2,1,0:T(8,128)(2,1)} %get-tuple-element.131.refs_1_, bf16[512,3072]{1,0:T(8,128)(2,1)} %collective-permute-done.11.refs_2_), custom_call_target="tpu_custom_call" | custom-call | flops 1 | bytes 1 | tf_op jit(solution)/shard_map/gradient/pallas_call | solution.py:1699
  244.2 5.6 %filter_backward.1 = (f32[192,128]{1,0:T(8,128)}, f32[192,128]{1,0:T(8,128)}, f32[192,128]{1,0:T(8,128)}, f32[192,128]{1,0:T(8,128)}) custom-call(s32[1]{0:T(128)} %bitcast.6.first_ref.refs_0_, s32[1]{0:T(128)} %bitcast.40.refs_1_, f32[2048,128]{1,0:T(8,128)} %bitcast.136, f32[2048,33]{1,0:T(8,128)} %constant.169.clone.feats_ref.refs_3_, ...), custom_call_target="tpu_custom_call" | custom-call | flops 49999998976 | bytes 200000000 | tf_op jit(solution)/shard_map/filter_backward/pallas_call | solution.py:141
  251.1 3.0 collective-permute-start.13
  267.5 2.9 collective-permute-start.22
  276.1 3.2 %collective-permute-done.20 = bf16[4,32,3072]{2,1,0:T(8,128)(2,1)} collective-permute-done((bf16[4,32,3072]{2,1,0:T(8,128)(2,1)S(1)}, bf16[4,32,3072]{2,1,0:T(8,128)(2,1)}, u32[]{:S(2)}, u32[]{:S(2)}) %collective-permute-start.20) | collective-permute-done | bytes 786464 | tf_op jit(solution)/shard_map/ppermute | solution.py:568
  290.3 3.7 %collective-permute-done.23.arrived_ref = bf16[2,32,3072]{2,1,0:T(8,128)(2,1)S(1)} collective-permute-done((bf16[2,32,3072]{2,1,0:T(8,128)(2,1)S(1)}, bf16[2,32,3072]{2,1,0:T(8,128)(2,1)S(1)}, u32[]{:S(2)}, u32[]{:S(2)}) %collective-permute-start.23) | collective-permute-done | bytes 393248 | tf_op jit(solution)/shard_map/ppermute | solution.py:568
  302.4 3.4 %collective-permute-done.24.last_ref = bf16[32,3072]{1,0:T(8,128)(2,1)S(1)} collective-permute-done((bf16[32,3072]{1,0:T(8,128)(2,1)S(1)}, bf16[32,3072]{1,0:T(8,128)(2,1)S(1)}, u32[]{:S(2)}, u32[]{:S(2)}) %collective-permute-start.24) | collective-permute-done | bytes 196640 | tf_op jit(solution)/shard_map/ppermute | solution.py:568
  (139 shorter events, 73.0 us)
Async XLA Ops:
  1.5 4.7 %collective-permute-start = (bf16[2,16,1024]{2,1,0:T(8,128)(2,1)S(1)}, bf16[2,16,1024]{2,1,0:T(8,128)(2,1)S(1)}, u32[]{:S(2)}, u32[]{:S(2)}) collective-permute-start(bf16[2,16,1024]{2,1,0:T(8,128)(2,1)S(1)} %get-tuple-element.185), channel_id=1, source_target_pairs={{0,1},{1,2},{2,3},{3,4},{4,5},{5,6},{6,7},{8,9},{9,10},{10,11},{11... | collective-permute-start | bytes 196616 | tf_op jit(solution)/shard_map/ppermute | solution.py:30
  3.9 5.3 %collective-permute-start.1 = (bf16[2,16,1024]{2,1,0:T(8,128)(2,1)S(1)}, bf16[2,16,1024]{2,1,0:T(8,128)(2,1)S(1)}, u32[]{:S(2)}, u32[]{:S(2)}) collective-permute-start(bf16[2,16,1024]{2,1,0:T(8,128)(2,1)S(1)} %get-tuple-element.184), channel_id=1, source_target_pairs={{1,0},{2,1},{3,2},{4,3},{5,4},{6,5},{7,6},{9,8},{10,9},{11,10},{12... | collective-permute-start | bytes 196616 | tf_op jit(solution)/shard_map/ppermute | solution.py:30
  20.7 21.8 %all-to-all-start = ((bf16[8,2,256,128]{3,2,1,0:T(8,128)(2,1)}), bf16[8,2,256,128]{3,2,1,0:T(8,128)(2,1)S(1)}, u32[]{:S(2)}, u32[]{:S(2)}) async-start(bf16[8,2,256,128]{3,2,1,0:T(8,128)(2,1)} %get-tuple-element.97._), calls=%async_computation | async-start | bytes 2097152 | tf_op jit(solution)/shard_map/all_to_all | solution.py:1942
  52.9 19.1 %all-to-all-start.1 = ((bf16[8,2,256,128]{3,2,1,0:T(8,128)(2,1)}), bf16[8,2,256,128]{3,2,1,0:T(8,128)(2,1)S(1)}, u32[]{:S(2)}, u32[]{:S(2)}) async-start(bf16[8,2,256,128]{3,2,1,0:T(8,128)(2,1)} %long_forward.1._), calls=%async_computation.1 | async-start | bytes 2097152 | tf_op jit(solution)/shard_map/all_to_all | solution.py:1942
  99.5 7.5 %collective-permute-start.2 = (bf16[2048,1024]{1,0:T(8,128)(2,1)}, bf16[2048,1024]{1,0:T(8,128)(2,1)}, u32[]{:S(2)}, u32[]{:S(2)}) collective-permute-start(bf16[2048,1024]{1,0:T(8,128)(2,1)} %get-tuple-element.104.refs_2_), channel_id=1, source_target_pairs={{0,1},{1,0},{2,3},{3,2},{4,5},{5,4},{6,7},{7,6},{8,9},{9,8},{10,11... | collective-permute-start | bytes 12582920 | tf_op jit(solution)/shard_map/ppermute | solution.py:568
  106.4 32.4 %collective-permute-start.3 = (bf16[512,4096]{1,0:T(8,128)(2,1)}, bf16[512,4096]{1,0:T(8,128)(2,1)}, u32[]{:S(2)}, u32[]{:S(2)}) collective-permute-start(bf16[512,4096]{1,0:T(8,128)(2,1)} %get-tuple-element.106.refs_3_), channel_id=1, source_target_pairs={{0,1},{1,0},{2,3},{3,2},{4,5},{5,4},{6,7},{7,6},{8,9},{9,8},{10,11... | collective-permute-start | bytes 12582920 | tf_op jit(solution)/shard_map/ppermute | solution.py:568
  114.9 37.8 %collective-permute-start.5 = (bf16[1024,1024]{1,0:T(8,128)(2,1)}, bf16[1024,1024]{1,0:T(8,128)(2,1)}, u32[]{:S(2)}, u32[]{:S(2)}) collective-permute-start(bf16[1024,1024]{1,0:T(8,128)(2,1)} %get-tuple-element.107._), channel_id=1, source_target_pairs={{0,2},{1,5},{2,0},{3,7},{4,6},{5,1},{6,4},{7,3},{8,10},{9,13},{10,... | collective-permute-start | bytes 6291464 | tf_op jit(solution)/shard_map/ppermute | solution.py:568
  134.3 4.5 %collective-permute-start.4 = (bf16[512,1024]{1,0:T(8,128)(2,1)}, bf16[512,1024]{1,0:T(8,128)(2,1)S(1)}, u32[]{:S(2)}, u32[]{:S(2)}) collective-permute-start(bf16[512,1024]{1,0:T(8,128)(2,1)} %get-tuple-element.111), channel_id=1, source_target_pairs={{0,1},{1,0},{2,3},{3,2},{4,5},{5,4},{6,7},{7,6},{8,9},{9,8},{10,11... | collective-permute-start | bytes 3145736 | tf_op jit(solution)/shard_map/ppermute | solution.py:568
  134.4 23.6 %all-to-all-start.2 = ((bf16[8,2,256,128]{3,2,1,0:T(8,128)(2,1)}), bf16[8,2,256,128]{3,2,1,0:T(8,128)(2,1)}, u32[]{:S(2)}, u32[]{:S(2)}) async-start(bf16[8,2,256,128]{3,2,1,0:T(8,128)(2,1)} %get-tuple-element.108), calls=%async_computation.2 | async-start | bytes 2097152 | tf_op jit(solution)/shard_map/all_to_all | solution.py:1942
  150.7 43.7 %collective-permute-start.8 = (bf16[256,5120]{1,0:T(8,128)(2,1)}, bf16[256,5120]{1,0:T(8,128)(2,1)}, u32[]{:S(2)}, u32[]{:S(2)}) collective-permute-start(bf16[256,5120]{1,0:T(8,128)(2,1)} %get-tuple-element.112.others_0_), channel_id=1, source_target_pairs={{0,2},{1,5},{2,0},{3,7},{4,6},{5,1},{6,4},{7,3},{8,10},{9,13},{10,... | collective-permute-start | bytes 7864328 | tf_op jit(solution)/shard_map/ppermute | solution.py:568
  156.2 34.4 %collective-permute-start.7 = (bf16[2,2,128,1024]{3,2,1,0:T(8,128)(2,1)}, bf16[2,2,128,1024]{3,2,1,0:T(8,128)(2,1)S(1)}, u32[]{:S(2)}, u32[]{:S(2)}) collective-permute-start(bf16[2,2,128,1024]{3,2,1,0:T(8,128)(2,1)} %get-tuple-element.181.others_1_), channel_id=1, source_target_pairs={{0,8},{1,9},{2,10},{3,11},{4,12},{5,13},{6,14},{7,15},{8,0},{9,1},... | collective-permute-start | bytes 3145736 | tf_op jit(solution)/shard_map/ppermute | solution.py:568
  173.1 27.7 %all-to-all-start.3 = ((bf16[8,2,272,128]{3,2,1,0:T(8,128)(2,1)}), bf16[8,2,272,128]{3,2,1,0:T(8,128)(2,1)}, u32[]{:S(2)}, u32[]{:S(2)}) async-start(bf16[8,2,272,128]{3,2,1,0:T(8,128)(2,1)} %get-tuple-element.115.refs_0_), calls=%async_computation.3 | async-start | bytes 2228224 | tf_op jit(solution)/shard_map/all_to_all | solution.py:1942
  178.4 22.5 %collective-permute-start.6 = (bf16[2,16,1024]{2,1,0:T(8,128)(2,1)S(1)}, bf16[2,16,1024]{2,1,0:T(8,128)(2,1)S(1)}, u32[]{:S(2)}, u32[]{:S(2)}) collective-permute-start(bf16[2,16,1024]{2,1,0:T(8,128)(2,1)S(1)} %slice.29), channel_id=1, source_target_pairs={{1,0},{2,1},{3,2},{4,3},{5,4},{6,5},{7,6},{9,8},{10,9},{11,10},{12... | collective-permute-start | bytes 196616 | tf_op jit(solution)/shard_map/ppermute | solution.py:30
  191.9 27.1 %copy-start.1 = (bf16[1,2,128,1024]{3,2,1,0:T(8,128)(2,1)}, bf16[1,2,128,1024]{3,2,1,0:T(8,128)(2,1)S(1)}, u32[]{:S(2)}) copy-start(bf16[1,2,128,1024]{3,2,1,0:T(8,128)(2,1)S(1)} %get-tuple-element.182) | copy-start | bytes 1572868
  191.9 27.1 %collective-permute-start.9 = (bf16[2,128,1024]{2,1,0:T(8,128)(2,1)}, bf16[2,128,1024]{2,1,0:T(8,128)(2,1)S(1)}, u32[]{:S(2)}, u32[]{:S(2)}) collective-permute-start(bf16[2,128,1024]{2,1,0:T(8,128)(2,1)} %get-tuple-element.183.others_0_), channel_id=1, source_target_pairs={{0,16},{1,17},{2,18},{3,19},{4,20},{5,21},{6,22},{7,23},{8,24},{9,... | collective-permute-start | bytes 1572872 | tf_op jit(solution)/shard_map/ppermute | solution.py:568
  197.1 24.8 %collective-permute-start.10 = (bf16[4,32,5120]{2,1,0:T(8,128)(2,1)}, bf16[4,32,5120]{2,1,0:T(8,128)(2,1)S(1)}, u32[]{:S(2)}, u32[]{:S(2)}) collective-permute-start(bf16[4,32,5120]{2,1,0:T(8,128)(2,1)} %fusion.others_1_), channel_id=1, source_target_pairs={{0,4},{1,3},{2,6},{3,1},{4,0},{5,7},{6,2},{7,5},{8,12},{9,11},{10,... | collective-permute-start | bytes 3932168 | tf_op jit(solution)/shard_map/ppermute | solution.py:568
  228.4 6.0 %collective-permute-start.11 = (bf16[512,3072]{1,0:T(8,128)(2,1)}, bf16[512,3072]{1,0:T(8,128)(2,1)}, u32[]{:S(2)}, u32[]{:S(2)}) collective-permute-start(bf16[512,3072]{1,0:T(8,128)(2,1)} %get-tuple-element.133), channel_id=1, source_target_pairs={{0,1},{1,0},{2,3},{3,2},{4,5},{5,4},{6,7},{7,6},{8,9},{9,8},{10,11... | collective-permute-start | bytes 9437192 | tf_op jit(solution)/shard_map/ppermute | solution.py:568
  228.6 28.7 %collective-permute-start.15 = (bf16[128,1024]{1,0:T(8,128)(2,1)S(1)}, bf16[128,1024]{1,0:T(8,128)(2,1)}, u32[]{:S(2)}, u32[]{:S(2)}) collective-permute-start(bf16[128,1024]{1,0:T(8,128)(2,1)S(1)} %copy-done.15), channel_id=1, source_target_pairs={{0,4},{1,3},{2,6},{3,1},{4,0},{5,7},{6,2},{7,5},{8,12},{9,11},{10,... | collective-permute-start | bytes 786440 | tf_op jit(solution)/shard_map/ppermute | solution.py:568
  230.6 23.5 %collective-permute-start.16 = (bf16[2,32,5120]{2,1,0:T(8,128)(2,1)}, bf16[2,32,5120]{2,1,0:T(8,128)(2,1)}, u32[]{:S(2)}, u32[]{:S(2)}) collective-permute-start(bf16[2,32,5120]{2,1,0:T(8,128)(2,1)} %fusion.5.refs_3_), channel_id=1, source_target_pairs={{0,8},{1,9},{2,10},{3,11},{4,12},{5,13},{6,14},{7,15},{8,0},{9,1},... | collective-permute-start | bytes 1966088 | tf_op jit(solution)/shard_map/ppermute | solution.py:568
  230.8 24.7 %copy-start = (bf16[2,1,32,5120]{3,2,1,0:T(8,128)(2,1)}, bf16[2,1,32,5120]{3,2,1,0:T(8,128)(2,1)S(1)}, u32[]{:S(2)}) copy-start(bf16[2,1,32,5120]{3,2,1,0:T(8,128)(2,1)S(1)} %add_convert_fusion.6) | copy-start | bytes 1966084
  242.0 23.7 %collective-permute-start.18 = (bf16[256,3072]{1,0:T(8,128)(2,1)}, bf16[256,3072]{1,0:T(8,128)(2,1)}, u32[]{:S(2)}, u32[]{:S(2)}) collective-permute-start(bf16[256,3072]{1,0:T(8,128)(2,1)} %get-tuple-element.134.refs_13_), channel_id=1, source_target_pairs={{0,2},{1,5},{2,0},{3,7},{4,6},{5,1},{6,4},{7,3},{8,10},{9,13},{10,... | collective-permute-start | bytes 4718600 | tf_op jit(solution)/shard_map/ppermute | solution.py:568
  249.8 15.9 %copy-start.6 = (bf16[256,3072]{1,0:T(8,128)(2,1)S(1)}, bf16[256,3072]{1,0:T(8,128)(2,1)}, u32[]{:S(2)}) copy-start(bf16[256,3072]{1,0:T(8,128)(2,1)} %get-tuple-element.142) | copy-start | bytes 4718596
  251.0 8.3 %collective-permute-start.12 = (f32[192,128]{1,0:T(8,128)}, f32[192,128]{1,0:T(8,128)S(1)}, u32[]{:S(2)}, u32[]{:S(2)}) collective-permute-start(f32[192,128]{1,0:T(8,128)} %get-tuple-element.136.refs_1_), channel_id=1, source_target_pairs={{0,8},{1,9},{2,10},{3,11},{4,12},{5,13},{6,14},{7,15},{8,0},{9,1},... | collective-permute-start | bytes 294920 | tf_op jit(solution)/shard_map/ppermute | solution.py:568
  251.1 11.0 %collective-permute-start.13 = (f32[192,128]{1,0:T(8,128)}, f32[192,128]{1,0:T(8,128)S(1)}, u32[]{:S(2)}, u32[]{:S(2)}) collective-permute-start(f32[192,128]{1,0:T(8,128)} %get-tuple-element.137.refs_2_), channel_id=1, source_target_pairs={{0,16},{1,17},{2,18},{3,19},{4,20},{5,21},{6,22},{7,23},{8,24},{9,... | collective-permute-start | bytes 294920 | tf_op jit(solution)/shard_map/ppermute | solution.py:568
  254.1 8.0 %collective-permute-start.14 = (f32[192,128]{1,0:T(8,128)}, f32[192,128]{1,0:T(8,128)S(1)}, u32[]{:S(2)}, u32[]{:S(2)}) collective-permute-start(f32[192,128]{1,0:T(8,128)} %get-tuple-element.138.refs_3_), channel_id=1, source_target_pairs={{0,24},{1,25},{2,26},{3,27},{4,28},{5,29},{6,30},{7,31},{8,16},{9,... | collective-permute-start | bytes 294920 | tf_op jit(solution)/shard_map/ppermute | solution.py:568
  267.1 12.2 %collective-permute-start.20 = (bf16[4,32,3072]{2,1,0:T(8,128)(2,1)S(1)}, bf16[4,32,3072]{2,1,0:T(8,128)(2,1)}, u32[]{:S(2)}, u32[]{:S(2)}) collective-permute-start(bf16[4,32,3072]{2,1,0:T(8,128)(2,1)S(1)} %fusion.4.refs_2_), channel_id=1, source_target_pairs={{0,4},{1,3},{2,6},{3,1},{4,0},{5,7},{6,2},{7,5},{8,12},{9,11},{10,... | collective-permute-start | bytes 2359304 | tf_op jit(solution)/shard_map/ppermute | solution.py:568
  267.5 3.0 collective-permute-start.17
  267.5 18.3 %collective-permute-start.22 = (bf16[32,5120]{1,0:T(8,128)(2,1)S(1)}, bf16[32,5120]{1,0:T(8,128)(2,1)}, u32[]{:S(2)}, u32[]{:S(2)}) collective-permute-start(bf16[32,5120]{1,0:T(8,128)(2,1)S(1)} %copy-done.8), channel_id=1, source_target_pairs={{0,16},{1,17},{2,18},{3,19},{4,20},{5,21},{6,22},{7,23},{8,24},{9,... | collective-permute-start | bytes 983048 | tf_op jit(solution)/shard_map/ppermute | solution.py:568
  273.3 8.8 %collective-permute-start.19 = (f32[120,128]{1,0:T(8,128)}, f32[120,128]{1,0:T(8,128)S(1)}, u32[]{:S(2)}, u32[]{:S(2)}) collective-permute-start(f32[120,128]{1,0:T(8,128)} %get-tuple-element.144.refs_0_), channel_id=1, source_target_pairs={{0,2},{1,3},{2,0},{3,1},{4,6},{5,7},{6,4},{7,5},{8,10},{9,11},{10,... | collective-permute-start | bytes 184328 | tf_op jit(solution)/shard_map/ppermute | solution.py:568
  280.4 13.6 %collective-permute-start.23 = (bf16[2,32,3072]{2,1,0:T(8,128)(2,1)S(1)}, bf16[2,32,3072]{2,1,0:T(8,128)(2,1)S(1)}, u32[]{:S(2)}, u32[]{:S(2)}) collective-permute-start(bf16[2,32,3072]{2,1,0:T(8,128)(2,1)S(1)} %fusion.9.refs_2_), channel_id=1, source_target_pairs={{0,8},{1,9},{2,10},{3,11},{4,12},{5,13},{6,14},{7,15},{8,0},{9,1},... | collective-permute-start | bytes 1179656 | tf_op jit(solution)/shard_map/ppermute | solution.py:568
  294.1 11.8 %collective-permute-start.24 = (bf16[32,3072]{1,0:T(8,128)(2,1)S(1)}, bf16[32,3072]{1,0:T(8,128)(2,1)S(1)}, u32[]{:S(2)}, u32[]{:S(2)}) collective-permute-start(bf16[32,3072]{1,0:T(8,128)(2,1)S(1)} %fusion.13.refs_2_), channel_id=1, source_target_pairs={{0,16},{1,17},{2,18},{3,19},{4,20},{5,21},{6,22},{7,23},{8,24},{9,... | collective-permute-start | bytes 589832 | tf_op jit(solution)/shard_map/ppermute | solution.py:568
  294.6 4.2 %collective-permute-start.21 = (f32[120,128]{1,0:T(8,128)S(1)}, f32[120,128]{1,0:T(8,128)S(1)}, u32[]{:S(2)}, u32[]{:S(2)}) collective-permute-start(f32[120,128]{1,0:T(8,128)S(1)} %copy-done.20), channel_id=1, source_target_pairs={{0,4},{1,5},{2,6},{3,7},{4,0},{5,1},{6,2},{7,3},{8,12},{9,13},{10,... | collective-permute-start | bytes 184328 | tf_op jit(solution)/shard_map/ppermute | solution.py:568
  (27 other events, 122.1 us)

commit v2 on v1

--- a/solution.py
+++ b/solution.py
@@ -1577,7 +1577,7 @@
 
 def down_forward(resid, act, down, bias, ready):
     tokens, width = resid.shape
-    depth = 1024
+    depth = 2048
     steps = act.shape[1] // depth
 
     def kernel(resid_ref, act_ref, down_ref, bias_ref, *refs):
@@ -2001,7 +2001,7 @@
     down_pairs = [(act_halves, grad)]
     *down_sent, _ = gradient(send_order, down_pairs, None, (), 512)
     down_arrived = to_sibling(down_sent)
-    *up_sent, _ = gradient(send_order, [(norm2_halves, g_pre)], None, down_sent, 1024)
+    *up_sent, _ = gradient(send_order, [(norm2_halves, g_pre)], None, down_sent, 2048)
     up_arrived = to_sibling(up_sent)
     down_send, down_keep, _ = gradient(first_order, down_pairs, down_arrived, up_sent, 512)
     down_arrived = swap_first(down_send)

time: 315 us -> 314 us (level)
  transfers between devices with their start and end apart: 29 -> 29, of which waited for: 11 -> 11; matrix products, arithmetic and copies ran while one was open for 6% -> 6% of each run, Pallas kernels for 42% -> 41%
where the time goes in v2:
time: 314 us; the launch traced here: 309 us
  Pallas kernels  183 us (58%)
  starting transfers between devices  52.6 us (17%)
  waiting for transfers between devices  37 us (12%)
  other arithmetic  19.7 us (6%)
  local copies, waits for them, and re-layouts  11 us (4%)
  between operations  6.04 us (2%)
    pallas_call x7, Pallas kernels, gradient(): pl.pallas_call(kernel, grid_spec=pltpu.PrefetchScalarGridSpec(num_scalar_...  45.7 us
    ppermute x22, starting transfers between devices, swapped(): lax.ppermute(value, BOTH, [(one, one ^ mask_of(one)) for one in range(cou...  28.8 us
    ppermute x22, waiting for transfers between devices, swapped(): lax.ppermute(value, BOTH, [(one, one ^ mask_of(one)) for one in range(cou...  21.8 us
    pallas_call x1, Pallas kernels, middle_forward(): pl.pallas_call(middle_forward_kernel, grid=(steps,), in_specs=[smem(), sm...  20.7 us
    all_to_all x4, starting transfers between devices, exchanged(): return lax.all_to_all(array, 'seq', split_axis=0, concat_axis=0, tiled=True)  18.9 us
    convert_element_type x13, other arithmetic, added(): return (kept.astype(F32) + arrived.astype(F32)).astype(kind)  18.1 us
    pallas_call x1, Pallas kernels, in_backward(): pl.pallas_call(in_backward_kernel, grid=(steps,), in_specs=[smem(), smem(...  16.7 us
    pallas_call x1, Pallas kernels, middle_backward(): pl.pallas_call(middle_backward_kernel, grid=(steps,), in_specs=[smem(), s...  15.8 us
  transfers between devices with their start and end apart: 29, of which 11 were waited for; matrix products, arithmetic and copies ran while one was open for 6% of the time, Pallas kernels for 41%

profile of v2, /device:TPU:0, one launch (start us, length us, event | category | flops | bytes accessed | tf_op | source)
XLA Modules:
  0.0 309.0 jit_solution(12754047323519612480)
XLA Ops:
  6.3 2.9 collective-permute-done.1.beyond_ref
  9.8 10.9 %in_forward.1 = (bf16[2,512,512]{2,1,0:T(8,128)(2,1)}, bf16[3,2,288,1024]{3,2,1,0:T(8,128)(2,1)}, bf16[8,2,256,128]{3,2,1,0:T(8,128)(2,1)}) custom-call(s32[2,2]{1,0:T(2,128)} %cuts_ref.7, s32[1]{0:T(128)} %bitcast.first_ref, bf16[2,16,1024]{2,1,0:T(8,128)(2,1)} %copy-done.28, bf16[2,256,1024]{2,1,0:T(8,128)(2,1)} %x_ref.1, bf16[2,16,1024]{2,1,0:T(8,128)(2,1)} %copy-done.29, ...), custom_call_target="tpu_custom_call" | custom-call | flops 49999998976 | bytes 200000000 | tf_op jit(solution)/shard_map/in_forward/pallas_call | solution.py:993
  20.7 6.4 %all-to-all-start = ((bf16[8,2,256,128]{3,2,1,0:T(8,128)(2,1)}), bf16[8,2,256,128]{3,2,1,0:T(8,128)(2,1)S(1)}, u32[]{:S(2)}, u32[]{:S(2)}) async-start(bf16[8,2,256,128]{3,2,1,0:T(8,128)(2,1)} %get-tuple-element.97._), calls=%async_computation | async-start | bytes 2097152 | tf_op jit(solution)/shard_map/all_to_all | solution.py:1942
  27.5 9.1 %taps_and_spectrum.1 = (f32[8,512,128]{2,1,0:T(8,128)}, f32[2048,128]{1,0:T(8,128)}, f32[2048,128]{1,0:T(8,128)}) custom-call(s32[1]{0:T(128)} %bitcast.6.first_ref.refs_0_, f32[2048,33]{1,0:T(8,128)} %constant.169.clone.feats_ref.refs_3_, bf16[33,64]{1,0:T(8,128)(2,1)} %w1.4, bf16[64]{0:T(256)(128)(2,1)} %b1.3, bf16[64,64]{1,0:T(8,128)(2,1)} %refs_6_.1, ...), custom_call_target="tpu_custom_call" | custom-call | flops 1 | bytes 1 | tf_op jit(solution)/shard_map/taps_and_spectrum/pallas_call | solution.py:268
  36.5 6.0 %all-to-all-done.series_ref = bf16[8,2,256,128]{3,2,1,0:T(8,128)(2,1)S(1)} async-done(((bf16[8,2,256,128]{3,2,1,0:T(8,128)(2,1)}), bf16[8,2,256,128]{3,2,1,0:T(8,128)(2,1)S(1)}, u32[]{:S(2)}, u32[]{:S(2)}) %all-to-all-start) | async-done | bytes 1048608 | tf_op jit(solution)/shard_map/all_to_all | solution.py:1942
  43.5 9.3 %long_forward.1._ = bf16[8,2,256,128]{3,2,1,0:T(8,128)(2,1)} custom-call(s32[5,2,10]{2,1,0:T(2,128)} %copy-done.26, bf16[8,2,256,128]{3,2,1,0:T(8,128)(2,1)} %copy-done.11, f32[8,512,128]{2,1,0:T(8,128)} %get-tuple-element.98.taps_ref, bf16[128]{0:T(256)(128)(2,1)} %skip_ref.3, bf16[512,256]{1,0:T(8,128)(2,1)} %constant.166.clone.high_ref.ahead_ref, ...), custom_call_target="tpu_custom_call" | custom-call | flops 49999998976 | bytes 200000000 | tf_op jit(solution)/shard_map/long_forward/pallas_call | solution.py:387
  52.8 3.8 %all-to-all-start.1 = ((bf16[8,2,256,128]{3,2,1,0:T(8,128)(2,1)}), bf16[8,2,256,128]{3,2,1,0:T(8,128)(2,1)S(1)}, u32[]{:S(2)}, u32[]{:S(2)}) async-start(bf16[8,2,256,128]{3,2,1,0:T(8,128)(2,1)} %long_forward.1._), calls=%async_computation.1 | async-start | bytes 2097152 | tf_op jit(solution)/shard_map/all_to_all | solution.py:1942
  56.6 9.0 %matmul_turned.1.g_act_ref = bf16[512,4096]{1,0:T(8,128)(2,1)} custom-call(bf16[512,1024]{1,0:T(8,128)(2,1)} %bitcast.111, bf16[4096,1024]{1,0:T(8,128)(2,1)} %down_ref.1, bf16[8,2,256,128]{3,2,1,0:T(8,128)(2,1)} %long_forward.1._), custom_call_target="tpu_custom_call" | custom-call | flops 1 | bytes 1 | tf_op jit(solution)/shard_map/matmul_turned/pallas_call | solution.py:1562
  65.5 6.4 %all-to-all-done.1.long_ref.long_at = bf16[8,2,256,128]{3,2,1,0:T(8,128)(2,1)S(1)} async-done(((bf16[8,2,256,128]{3,2,1,0:T(8,128)(2,1)}), bf16[8,2,256,128]{3,2,1,0:T(8,128)(2,1)S(1)}, u32[]{:S(2)}, u32[]{:S(2)}) %all-to-all-start.1) | async-done | bytes 1048608 | tf_op jit(solution)/shard_map/all_to_all | solution.py:1942
  72.9 20.7 %middle_forward.1 = (bf16[2,512,512]{2,1,0:T(8,128)(2,1)}, f32[512,1024]{1,0:T(8,128)}, bf16[2,512,512]{2,1,0:T(8,128)(2,1)}, bf16[512,4096]{1,0:T(8,128)(2,1)},...) custom-call(s32[2,2]{1,0:T(2,128)} %cuts_ref.7, s32[1]{0:T(128)} %bitcast.first_ref, ...), custom_call_target="tpu_custom_call" | custom-call | flops 49999998976 | bytes 200000000 | tf_op jit(solution)/shard_map/middle_forward/pallas_call | solution.py:1121
  93.6 5.8 %gradient.7 = (bf16[2048,1024]{1,0:T(8,128)(2,1)}, s32[1]{0:T(128)}) custom-call(s32[1]{0:T(128)} %bitcast.26.order_ref, bf16[2,2048,512]{2,1,0:T(8,128)(2,1)} %get-tuple-element.103.refs_0_, bf16[512,1024]{1,0:T(8,128)(2,1)} %bitcast.112), custom_call_target="tpu_custom_call" | custom-call | flops 1 | bytes 1 | tf_op jit(solution)/shard_map/gradient/pallas_call | solution.py:1699
  100.1 5.7 %gradient.8 = (bf16[512,4096]{1,0:T(8,128)(2,1)}, s32[1]{0:T(128)}) custom-call(s32[1]{0:T(128)} %bitcast.26.order_ref, bf16[2,512,512]{2,1,0:T(8,128)(2,1)} %get-tuple-element.105.refs_0_, bf16[512,4096]{1,0:T(8,128)(2,1)} %get-tuple-element.102.refs_1_.g_pre_ref.refs_2_, bf16[2048,1024]{1,0:T(8,128)(2,1)} %get-tuple-element.104.refs_2_), custom_call_target="tpu_custom_call" | custom-call | flops 1 | bytes 1 | tf_op jit(solution)/shard_map/gradient/pallas_call | solution.py:1699
  106.9 7.9 %gradient.9 = (bf16[1024,1024]{1,0:T(8,128)(2,1)}, bf16[1024,1024]{1,0:T(8,128)(2,1)}, s32[1]{0:T(128)}) custom-call(s32[17]{0:T(128)} %stack.107.order_ref, bf16[2,2048,512]{2,1,0:T(8,128)(2,1)} %get-tuple-element.103.refs_0_, bf16[512,1024]{1,0:T(8,128)(2,1)} %bitcast.113, bf16[2048,1024]{1,0:T(8,128)(2,1)} %collective-permute-done.2.refs_2_, ...), custom_call_target="tpu_custom_call" | custom-call | flops 1 | bytes 1 | tf_op jit(solution)/shard_map/gradient/pallas_call | solution.py:1699
  115.4 15.8 %middle_backward.1 = (bf16[8,2,256,128]{3,2,1,0:T(8,128)(2,1)}, f32[2,256,1024]{2,1,0:T(8,128)}, f32[512,1024]{1,0:T(8,128)}, bf16[512,1024]{1,0:T(8,128)(2,1)}, f32[8,1024]{1,0:T(8,128)}, /*index=5*/s32[1]{0:T(128)}) custom-call(s32[2,2]{1,0:T(2,128)} %cuts_ref.7, s32[1]{0:T(128)} %bitcast.first_ref, bf16[8,2,256,128]{3,2,1,0:T(8,128)(2,1)} %copy-done.12, ...), custom_call_target="tpu_custom_call" | custom-call | flops 49999998976 | bytes 200000000 | tf_op jit(solution)/shard_map/middle_backward/pallas_call | solution.py:1294
  131.2 3.1 gradient.10
  134.4 4.4 %all-to-all-start.2 = ((bf16[8,2,256,128]{3,2,1,0:T(8,128)(2,1)}), bf16[8,2,256,128]{3,2,1,0:T(8,128)(2,1)}, u32[]{:S(2)}, u32[]{:S(2)}) async-start(bf16[8,2,256,128]{3,2,1,0:T(8,128)(2,1)} %get-tuple-element.108), calls=%async_computation.2 | async-start | bytes 2097152 | tf_op jit(solution)/shard_map/all_to_all | solution.py:1942
  139.8 10.2 %gradient.11 = (bf16[256,5120]{1,0:T(8,128)(2,1)}, bf16[256,5120]{1,0:T(8,128)(2,1)}, s32[1]{0:T(128)}) custom-call(s32[17]{0:T(128)} %stack.107.order_ref, bf16[2,512,512]{2,1,0:T(8,128)(2,1)} %get-tuple-element.105.refs_0_, bf16[2,512,512]{2,1,0:T(8,128)(2,1)} %get-tuple-element.109.refs_0_.refs_1_, ...), custom_call_target="tpu_custom_call" | custom-call | flops 1 | bytes 1 | tf_op jit(solution)/shard_map/gradient/pallas_call | solution.py:1699
  152.7 3.5 %add_convert_fusion.2 = (bf16[2,1,2,128,1024]{4,3,2,1,0:T(8,128)(2,1)S(1)}, bf16[2,2,128,1024]{3,2,1,0:T(8,128)(2,1)}) fusion(bf16[2,2,2,128,1024]{4,3,2,1,0:T(8,128)(2,1)} %bitcast.29, s32[]{:T(128)S(6)} %select_n.150, bf16[2,2,2,128,1024]{4,3,2,1,0:T(8,128)(2,1)S(1)} %bitcast.124, s32[]{:T(128)S(6)} %select_n.149), kind=kLoop, calls=%fused_computation.2 | loop fusion | flops 4194304 | bytes 6291464 | tf_op jit(solution)/shard_map/convert_element_type | solution.py:576
  158.2 15.0 %long_backward.1 = (bf16[8,2,272,128]{3,2,1,0:T(8,128)(2,1)}, f32[8,256,128]{2,1,0:T(8,128)}, f32[1,128]{1,0:T(1,128)}, s32[1]{0:T(128)}) custom-call(s32[5,2,10]{2,1,0:T(2,128)} %copy-done.26, bf16[8,2,256,128]{3,2,1,0:T(8,128)(2,1)} %all-to-all-done.2.grad_ref, bf16[8,2,256,128]{3,2,1,0:T(8,128)(2,1)} %copy-done.11, ...), custom_call_target="tpu_custom_call" | custom-call | flops 49999998976 | bytes 200000000 | tf_op jit(solution)/shard_map/long_backward/pallas_call | solution.py:434
  173.2 4.3 %all-to-all-start.3 = ((bf16[8,2,272,128]{3,2,1,0:T(8,128)(2,1)}), bf16[8,2,272,128]{3,2,1,0:T(8,128)(2,1)}, u32[]{:S(2)}, u32[]{:S(2)}) async-start(bf16[8,2,272,128]{3,2,1,0:T(8,128)(2,1)} %get-tuple-element.115.refs_0_), calls=%async_computation.3 | async-start | bytes 2228224 | tf_op jit(solution)/shard_map/all_to_all | solution.py:1942
  179.7 9.9 %down_forward.1 = (bf16[512,1024]{1,0:T(8,128)(2,1)}, s32[1]{0:T(128)}) custom-call(f32[512,1024]{1,0:T(8,128)} %get-tuple-element.100.resid_at.resid_ref, bf16[512,4096]{1,0:T(8,128)(2,1)} %get-tuple-element.101.act_ref, bf16[4096,1024]{1,0:T(8,128)(2,1)} %down_ref.1, bf16[1024]{0:T(1024)(128)(2,1)} %bias_ref.5, ...), custom_call_target="tpu_custom_call" | custom-call | flops 1 | bytes 1 | tf_op jit(solution)/shard_map/down_forward/pallas_call | solution.py:1601
  191.6 2.8 collective-permute-start.9
  197.1 3.7 %collective-permute-start.10 = (bf16[4,32,5120]{2,1,0:T(8,128)(2,1)}, bf16[4,32,5120]{2,1,0:T(8,128)(2,1)S(1)}, u32[]{:S(2)}, u32[]{:S(2)}) collective-permute-start(bf16[4,32,5120]{2,1,0:T(8,128)(2,1)} %fusion.others_1_), channel_id=1, source_target_pairs={{0,4},{1,3},{2,6},{3,1},{4,0},{5,7},{6,2},{7,5},{8,12},{9,11},{10,... | collective-permute-start | bytes 3932168 | tf_op jit(solution)/shard_map/ppermute | solution.py:568
  201.5 16.7 %in_backward.1 = (bf16[3,512,1024]{2,1,0:T(8,128)(2,1)}, f32[3,8,1024]{2,1,0:T(8,128)}, f32[512,1024]{1,0:T(8,128)}, f32[8,1024]{1,0:T(8,128)}, s32[1]{0:T(128)}) custom-call(s32[2,2]{1,0:T(2,128)} %cuts_ref.7, s32[1]{0:T(128)} %bitcast.first_ref, bf16[8,2,272,128]{3,2,1,0:T(8,128)(2,1)} %all-to-all-done.3.g_carried_ref, ...), custom_call_target="tpu_custom_call" | custom-call | flops 49999998976 | bytes 200000000 | tf_op jit(solution)/shard_map/in_backward/pallas_call | solution.py:1486
  222.8 5.5 %gradient.12 = (bf16[512,3072]{1,0:T(8,128)(2,1)}, s32[1]{0:T(128)}) custom-call(s32[1]{0:T(128)} %bitcast.26.order_ref, bf16[2,512,512]{2,1,0:T(8,128)(2,1)} %get-tuple-element.130.refs_0_, bf16[3,512,1024]{2,1,0:T(8,128)(2,1)} %get-tuple-element.131.refs_1_, bf16[128,1024]{1,0:T(8,128)(2,1)} %fusion.12.refs_2_, bf16[2,32,5120]{2,1,0:T(8,128)(2,1)} %fusion.5.refs_3_), custom_call_target="tpu_custom_call" | custom-call | flops 49999998976 | bytes 200000000 | tf_op jit(solution)/shard_map/gradient/pallas_call | solution.py:1699
  230.6 3.7 %collective-permute-done.11.refs_2_ = bf16[512,3072]{1,0:T(8,128)(2,1)} collective-permute-done((bf16[512,3072]{1,0:T(8,128)(2,1)}, bf16[512,3072]{1,0:T(8,128)(2,1)}, u32[]{:S(2)}, u32[]{:S(2)}) %collective-permute-start.11) | collective-permute-done | bytes 3145760 | tf_op jit(solution)/shard_map/ppermute | solution.py:568
  234.3 7.6 %gradient.13 = (bf16[256,3072]{1,0:T(8,128)(2,1)}, bf16[256,3072]{1,0:T(8,128)(2,1)}, s32[1]{0:T(128)}) custom-call(s32[17]{0:T(128)} %stack.107.order_ref, bf16[2,512,512]{2,1,0:T(8,128)(2,1)} %get-tuple-element.130.refs_0_, bf16[3,512,1024]{2,1,0:T(8,128)(2,1)} %get-tuple-element.131.refs_1_, bf16[512,3072]{1,0:T(8,128)(2,1)} %collective-permute-done.11.refs_2_), custom_call_target="tpu_custom_call" | custom-call | flops 1 | bytes 1 | tf_op jit(solution)/shard_map/gradient/pallas_call | solution.py:1699
  244.0 5.6 %filter_backward.1 = (f32[192,128]{1,0:T(8,128)}, f32[192,128]{1,0:T(8,128)}, f32[192,128]{1,0:T(8,128)}, f32[192,128]{1,0:T(8,128)}) custom-call(s32[1]{0:T(128)} %bitcast.6.first_ref.refs_0_, s32[1]{0:T(128)} %bitcast.40.refs_1_, f32[2048,128]{1,0:T(8,128)} %bitcast.136, f32[2048,33]{1,0:T(8,128)} %constant.169.clone.feats_ref.refs_3_, ...), custom_call_target="tpu_custom_call" | custom-call | flops 49999998976 | bytes 200000000 | tf_op jit(solution)/shard_map/filter_backward/pallas_call | solution.py:141
  259.1 2.8 collective-permute-done.13.refs_2_
  275.7 3.5 %collective-permute-done.20 = bf16[4,32,3072]{2,1,0:T(8,128)(2,1)} collective-permute-done((bf16[4,32,3072]{2,1,0:T(8,128)(2,1)S(1)}, bf16[4,32,3072]{2,1,0:T(8,128)(2,1)}, u32[]{:S(2)}, u32[]{:S(2)}) %collective-permute-start.20) | collective-permute-done | bytes 786464 | tf_op jit(solution)/shard_map/ppermute | solution.py:568
  290.1 3.7 %collective-permute-done.23.arrived_ref = bf16[2,32,3072]{2,1,0:T(8,128)(2,1)S(1)} collective-permute-done((bf16[2,32,3072]{2,1,0:T(8,128)(2,1)S(1)}, bf16[2,32,3072]{2,1,0:T(8,128)(2,1)S(1)}, u32[]{:S(2)}, u32[]{:S(2)}) %collective-permute-start.23) | collective-permute-done | bytes 393248 | tf_op jit(solution)/shard_map/ppermute | solution.py:568
  302.0 3.4 %collective-permute-done.24.last_ref = bf16[32,3072]{1,0:T(8,128)(2,1)S(1)} collective-permute-done((bf16[32,3072]{1,0:T(8,128)(2,1)S(1)}, bf16[32,3072]{1,0:T(8,128)(2,1)S(1)}, u32[]{:S(2)}, u32[]{:S(2)}) %collective-permute-start.24) | collective-permute-done | bytes 196640 | tf_op jit(solution)/shard_map/ppermute | solution.py:568
  (139 shorter events, 73.9 us)
Async XLA Ops:
  1.5 4.7 %collective-permute-start = (bf16[2,16,1024]{2,1,0:T(8,128)(2,1)S(1)}, bf16[2,16,1024]{2,1,0:T(8,128)(2,1)S(1)}, u32[]{:S(2)}, u32[]{:S(2)}) collective-permute-start(bf16[2,16,1024]{2,1,0:T(8,128)(2,1)S(1)} %get-tuple-element.185), channel_id=1, source_target_pairs={{0,1},{1,2},{2,3},{3,4},{4,5},{5,6},{6,7},{8,9},{9,10},{10,11},{11... | collective-permute-start | bytes 196616 | tf_op jit(solution)/shard_map/ppermute | solution.py:30
  3.9 5.3 %collective-permute-start.1 = (bf16[2,16,1024]{2,1,0:T(8,128)(2,1)S(1)}, bf16[2,16,1024]{2,1,0:T(8,128)(2,1)S(1)}, u32[]{:S(2)}, u32[]{:S(2)}) collective-permute-start(bf16[2,16,1024]{2,1,0:T(8,128)(2,1)S(1)} %get-tuple-element.184), channel_id=1, source_target_pairs={{1,0},{2,1},{3,2},{4,3},{5,4},{6,5},{7,6},{9,8},{10,9},{11,10},{12... | collective-permute-start | bytes 196616 | tf_op jit(solution)/shard_map/ppermute | solution.py:30
  20.7 21.8 %all-to-all-start = ((bf16[8,2,256,128]{3,2,1,0:T(8,128)(2,1)}), bf16[8,2,256,128]{3,2,1,0:T(8,128)(2,1)S(1)}, u32[]{:S(2)}, u32[]{:S(2)}) async-start(bf16[8,2,256,128]{3,2,1,0:T(8,128)(2,1)} %get-tuple-element.97._), calls=%async_computation | async-start | bytes 2097152 | tf_op jit(solution)/shard_map/all_to_all | solution.py:1942
  52.8 19.1 %all-to-all-start.1 = ((bf16[8,2,256,128]{3,2,1,0:T(8,128)(2,1)}), bf16[8,2,256,128]{3,2,1,0:T(8,128)(2,1)S(1)}, u32[]{:S(2)}, u32[]{:S(2)}) async-start(bf16[8,2,256,128]{3,2,1,0:T(8,128)(2,1)} %long_forward.1._), calls=%async_computation.1 | async-start | bytes 2097152 | tf_op jit(solution)/shard_map/all_to_all | solution.py:1942
  99.4 7.5 %collective-permute-start.2 = (bf16[2048,1024]{1,0:T(8,128)(2,1)}, bf16[2048,1024]{1,0:T(8,128)(2,1)}, u32[]{:S(2)}, u32[]{:S(2)}) collective-permute-start(bf16[2048,1024]{1,0:T(8,128)(2,1)} %get-tuple-element.104.refs_2_), channel_id=1, source_target_pairs={{0,1},{1,0},{2,3},{3,2},{4,5},{5,4},{6,7},{7,6},{8,9},{9,8},{10,11... | collective-permute-start | bytes 12582920 | tf_op jit(solution)/shard_map/ppermute | solution.py:568
  105.8 33.1 %collective-permute-start.3 = (bf16[512,4096]{1,0:T(8,128)(2,1)}, bf16[512,4096]{1,0:T(8,128)(2,1)}, u32[]{:S(2)}, u32[]{:S(2)}) collective-permute-start(bf16[512,4096]{1,0:T(8,128)(2,1)} %get-tuple-element.106.refs_3_), channel_id=1, source_target_pairs={{0,1},{1,0},{2,3},{3,2},{4,5},{5,4},{6,7},{7,6},{8,9},{9,8},{10,11... | collective-permute-start | bytes 12582920 | tf_op jit(solution)/shard_map/ppermute | solution.py:568
  114.8 37.8 %collective-permute-start.5 = (bf16[1024,1024]{1,0:T(8,128)(2,1)}, bf16[1024,1024]{1,0:T(8,128)(2,1)}, u32[]{:S(2)}, u32[]{:S(2)}) collective-permute-start(bf16[1024,1024]{1,0:T(8,128)(2,1)} %get-tuple-element.107._), channel_id=1, source_target_pairs={{0,2},{1,5},{2,0},{3,7},{4,6},{5,1},{6,4},{7,3},{8,10},{9,13},{10,... | collective-permute-start | bytes 6291464 | tf_op jit(solution)/shard_map/ppermute | solution.py:568
  134.3 4.5 %collective-permute-start.4 = (bf16[512,1024]{1,0:T(8,128)(2,1)}, bf16[512,1024]{1,0:T(8,128)(2,1)S(1)}, u32[]{:S(2)}, u32[]{:S(2)}) collective-permute-start(bf16[512,1024]{1,0:T(8,128)(2,1)} %get-tuple-element.111), channel_id=1, source_target_pairs={{0,1},{1,0},{2,3},{3,2},{4,5},{5,4},{6,7},{7,6},{8,9},{9,8},{10,11... | collective-permute-start | bytes 3145736 | tf_op jit(solution)/shard_map/ppermute | solution.py:568
  134.4 23.8 %all-to-all-start.2 = ((bf16[8,2,256,128]{3,2,1,0:T(8,128)(2,1)}), bf16[8,2,256,128]{3,2,1,0:T(8,128)(2,1)}, u32[]{:S(2)}, u32[]{:S(2)}) async-start(bf16[8,2,256,128]{3,2,1,0:T(8,128)(2,1)} %get-tuple-element.108), calls=%async_computation.2 | async-start | bytes 2097152 | tf_op jit(solution)/shard_map/all_to_all | solution.py:1942
  150.7 43.7 %collective-permute-start.8 = (bf16[256,5120]{1,0:T(8,128)(2,1)}, bf16[256,5120]{1,0:T(8,128)(2,1)}, u32[]{:S(2)}, u32[]{:S(2)}) collective-permute-start(bf16[256,5120]{1,0:T(8,128)(2,1)} %get-tuple-element.112.others_0_), channel_id=1, source_target_pairs={{0,2},{1,5},{2,0},{3,7},{4,6},{5,1},{6,4},{7,3},{8,10},{9,13},{10,... | collective-permute-start | bytes 7864328 | tf_op jit(solution)/shard_map/ppermute | solution.py:568
  156.2 34.2 %collective-permute-start.7 = (bf16[2,2,128,1024]{3,2,1,0:T(8,128)(2,1)}, bf16[2,2,128,1024]{3,2,1,0:T(8,128)(2,1)S(1)}, u32[]{:S(2)}, u32[]{:S(2)}) collective-permute-start(bf16[2,2,128,1024]{3,2,1,0:T(8,128)(2,1)} %get-tuple-element.181.others_1_), channel_id=1, source_target_pairs={{0,8},{1,9},{2,10},{3,11},{4,12},{5,13},{6,14},{7,15},{8,0},{9,1},... | collective-permute-start | bytes 3145736 | tf_op jit(solution)/shard_map/ppermute | solution.py:568
  173.2 27.6 %all-to-all-start.3 = ((bf16[8,2,272,128]{3,2,1,0:T(8,128)(2,1)}), bf16[8,2,272,128]{3,2,1,0:T(8,128)(2,1)}, u32[]{:S(2)}, u32[]{:S(2)}) async-start(bf16[8,2,272,128]{3,2,1,0:T(8,128)(2,1)} %get-tuple-element.115.refs_0_), calls=%async_computation.3 | async-start | bytes 2228224 | tf_op jit(solution)/shard_map/all_to_all | solution.py:1942
  178.4 22.4 %collective-permute-start.6 = (bf16[2,16,1024]{2,1,0:T(8,128)(2,1)S(1)}, bf16[2,16,1024]{2,1,0:T(8,128)(2,1)S(1)}, u32[]{:S(2)}, u32[]{:S(2)}) collective-permute-start(bf16[2,16,1024]{2,1,0:T(8,128)(2,1)S(1)} %slice.29), channel_id=1, source_target_pairs={{1,0},{2,1},{3,2},{4,3},{5,4},{6,5},{7,6},{9,8},{10,9},{11,10},{12... | collective-permute-start | bytes 196616 | tf_op jit(solution)/shard_map/ppermute | solution.py:30
  191.6 27.3 %copy-start.1 = (bf16[1,2,128,1024]{3,2,1,0:T(8,128)(2,1)}, bf16[1,2,128,1024]{3,2,1,0:T(8,128)(2,1)S(1)}, u32[]{:S(2)}) copy-start(bf16[1,2,128,1024]{3,2,1,0:T(8,128)(2,1)S(1)} %get-tuple-element.182) | copy-start | bytes 1572868
  191.6 27.3 %collective-permute-start.9 = (bf16[2,128,1024]{2,1,0:T(8,128)(2,1)}, bf16[2,128,1024]{2,1,0:T(8,128)(2,1)S(1)}, u32[]{:S(2)}, u32[]{:S(2)}) collective-permute-start(bf16[2,128,1024]{2,1,0:T(8,128)(2,1)} %get-tuple-element.183.others_0_), channel_id=1, source_target_pairs={{0,16},{1,17},{2,18},{3,19},{4,20},{5,21},{6,22},{7,23},{8,24},{9,... | collective-permute-start | bytes 1572872 | tf_op jit(solution)/shard_map/ppermute | solution.py:568
  197.1 24.6 %collective-permute-start.10 = (bf16[4,32,5120]{2,1,0:T(8,128)(2,1)}, bf16[4,32,5120]{2,1,0:T(8,128)(2,1)S(1)}, u32[]{:S(2)}, u32[]{:S(2)}) collective-permute-start(bf16[4,32,5120]{2,1,0:T(8,128)(2,1)} %fusion.others_1_), channel_id=1, source_target_pairs={{0,4},{1,3},{2,6},{3,1},{4,0},{5,7},{6,2},{7,5},{8,12},{9,11},{10,... | collective-permute-start | bytes 3932168 | tf_op jit(solution)/shard_map/ppermute | solution.py:568
  228.3 6.0 %collective-permute-start.11 = (bf16[512,3072]{1,0:T(8,128)(2,1)}, bf16[512,3072]{1,0:T(8,128)(2,1)}, u32[]{:S(2)}, u32[]{:S(2)}) collective-permute-start(bf16[512,3072]{1,0:T(8,128)(2,1)} %get-tuple-element.133), channel_id=1, source_target_pairs={{0,1},{1,0},{2,3},{3,2},{4,5},{5,4},{6,7},{7,6},{8,9},{9,8},{10,11... | collective-permute-start | bytes 9437192 | tf_op jit(solution)/shard_map/ppermute | solution.py:568
  228.3 28.8 %collective-permute-start.15 = (bf16[128,1024]{1,0:T(8,128)(2,1)S(1)}, bf16[128,1024]{1,0:T(8,128)(2,1)}, u32[]{:S(2)}, u32[]{:S(2)}) collective-permute-start(bf16[128,1024]{1,0:T(8,128)(2,1)S(1)} %copy-done.15), channel_id=1, source_target_pairs={{0,4},{1,3},{2,6},{3,1},{4,0},{5,7},{6,2},{7,5},{8,12},{9,11},{10,... | collective-permute-start | bytes 786440 | tf_op jit(solution)/shard_map/ppermute | solution.py:568
  230.4 23.2 %collective-permute-start.16 = (bf16[2,32,5120]{2,1,0:T(8,128)(2,1)}, bf16[2,32,5120]{2,1,0:T(8,128)(2,1)}, u32[]{:S(2)}, u32[]{:S(2)}) collective-permute-start(bf16[2,32,5120]{2,1,0:T(8,128)(2,1)} %fusion.5.refs_3_), channel_id=1, source_target_pairs={{0,8},{1,9},{2,10},{3,11},{4,12},{5,13},{6,14},{7,15},{8,0},{9,1},... | collective-permute-start | bytes 1966088 | tf_op jit(solution)/shard_map/ppermute | solution.py:568
  230.6 24.7 %copy-start = (bf16[2,1,32,5120]{3,2,1,0:T(8,128)(2,1)}, bf16[2,1,32,5120]{3,2,1,0:T(8,128)(2,1)S(1)}, u32[]{:S(2)}) copy-start(bf16[2,1,32,5120]{3,2,1,0:T(8,128)(2,1)S(1)} %add_convert_fusion.6) | copy-start | bytes 1966084
  241.8 23.8 %collective-permute-start.18 = (bf16[256,3072]{1,0:T(8,128)(2,1)}, bf16[256,3072]{1,0:T(8,128)(2,1)}, u32[]{:S(2)}, u32[]{:S(2)}) collective-permute-start(bf16[256,3072]{1,0:T(8,128)(2,1)} %get-tuple-element.134.refs_13_), channel_id=1, source_target_pairs={{0,2},{1,5},{2,0},{3,7},{4,6},{5,1},{6,4},{7,3},{8,10},{9,13},{10,... | collective-permute-start | bytes 4718600 | tf_op jit(solution)/shard_map/ppermute | solution.py:568
  249.7 16.0 %copy-start.6 = (bf16[256,3072]{1,0:T(8,128)(2,1)S(1)}, bf16[256,3072]{1,0:T(8,128)(2,1)}, u32[]{:S(2)}) copy-start(bf16[256,3072]{1,0:T(8,128)(2,1)} %get-tuple-element.142) | copy-start | bytes 4718596
  250.8 8.3 %collective-permute-start.12 = (f32[192,128]{1,0:T(8,128)}, f32[192,128]{1,0:T(8,128)S(1)}, u32[]{:S(2)}, u32[]{:S(2)}) collective-permute-start(f32[192,128]{1,0:T(8,128)} %get-tuple-element.136.refs_1_), channel_id=1, source_target_pairs={{0,8},{1,9},{2,10},{3,11},{4,12},{5,13},{6,14},{7,15},{8,0},{9,1},... | collective-permute-start | bytes 294920 | tf_op jit(solution)/shard_map/ppermute | solution.py:568
  250.9 11.0 %collective-permute-start.13 = (f32[192,128]{1,0:T(8,128)}, f32[192,128]{1,0:T(8,128)S(1)}, u32[]{:S(2)}, u32[]{:S(2)}) collective-permute-start(f32[192,128]{1,0:T(8,128)} %get-tuple-element.137.refs_2_), channel_id=1, source_target_pairs={{0,16},{1,17},{2,18},{3,19},{4,20},{5,21},{6,22},{7,23},{8,24},{9,... | collective-permute-start | bytes 294920 | tf_op jit(solution)/shard_map/ppermute | solution.py:568
  253.7 8.2 %collective-permute-start.14 = (f32[192,128]{1,0:T(8,128)}, f32[192,128]{1,0:T(8,128)S(1)}, u32[]{:S(2)}, u32[]{:S(2)}) collective-permute-start(f32[192,128]{1,0:T(8,128)} %get-tuple-element.138.refs_3_), channel_id=1, source_target_pairs={{0,24},{1,25},{2,26},{3,27},{4,28},{5,29},{6,30},{7,31},{8,16},{9,... | collective-permute-start | bytes 294920 | tf_op jit(solution)/shard_map/ppermute | solution.py:568
  267.0 12.2 %collective-permute-start.20 = (bf16[4,32,3072]{2,1,0:T(8,128)(2,1)S(1)}, bf16[4,32,3072]{2,1,0:T(8,128)(2,1)}, u32[]{:S(2)}, u32[]{:S(2)}) collective-permute-start(bf16[4,32,3072]{2,1,0:T(8,128)(2,1)S(1)} %fusion.4.refs_2_), channel_id=1, source_target_pairs={{0,4},{1,3},{2,6},{3,1},{4,0},{5,7},{6,2},{7,5},{8,12},{9,11},{10,... | collective-permute-start | bytes 2359304 | tf_op jit(solution)/shard_map/ppermute | solution.py:568
  267.3 2.8 collective-permute-start.17
  267.4 18.3 %collective-permute-start.22 = (bf16[32,5120]{1,0:T(8,128)(2,1)S(1)}, bf16[32,5120]{1,0:T(8,128)(2,1)}, u32[]{:S(2)}, u32[]{:S(2)}) collective-permute-start(bf16[32,5120]{1,0:T(8,128)(2,1)S(1)} %copy-done.8), channel_id=1, source_target_pairs={{0,16},{1,17},{2,18},{3,19},{4,20},{5,21},{6,22},{7,23},{8,24},{9,... | collective-permute-start | bytes 983048 | tf_op jit(solution)/shard_map/ppermute | solution.py:568
  272.9 9.0 %collective-permute-start.19 = (f32[120,128]{1,0:T(8,128)}, f32[120,128]{1,0:T(8,128)S(1)}, u32[]{:S(2)}, u32[]{:S(2)}) collective-permute-start(f32[120,128]{1,0:T(8,128)} %get-tuple-element.144.refs_0_), channel_id=1, source_target_pairs={{0,2},{1,3},{2,0},{3,1},{4,6},{5,7},{6,4},{7,5},{8,10},{9,11},{10,... | collective-permute-start | bytes 184328 | tf_op jit(solution)/shard_map/ppermute | solution.py:568
  280.2 13.6 %collective-permute-start.23 = (bf16[2,32,3072]{2,1,0:T(8,128)(2,1)S(1)}, bf16[2,32,3072]{2,1,0:T(8,128)(2,1)S(1)}, u32[]{:S(2)}, u32[]{:S(2)}) collective-permute-start(bf16[2,32,3072]{2,1,0:T(8,128)(2,1)S(1)} %fusion.9.refs_2_), channel_id=1, source_target_pairs={{0,8},{1,9},{2,10},{3,11},{4,12},{5,13},{6,14},{7,15},{8,0},{9,1},... | collective-permute-start | bytes 1179656 | tf_op jit(solution)/shard_map/ppermute | solution.py:568
  293.9 11.6 %collective-permute-start.24 = (bf16[32,3072]{1,0:T(8,128)(2,1)S(1)}, bf16[32,3072]{1,0:T(8,128)(2,1)S(1)}, u32[]{:S(2)}, u32[]{:S(2)}) collective-permute-start(bf16[32,3072]{1,0:T(8,128)(2,1)S(1)} %fusion.13.refs_2_), channel_id=1, source_target_pairs={{0,16},{1,17},{2,18},{3,19},{4,20},{5,21},{6,22},{7,23},{8,24},{9,... | collective-permute-start | bytes 589832 | tf_op jit(solution)/shard_map/ppermute | solution.py:568
  294.2 4.2 %collective-permute-start.21 = (f32[120,128]{1,0:T(8,128)S(1)}, f32[120,128]{1,0:T(8,128)S(1)}, u32[]{:S(2)}, u32[]{:S(2)}) collective-permute-start(f32[120,128]{1,0:T(8,128)S(1)} %copy-done.20), channel_id=1, source_target_pairs={{0,4},{1,5},{2,6},{3,7},{4,0},{5,1},{6,2},{7,3},{8,12},{9,13},{10,... | collective-permute-start | bytes 184328 | tf_op jit(solution)/shard_map/ppermute | solution.py:568
  (27 other events, 121.1 us)
